TPU v7x, 256 devices: a whole 4x4x8 slice. The times are simulated.
256 devices in a mesh: shot: 4 (over x_hi, core), gy: 64 (over z, x_lo, y).
Axes of the slice: x: 4 (x_hi: 2, x_lo: 2; x = x_hi * 2 + x_lo), y: 4, z: 8, core: 2. Of those that a mesh axis runs over, the one named last changes fastest.
Arguments:
- stiffness: float32 [16, 512, 1024], P(None, 'gy'), may hold values from 0.5 to 2
- first_moment: float32 [16, 512, 1024], P('shot', 'gy'), may hold values from -6 to 6
- second_moment: float32 [16, 512, 1024], P('shot', 'gy'), may hold values from 0.1 to 4
- wave_prev: float32 [4, 16, 512, 1024], P('shot', None, 'gy'), may hold values from -6 to 6
- wave_now: float32 [4, 16, 512, 1024], P('shot', None, 'gy'), may hold values from -6 to 6
- adjoint_next: float32 [4, 16, 512, 1024], P('shot', None, 'gy'), may hold values from -6 to 6
- adjoint_now: float32 [4, 16, 512, 1024], P('shot', None, 'gy'), may hold values from -6 to 6
- observed: float32 [4, 4, 512, 128], P('shot', None, 'gy'), may hold values from -12 to 12
- receiver_x: int32 [4, 512, 128], P('shot', 'gy'), may hold values from 0 to 1023
- source_pos: int32 [4, 3], P('shot'), may hold values from 0 to 1023, as said below
- source_wave: float32 [4, 4], P('shot'), may hold values from -240 to 240
Outputs:
- stiffness_new: float32 [16, 512, 1024], P(None, 'gy')
- first_new: float32 [16, 512, 1024], P('shot', 'gy')
- second_new: float32 [16, 512, 1024], P('shot', 'gy')
Inputs may be any that keep to these rules, and one draw needn't show every extreme that they name: `source_pos`: each row gives a source cell inside the grid: z below 16, y below 512, x below 1024; some shot's source lies in the last x cell and some shot's in the last y row.
All inputs are finite; a program needn't handle non-finite values.
Results may differ from a plain program's by a relative error of at most 0.00002.
Values sent between devices are 32-bit elements; how exact they have to be, the bound alone decides.
No kernel may reach another device: no remote copies, remote signals or barrier semaphores. Data moves between devices by JAX's collectives and lax.ppermute only.
A program may use at most 128 MiB of HBM per device.

v0:
```python
import jax
import jax.numpy as jnp
from jax import lax
from jax.sharding import PartitionSpec as P

TIME_STEP_SQ = 0.15
BETA_ONE = 0.9
BETA_TWO = 0.999
LEARN_RATE = 0.05
ADAM_EPS = 1e-08
ADAM_TICKS = 10.0


def padded_2(block, sides, width):
    for axis, dim in sides:
        count = lax.axis_size(axis)
        forward = [(i, i + 1) for i in range(count - 1)]
        backward = [(target, source) for source, target in forward]
        low = lax.ppermute(
            lax.slice_in_dim(block, block.shape[dim] - width, None, axis=dim), axis, forward
        )
        high = lax.ppermute(lax.slice_in_dim(block, 0, width, axis=dim), axis, backward)
        block = jnp.concatenate([low, block, high], axis=dim)
    return block


def toward_next(field, dim_index):
    length = field.shape[dim_index]
    inner = lax.slice_in_dim(field, 1, length, axis=dim_index)
    blank_rows = jnp.zeros_like(lax.slice_in_dim(field, 0, 1, axis=dim_index))
    return jnp.concatenate([inner, blank_rows], dim_index)


def toward_prev(field, dim_index):
    length = field.shape[dim_index]
    inner = lax.slice_in_dim(field, 0, length - 1, axis=dim_index)
    blank_rows = jnp.zeros_like(lax.slice_in_dim(field, 0, 1, axis=dim_index))
    return jnp.concatenate([blank_rows, inner], dim_index)


def neighbours(padded, dim_index):
    center = padded[:, 1:-1]
    if dim_index == 1:
        return (padded[:, 2:], padded[:, :-2])
    return (toward_next(center, dim_index), toward_prev(center, dim_index))


def operate(padded, stiff_pad):
    field = padded[:, 1:-1]
    stiffness = stiff_pad[:, 1:-1]
    summed = jnp.zeros_like(field)
    for dim_index in range(3):
        field_after, field_before = neighbours(padded, dim_index)
        stiff_after, stiff_before = neighbours(stiff_pad, dim_index)
        summed = (
            summed
            + 0.5 * (stiffness + stiff_after) * (field_after - field)
            - 0.5 * (stiffness + stiff_before) * (field - field_before)
        )
    return summed


def face_sum(wave_pad, adj_pad):
    wave = wave_pad[:, 1:-1]
    adjoint = adj_pad[:, 1:-1]
    summed = jnp.zeros_like(wave)
    for dim_index in range(3):
        wave_after, wave_before = neighbours(wave_pad, dim_index)
        adj_after, adj_before = neighbours(adj_pad, dim_index)
        summed = (
            summed
            + (wave_after - wave) * (adj_after - adjoint)
            + (wave - wave_before) * (adjoint - adj_before)
        )
    return summed


def pad_wave(field):
    return padded_2(field, (("gy", 1),), 1)


def pad_adjoint(field):
    return padded_2(field, (("gy", 1),), 1)


def source_cells(source_pos, planes, extent, row_width, first_row):
    shape = (planes, extent, row_width)
    z_index = lax.broadcasted_iota(jnp.int32, shape, 0)
    y_index = lax.broadcasted_iota(jnp.int32, shape, 1) + first_row
    x_index = lax.broadcasted_iota(jnp.int32, shape, 2)
    hit = (
        (z_index == source_pos[0, 0])
        & (y_index == source_pos[0, 1])
        & (x_index == source_pos[0, 2])
    )
    return (hit.astype(jnp.float32), y_index)


def body(
    stiffness,
    first_moment,
    second_moment,
    wave_prev,
    wave_now,
    adjoint_next,
    adjoint_now,
    observed,
    receiver_x,
    source_pos,
    source_wave,
):
    planes, rows_dev, row_width = stiffness.shape
    steps_count = source_wave.shape[1]
    row_start = lax.axis_index("gy") * rows_dev
    receivers = receiver_x[0]
    row_ids = lax.broadcasted_iota(jnp.int32, receivers.shape, 0)
    stiff_pad = padded_2(stiffness, (("gy", 1),), 1)
    source_mask, cell_y = source_cells(source_pos, planes, rows_dev, row_width, row_start)
    waves = [wave_prev[0], wave_now[0]]
    padded_waves = [None]
    for level in range(1, steps_count + 2):
        padded = pad_wave(waves[level])
        padded_waves.append(padded)
        if level <= steps_count:
            fresh = (
                2.0 * waves[level]
                - waves[level - 1]
                + TIME_STEP_SQ
                * (operate(padded, stiff_pad) + source_wave[0, level - 1] * source_mask)
            )
            waves.append(fresh)
    lam_after = adjoint_next[0]
    lam_here = adjoint_now[0]
    gradient = jnp.zeros_like(stiffness)
    for level in range(steps_count + 2, 1, -1):
        lam_pad = pad_adjoint(lam_here)
        gradient = gradient + face_sum(padded_waves[level - 1], lam_pad)
        if level >= 3:
            record = jnp.take_along_axis(waves[level - 1][0], receivers, axis=1)
            misfit = record - observed[0, level - 3]
            surface = (
                jnp.zeros((rows_dev, row_width), jnp.float32).at[row_ids, receivers].add(misfit)
            )
            injected = jnp.concatenate(
                [surface[None], jnp.zeros((planes - 1, rows_dev, row_width), jnp.float32)], 0
            )
            lam_before = (
                2.0 * lam_here - lam_after + TIME_STEP_SQ * operate(lam_pad, stiff_pad) + injected
            )
            lam_after = lam_here
            lam_here = lam_before
    gradient = -0.5 * TIME_STEP_SQ * gradient
    own_planes = first_moment.shape[0]
    plane_start = lax.axis_index("shot") * own_planes
    summed_grad = lax.psum(gradient, "shot")
    share = lax.dynamic_slice_in_dim(summed_grad, plane_start, own_planes, 0)
    stiff_own = lax.dynamic_slice_in_dim(stiffness, plane_start, own_planes, 0)
    first_new = BETA_ONE * first_moment + (1.0 - BETA_ONE) * share
    second_new = BETA_TWO * second_moment + (1.0 - BETA_TWO) * share * share
    updated = stiff_own - LEARN_RATE * (first_new / (1.0 - BETA_ONE**ADAM_TICKS)) / (
        jnp.sqrt(second_new / (1.0 - BETA_TWO**ADAM_TICKS)) + ADAM_EPS
    )
    stiffness_new = lax.all_gather(updated, "shot", axis=0, tiled=True)
    return (stiffness_new, first_new, second_new)


def solution(mesh):
    return jax.shard_map(
        body,
        mesh=mesh,
        in_specs=(
            P(None, "gy", None),
            P("shot", "gy", None),
            P("shot", "gy", None),
            P("shot", None, "gy", None),
            P("shot", None, "gy", None),
            P("shot", None, "gy", None),
            P("shot", None, "gy", None),
            P("shot", None, "gy", None),
            P("shot", "gy", None),
            P("shot", None),
            P("shot", None),
        ),
        out_specs=(P(None, "gy", None), P("shot", "gy", None), P("shot", "gy", None)),
        check_vma=False,
    )
```

profile of v0, /device:TPU:97, one launch (start us, length us, event | category | flops | bytes accessed | tf_op | source)
XLA Modules:
  0.0 319.9 jit_solution(15148694241307611978)
XLA Ops:
  11.8 5.1 %collective-permute-start.1 = (f32[16,1,1024]{2,1,0:T(1,128)S(1)}, f32[16,1,1024]{2,1,0:T(1,128)S(1)}, u32[]{:S(2)}, u32[]{:S(2)}) collective-permute-start(f32[16,1,1024]{2,1,0:T(1,128)S(1)} %get-tuple-element.79), channel_id=1, source_target_pairs={{1,0},{2,1},{3,2},{4,3},{5,4},{6,5},{7,6},{8,7},{9,8},{10,9},{11,1... | collective-permute-start | bytes 196616 | tf_op jit(solution)/shard_map/ppermute | solution.py:22
  22.8 6.4 %collective-permute-start = (f32[16,1,1024]{2,1,0:T(1,128)S(1)}, f32[16,1,1024]{2,1,0:T(1,128)S(1)}, u32[]{:S(2)}, u32[]{:S(2)}) collective-permute-start(f32[16,1,1024]{2,1,0:T(1,128)S(1)} %get-tuple-element.73), channel_id=1, source_target_pairs={{1,0},{2,1},{3,2},{4,3},{5,4},{6,5},{7,6},{8,7},{9,8},{10,9},{11,1... | collective-permute-start | bytes 196616 | tf_op jit(solution)/shard_map/ppermute | solution.py:22
  45.8 4.7 %fusion.43 = (f32[16,8,1024]{2,1,0:T(8,128)S(1)}, f32[16,8,1024]{2,1,0:T(8,128)S(1)}, f32[16,8,1024]{2,1,0:T(8,128)S(1)}, f32[16,8,1024]{2,1,0:T(8,128)S(1)}, f32[16,8,1024]{2,1,0:T(8,128)}) fusion(f32[1,16,8,1024]{3,2,1,0:T(8,128)} %param.16, f32[16,8,1024]{2,1,0:T(8,128)S(1)} %bitcast.96, f32[16,1,1024]{2,1,0:T(1,128)S(1)} %collective-permute-done.1, ...), kind=kLoop, calls=%fused_computation.75 | loop fusion | flops 5373952 | bytes 8518684 | tf_op jit(solution)/shard_map/add | solution.py:126
  54.7 6.4 %collective-permute-start.4 = (f32[16,1,1024]{2,1,0:T(1,128)S(1)}, f32[16,1,1024]{2,1,0:T(1,128)S(1)}, u32[]{:S(2)}, u32[]{:S(2)}) collective-permute-start(f32[16,1,1024]{2,1,0:T(1,128)S(1)} %get-tuple-element.67), channel_id=1, source_target_pairs={{1,0},{2,1},{3,2},{4,3},{5,4},{6,5},{7,6},{8,7},{9,8},{10,9},{11,1... | collective-permute-start | bytes 196616 | tf_op jit(solution)/shard_map/ppermute | solution.py:22
  61.1 6.8 %gather_fusion.3 = f32[1024]{0:T(1024)S(1)} fusion(f32[8,1024]{1,0:T(8,128)S(1)} %slice_bitcast_fusion.4, s32[1024]{0:T(1024)S(1)} %get-tuple-element.83), kind=kCustom, calls=%fused_computation.3.clone | custom fusion | bytes 16384 | tf_op jit(solution)/shard_map/jit(take_along_axis)/gather | solution.py:139
  68.5 3.4 %multiply_add_fusion.2 = f32[16,8,1024]{2,1,0:T(8,128)S(1)} fusion(f32[16,8,1024]{2,1,0:T(8,128)} %get-tuple-element.13, f32[16,8,1024]{2,1,0:T(8,128)S(1)} %get-tuple-element.12, f32[16,8,1024]{2,1,0:T(8,128)S(1)} %get-tuple-element.11, f32[16,8,1024]{2,1,0:T(8,128)S(1)} %get-tuple-element.10, f32[16,8,1024]{2,1,0:T(8,128)S(1)} %get-tuple-element.9, ...), kind=kLoop, calls=%fused_computation.105 | loop fusion | flops 4325376 | bytes 6488092 | tf_op jit(solution)/shard_map/add | solution.py:126
  75.0 6.8 %gather_fusion.2 = f32[1024]{0:T(1024)S(1)} fusion(f32[8,1024]{1,0:T(8,128)S(1)} %slice_bitcast_fusion.5, s32[1024]{0:T(1024)S(1)} %get-tuple-element.83), kind=kCustom, calls=%fused_computation.2.clone | custom fusion | bytes 16384 | tf_op jit(solution)/shard_map/jit(take_along_axis)/gather | solution.py:139
  83.7 6.4 %collective-permute-start.6 = (f32[16,1,1024]{2,1,0:T(1,128)}, f32[16,1,1024]{2,1,0:T(1,128)}, u32[]{:S(2)}, u32[]{:S(2)}) collective-permute-start(f32[16,1,1024]{2,1,0:T(1,128)} %get-tuple-element.61), channel_id=1, source_target_pairs={{1,0},{2,1},{3,2},{4,3},{5,4},{6,5},{7,6},{8,7},{9,8},{10,9},{11,1... | collective-permute-start | bytes 196616 | tf_op jit(solution)/shard_map/ppermute | solution.py:22
  91.3 7.6 %scatter_custom_fusion.2 = f32[8192]{0:T(1024)S(1)} fusion(s32[1024]{0:T(1024)S(1)} %select_bitcast_fusion, f32[1024]{0:T(1024)S(1)} %get-tuple-element.7, f32[]{:T(128)} %constant.15.clone.1), kind=kCustom, calls=%fused_computation.133 | custom fusion | flops 1024 | bytes 32772
  107.9 6.4 %collective-permute-start.8 = (f32[16,1,1024]{2,1,0:T(1,128)}, f32[16,1,1024]{2,1,0:T(1,128)}, u32[]{:S(2)}, u32[]{:S(2)}) collective-permute-start(f32[16,1,1024]{2,1,0:T(1,128)} %get-tuple-element.55), channel_id=1, source_target_pairs={{1,0},{2,1},{3,2},{4,3},{5,4},{6,5},{7,6},{8,7},{9,8},{10,9},{11,1... | collective-permute-start | bytes 196616 | tf_op jit(solution)/shard_map/ppermute | solution.py:22
  114.3 6.8 %gather_fusion.1 = f32[1024]{0:T(1024)S(1)} fusion(f32[8,1024]{1,0:T(8,128)S(1)} %slice_bitcast_fusion.6, s32[1024]{0:T(1024)S(1)} %get-tuple-element.83), kind=kCustom, calls=%fused_computation.1.clone | custom fusion | bytes 16384 | tf_op jit(solution)/shard_map/jit(take_along_axis)/gather | solution.py:139
  121.8 3.8 %multiply_add_fusion = f32[16,8,1024]{2,1,0:T(8,128)S(1)} fusion(f32[16,8,1024]{2,1,0:T(8,128)} %get-tuple-element.13, f32[16,8,1024]{2,1,0:T(8,128)S(1)} %get-tuple-element.12, f32[16,8,1024]{2,1,0:T(8,128)S(1)} %get-tuple-element.11, f32[16,8,1024]{2,1,0:T(8,128)S(1)} %get-tuple-element.10, f32[16,8,1024]{2,1,0:T(8,128)S(1)} %multiply_add_fusion.2, ...), kind=kLoop, calls=%fused_computation.95 | loop fusion | flops 4325376 | bytes 6488092 | tf_op jit(solution)/shard_map/add | solution.py:126
  126.4 6.8 %gather_fusion = f32[1024]{0:T(1024)S(1)} fusion(f32[8,1024]{1,0:T(8,128)S(1)} %slice_bitcast_fusion.7, s32[1024]{0:T(1024)S(1)} %get-tuple-element.83), kind=kCustom, calls=%fused_computation.clone | custom fusion | bytes 16384 | tf_op jit(solution)/shard_map/jit(take_along_axis)/gather | solution.py:139
  134.4 8.0 %scatter_custom_fusion = f32[8192]{0:T(1024)S(1)} fusion(s32[1024]{0:T(1024)} %copy-done.53, f32[1024]{0:T(1024)S(1)} %get-tuple-element.80, f32[]{:T(128)} %constant.15.clone.1), kind=kCustom, calls=%fused_computation.137 | custom fusion | flops 1024 | bytes 33280
  152.9 6.4 %collective-permute-start.14 = (f32[16,1,1024]{2,1,0:T(1,128)}, f32[16,1,1024]{2,1,0:T(1,128)}, u32[]{:S(2)}, u32[]{:S(2)}) collective-permute-start(f32[16,1,1024]{2,1,0:T(1,128)} %get-tuple-element.39), channel_id=1, source_target_pairs={{1,0},{2,1},{3,2},{4,3},{5,4},{6,5},{7,6},{8,7},{9,8},{10,9},{11,1... | collective-permute-start | bytes 196616 | tf_op jit(solution)/shard_map/ppermute | solution.py:22
  160.0 8.3 %scatter_custom_fusion.3 = f32[8192]{0:T(1024)} fusion(s32[1024]{0:T(1024)} %copy-done.53, f32[1024]{0:T(1024)} %get-tuple-element.81, f32[]{:T(128)} %constant.15.clone.1), kind=kCustom, calls=%fused_computation.131 | custom fusion | flops 1024 | bytes 33280
  169.1 8.3 %scatter_custom_fusion.1 = f32[8192]{0:T(1024)} fusion(s32[1024]{0:T(1024)} %copy-done.53, f32[1024]{0:T(1024)S(1)} %get-tuple-element.82, f32[]{:T(128)} %constant.15.clone.1), kind=kCustom, calls=%fused_computation.135 | custom fusion | flops 1024 | bytes 33280
  189.3 6.5 %collective-permute-start.16 = (f32[16,1,1024]{2,1,0:T(1,128)S(1)}, f32[16,1,1024]{2,1,0:T(1,128)S(1)}, u32[]{:S(2)}, u32[]{:S(2)}) collective-permute-start(f32[16,1,1024]{2,1,0:T(1,128)S(1)} %get-tuple-element.33), channel_id=1, source_target_pairs={{1,0},{2,1},{3,2},{4,3},{5,4},{6,5},{7,6},{8,7},{9,8},{10,9},{11,1... | collective-permute-start | bytes 196616 | tf_op jit(solution)/shard_map/ppermute | solution.py:22
  200.2 6.7 %collective-permute-start.18 = (f32[16,1,1024]{2,1,0:T(1,128)S(1)}, f32[16,1,1024]{2,1,0:T(1,128)S(1)}, u32[]{:S(2)}, u32[]{:S(2)}) collective-permute-start(f32[16,1,1024]{2,1,0:T(1,128)S(1)} %get-tuple-element.27), channel_id=1, source_target_pairs={{1,0},{2,1},{3,2},{4,3},{5,4},{6,5},{7,6},{8,7},{9,8},{10,9},{11,1... | collective-permute-start | bytes 196616 | tf_op jit(solution)/shard_map/ppermute | solution.py:22
  210.5 7.0 %collective-permute-start.20 = (f32[16,1,1024]{2,1,0:T(1,128)S(1)}, f32[16,1,1024]{2,1,0:T(1,128)S(1)}, u32[]{:S(2)}, u32[]{:S(2)}) collective-permute-start(f32[16,1,1024]{2,1,0:T(1,128)S(1)} %get-tuple-element.24), channel_id=1, source_target_pairs={{1,0},{2,1},{3,2},{4,3},{5,4},{6,5},{7,6},{8,7},{9,8},{10,9},{11,1... | collective-permute-start | bytes 196616 | tf_op jit(solution)/shard_map/ppermute | solution.py:22
  220.6 5.0 %collective-permute-done.21 = f32[16,1,1024]{2,1,0:T(1,128)S(1)} collective-permute-done((f32[16,1,1024]{2,1,0:T(1,128)S(1)}, f32[16,1,1024]{2,1,0:T(1,128)S(1)}, u32[]{:S(2)}, u32[]{:S(2)}) %collective-permute-start.21) | collective-permute-done | bytes 65568 | tf_op jit(solution)/shard_map/ppermute | solution.py:19
  225.8 8.3 %fusion.6 = f32[16,8,1024]{2,1,0:T(8,128)} fusion(f32[16,8,1024]{2,1,0:T(8,128)S(1)} %pad_add_fusion, f32[16,1,1024]{2,1,0:T(1,128)S(1)} %collective-permute-done.21, f32[16,1,1024]{2,1,0:T(1,128)S(1)} %collective-permute-done.20, f32[16,8,1024]{2,1,0:T(8,128)S(1)} %copy-done.12, f32[16,1,1024]{2,1,0:T(1,128)} %collective-permute-done.12, ...), kind=kLoop, calls=%fused_computation.15 | loop fusion | flops 18350080 | bytes 27383808 | tf_op jit(solution)/shard_map/mul | solution.py:152
  234.2 67.6 %all-reduce.50.cloned.1.call-done = f32[16,8,1024]{2,1,0:T(8,128)} async-done(((f32[16,8,1024]{2,1,0:T(8,128)}), f32[16,8,1024]{2,1,0:T(8,128)}) %all-reduce.50.cloned.1.call-update) | async-done | bytes 524304 | tf_op jit(solution)/shard_map/psum | solution.py:155
  303.5 8.8 %all_gather.3 = f32[16,8,1024]{2,1,0:T(8,128)S(1)} all-gather(f32[4,8,1024]{2,1,0:T(8,128)S(1)} %get-tuple-element.4), channel_id=1, replica_groups=mesh['shot'=4,'gy'=64] {'shot'}, dimensions={0}, use_global_device_ids=true | all-gather | bytes 655360 | tf_op jit(solution)/shard_map/all_gather | solution.py:163
  (208 shorter events, 86.8 us)
Async XLA Ops:
  7.2 294.6 %all-reduce.50.cloned.1.call-start = ((), (), s32[]{:S(2)}) async-start(), calls=%async_computation | async-start | bytes 1048576 | tf_op jit(solution)/shard_map/psum | solution.py:155
  8.6 33.8 %collective-permute-start.3 = (f32[16,1,1024]{2,1,0:T(1,128)S(1)}, f32[16,1,1024]{2,1,0:T(1,128)S(1)}, u32[]{:S(2)}, u32[]{:S(2)}) collective-permute-start(f32[16,1,1024]{2,1,0:T(1,128)S(1)} %get-tuple-element.78), channel_id=1, source_target_pairs={{0,1},{1,2},{2,3},{3,4},{4,5},{5,6},{6,7},{7,8},{8,9},{9,10},{10,1... | collective-permute-start | bytes 196616 | tf_op jit(solution)/shard_map/ppermute | solution.py:19
  11.8 34.0 %collective-permute-start.1 = (f32[16,1,1024]{2,1,0:T(1,128)S(1)}, f32[16,1,1024]{2,1,0:T(1,128)S(1)}, u32[]{:S(2)}, u32[]{:S(2)}) collective-permute-start(f32[16,1,1024]{2,1,0:T(1,128)S(1)} %get-tuple-element.79), channel_id=1, source_target_pairs={{1,0},{2,1},{3,2},{4,3},{5,4},{6,5},{7,6},{8,7},{9,8},{10,9},{11,1... | collective-permute-start | bytes 196616 | tf_op jit(solution)/shard_map/ppermute | solution.py:22
  18.9 123.5 %collective-permute-start.13 = (f32[16,1,1024]{2,1,0:T(1,128)}, f32[16,1,1024]{2,1,0:T(1,128)S(1)}, u32[]{:S(2)}, u32[]{:S(2)}) collective-permute-start(f32[16,1,1024]{2,1,0:T(1,128)} %get-tuple-element.44), channel_id=1, source_target_pairs={{0,1},{1,2},{2,3},{3,4},{4,5},{5,6},{6,7},{7,8},{8,9},{9,10},{10,1... | collective-permute-start | bytes 196616 | tf_op jit(solution)/shard_map/ppermute | solution.py:19
  20.9 24.9 %collective-permute-start.2 = (f32[16,1,1024]{2,1,0:T(1,128)S(1)}, f32[16,1,1024]{2,1,0:T(1,128)S(1)}, u32[]{:S(2)}, u32[]{:S(2)}) collective-permute-start(f32[16,1,1024]{2,1,0:T(1,128)S(1)} %get-tuple-element.72), channel_id=1, source_target_pairs={{0,1},{1,2},{2,3},{3,4},{4,5},{5,6},{6,7},{7,8},{8,9},{9,10},{10,1... | collective-permute-start | bytes 196616 | tf_op jit(solution)/shard_map/ppermute | solution.py:19
  22.8 23.0 %collective-permute-start = (f32[16,1,1024]{2,1,0:T(1,128)S(1)}, f32[16,1,1024]{2,1,0:T(1,128)S(1)}, u32[]{:S(2)}, u32[]{:S(2)}) collective-permute-start(f32[16,1,1024]{2,1,0:T(1,128)S(1)} %get-tuple-element.73), channel_id=1, source_target_pairs={{1,0},{2,1},{3,2},{4,3},{5,4},{6,5},{7,6},{8,7},{9,8},{10,9},{11,1... | collective-permute-start | bytes 196616 | tf_op jit(solution)/shard_map/ppermute | solution.py:22
  42.4 100.0 %collective-permute-start.11 = (f32[16,1,1024]{2,1,0:T(1,128)}, f32[16,1,1024]{2,1,0:T(1,128)}, u32[]{:S(2)}, u32[]{:S(2)}) collective-permute-start(f32[16,1,1024]{2,1,0:T(1,128)} %get-tuple-element.45), channel_id=1, source_target_pairs={{1,0},{2,1},{3,2},{4,3},{5,4},{6,5},{7,6},{8,7},{9,8},{10,9},{11,1... | collective-permute-start | bytes 196616 | tf_op jit(solution)/shard_map/ppermute | solution.py:22
  50.5 70.7 %copy-start.1 = (f32[16,8,1024]{2,1,0:T(8,128)}, f32[16,8,1024]{2,1,0:T(8,128)S(1)}, u32[]{:S(2)}) copy-start(f32[16,8,1024]{2,1,0:T(8,128)S(1)} %get-tuple-element.12) | copy-start | bytes 1572868
  52.8 15.1 %collective-permute-start.5 = (f32[16,1,1024]{2,1,0:T(1,128)S(1)}, f32[16,1,1024]{2,1,0:T(1,128)S(1)}, u32[]{:S(2)}, u32[]{:S(2)}) collective-permute-start(f32[16,1,1024]{2,1,0:T(1,128)S(1)} %get-tuple-element.66), channel_id=1, source_target_pairs={{0,1},{1,2},{2,3},{3,4},{4,5},{5,6},{6,7},{7,8},{8,9},{9,10},{10,1... | collective-permute-start | bytes 196616 | tf_op jit(solution)/shard_map/ppermute | solution.py:19
  54.7 13.2 %collective-permute-start.4 = (f32[16,1,1024]{2,1,0:T(1,128)S(1)}, f32[16,1,1024]{2,1,0:T(1,128)S(1)}, u32[]{:S(2)}, u32[]{:S(2)}) collective-permute-start(f32[16,1,1024]{2,1,0:T(1,128)S(1)} %get-tuple-element.67), channel_id=1, source_target_pairs={{1,0},{2,1},{3,2},{4,3},{5,4},{6,5},{7,6},{8,7},{9,8},{10,9},{11,1... | collective-permute-start | bytes 196616 | tf_op jit(solution)/shard_map/ppermute | solution.py:22
  81.7 17.2 %collective-permute-start.7 = (f32[16,1,1024]{2,1,0:T(1,128)}, f32[16,1,1024]{2,1,0:T(1,128)}, u32[]{:S(2)}, u32[]{:S(2)}) collective-permute-start(f32[16,1,1024]{2,1,0:T(1,128)} %get-tuple-element.60), channel_id=1, source_target_pairs={{0,1},{1,2},{2,3},{3,4},{4,5},{5,6},{6,7},{7,8},{8,9},{9,10},{10,1... | collective-permute-start | bytes 196616 | tf_op jit(solution)/shard_map/ppermute | solution.py:19
  83.7 15.3 %collective-permute-start.6 = (f32[16,1,1024]{2,1,0:T(1,128)}, f32[16,1,1024]{2,1,0:T(1,128)}, u32[]{:S(2)}, u32[]{:S(2)}) collective-permute-start(f32[16,1,1024]{2,1,0:T(1,128)} %get-tuple-element.61), channel_id=1, source_target_pairs={{1,0},{2,1},{3,2},{4,3},{5,4},{6,5},{7,6},{8,7},{9,8},{10,9},{11,1... | collective-permute-start | bytes 196616 | tf_op jit(solution)/shard_map/ppermute | solution.py:22
  106.0 15.1 %collective-permute-start.9 = (f32[16,1,1024]{2,1,0:T(1,128)}, f32[16,1,1024]{2,1,0:T(1,128)}, u32[]{:S(2)}, u32[]{:S(2)}) collective-permute-start(f32[16,1,1024]{2,1,0:T(1,128)} %get-tuple-element.54), channel_id=1, source_target_pairs={{0,1},{1,2},{2,3},{3,4},{4,5},{5,6},{6,7},{7,8},{8,9},{9,10},{10,1... | collective-permute-start | bytes 196616 | tf_op jit(solution)/shard_map/ppermute | solution.py:19
  107.9 13.2 %collective-permute-start.8 = (f32[16,1,1024]{2,1,0:T(1,128)}, f32[16,1,1024]{2,1,0:T(1,128)}, u32[]{:S(2)}, u32[]{:S(2)}) collective-permute-start(f32[16,1,1024]{2,1,0:T(1,128)} %get-tuple-element.55), channel_id=1, source_target_pairs={{1,0},{2,1},{3,2},{4,3},{5,4},{6,5},{7,6},{8,7},{9,8},{10,9},{11,1... | collective-permute-start | bytes 196616 | tf_op jit(solution)/shard_map/ppermute | solution.py:22
  151.0 33.2 %collective-permute-start.15 = (f32[16,1,1024]{2,1,0:T(1,128)}, f32[16,1,1024]{2,1,0:T(1,128)}, u32[]{:S(2)}, u32[]{:S(2)}) collective-permute-start(f32[16,1,1024]{2,1,0:T(1,128)} %get-tuple-element.38), channel_id=1, source_target_pairs={{0,1},{1,2},{2,3},{3,4},{4,5},{5,6},{6,7},{7,8},{8,9},{9,10},{10,1... | collective-permute-start | bytes 196616 | tf_op jit(solution)/shard_map/ppermute | solution.py:19
  152.9 31.2 %collective-permute-start.14 = (f32[16,1,1024]{2,1,0:T(1,128)}, f32[16,1,1024]{2,1,0:T(1,128)}, u32[]{:S(2)}, u32[]{:S(2)}) collective-permute-start(f32[16,1,1024]{2,1,0:T(1,128)} %get-tuple-element.39), channel_id=1, source_target_pairs={{1,0},{2,1},{3,2},{4,3},{5,4},{6,5},{7,6},{8,7},{9,8},{10,9},{11,1... | collective-permute-start | bytes 196616 | tf_op jit(solution)/shard_map/ppermute | solution.py:22
  178.8 41.8 %collective-permute-start.10 = (f32[16,1,1024]{2,1,0:T(1,128)}, f32[16,1,1024]{2,1,0:T(1,128)}, u32[]{:S(2)}, u32[]{:S(2)}) collective-permute-start(f32[16,1,1024]{2,1,0:T(1,128)} %get-tuple-element.22), channel_id=1, source_target_pairs={{1,0},{2,1},{3,2},{4,3},{5,4},{6,5},{7,6},{8,7},{9,8},{10,9},{11,1... | collective-permute-start | bytes 196616 | tf_op jit(solution)/shard_map/ppermute | solution.py:22
  180.8 39.9 %collective-permute-start.12 = (f32[16,1,1024]{2,1,0:T(1,128)}, f32[16,1,1024]{2,1,0:T(1,128)}, u32[]{:S(2)}, u32[]{:S(2)}) collective-permute-start(f32[16,1,1024]{2,1,0:T(1,128)} %get-tuple-element.23), channel_id=1, source_target_pairs={{0,1},{1,2},{2,3},{3,4},{4,5},{5,6},{6,7},{7,8},{8,9},{9,10},{10,1... | collective-permute-start | bytes 196616 | tf_op jit(solution)/shard_map/ppermute | solution.py:19
  187.3 8.6 %collective-permute-start.17 = (f32[16,1,1024]{2,1,0:T(1,128)S(1)}, f32[16,1,1024]{2,1,0:T(1,128)S(1)}, u32[]{:S(2)}, u32[]{:S(2)}) collective-permute-start(f32[16,1,1024]{2,1,0:T(1,128)S(1)} %get-tuple-element.32), channel_id=1, source_target_pairs={{0,1},{1,2},{2,3},{3,4},{4,5},{5,6},{6,7},{7,8},{8,9},{9,10},{10,1... | collective-permute-start | bytes 196616 | tf_op jit(solution)/shard_map/ppermute | solution.py:19
  189.3 7.8 %collective-permute-start.16 = (f32[16,1,1024]{2,1,0:T(1,128)S(1)}, f32[16,1,1024]{2,1,0:T(1,128)S(1)}, u32[]{:S(2)}, u32[]{:S(2)}) collective-permute-start(f32[16,1,1024]{2,1,0:T(1,128)S(1)} %get-tuple-element.33), channel_id=1, source_target_pairs={{1,0},{2,1},{3,2},{4,3},{5,4},{6,5},{7,6},{8,7},{9,8},{10,9},{11,1... | collective-permute-start | bytes 196616 | tf_op jit(solution)/shard_map/ppermute | solution.py:22
  198.2 8.8 %collective-permute-start.19 = (f32[16,1,1024]{2,1,0:T(1,128)S(1)}, f32[16,1,1024]{2,1,0:T(1,128)S(1)}, u32[]{:S(2)}, u32[]{:S(2)}) collective-permute-start(f32[16,1,1024]{2,1,0:T(1,128)S(1)} %get-tuple-element.26), channel_id=1, source_target_pairs={{0,1},{1,2},{2,3},{3,4},{4,5},{5,6},{6,7},{7,8},{8,9},{9,10},{10,1... | collective-permute-start | bytes 196616 | tf_op jit(solution)/shard_map/ppermute | solution.py:19
  200.2 8.0 %collective-permute-start.18 = (f32[16,1,1024]{2,1,0:T(1,128)S(1)}, f32[16,1,1024]{2,1,0:T(1,128)S(1)}, u32[]{:S(2)}, u32[]{:S(2)}) collective-permute-start(f32[16,1,1024]{2,1,0:T(1,128)S(1)} %get-tuple-element.27), channel_id=1, source_target_pairs={{1,0},{2,1},{3,2},{4,3},{5,4},{6,5},{7,6},{8,7},{9,8},{10,9},{11,1... | collective-permute-start | bytes 196616 | tf_op jit(solution)/shard_map/ppermute | solution.py:22
  210.5 10.1 %collective-permute-start.20 = (f32[16,1,1024]{2,1,0:T(1,128)S(1)}, f32[16,1,1024]{2,1,0:T(1,128)S(1)}, u32[]{:S(2)}, u32[]{:S(2)}) collective-permute-start(f32[16,1,1024]{2,1,0:T(1,128)S(1)} %get-tuple-element.24), channel_id=1, source_target_pairs={{1,0},{2,1},{3,2},{4,3},{5,4},{6,5},{7,6},{8,7},{9,8},{10,9},{11,1... | collective-permute-start | bytes 196616 | tf_op jit(solution)/shard_map/ppermute | solution.py:22
  217.5 8.2 %collective-permute-start.21 = (f32[16,1,1024]{2,1,0:T(1,128)S(1)}, f32[16,1,1024]{2,1,0:T(1,128)S(1)}, u32[]{:S(2)}, u32[]{:S(2)}) collective-permute-start(f32[16,1,1024]{2,1,0:T(1,128)S(1)} %get-tuple-element.25), channel_id=1, source_target_pairs={{0,1},{1,2},{2,3},{3,4},{4,5},{5,6},{6,7},{7,8},{8,9},{9,10},{10,1... | collective-permute-start | bytes 196616 | tf_op jit(solution)/shard_map/ppermute | solution.py:19
  (55 other events, 738.1 us)
Sparse Core Ops, SparseCore 0:
  234.3 67.4 all-reduce.49
where the time goes:
time: 323 us; the launch traced here: 320 us
  starting transfers between devices  86.4 us (27%)
  waiting for transfers between devices  75 us (23%)
  other arithmetic  69.3 us (21%)
  local copies, waits for them, and re-layouts  65.4 us (20%)
  between operations  15.2 us (5%)
  blocking collectives  8.78 us (3%)
    psum x1, waiting for transfers between devices, body(): summed_grad = lax.psum(gradient, 'shot')  67.6 us
    ppermute x11, starting transfers between devices, padded_2(): lax.ppermute(lax.slice_in_dim(block, 0, width, axis=dim), axis, backward)  62.4 us
    unnamed x7, other arithmetic  32.4 us
    gather x4, local copies, waits for them, and re-layouts, body(): record = jnp.take_along_axis(waves[level - 1][0], receivers, axis=1)  27 us
    ppermute x11, starting transfers between devices, padded_2(): lax.ppermute(lax.slice_in_dim(block, block.shape[dim] - width, None, axis...  23.9 us
    slice x18, local copies, waits for them, and re-layouts, toward_prev(): inner = lax.slice_in_dim(field, 0, length - 1, axis=dim_index)  17.5 us
    add x4, other arithmetic, body(): 2.0 * waves[level] - waves[level - 1]  15.1 us
    all_gather x1, blocking collectives, body(): stiffness_new = lax.all_gather(updated, 'shot', axis=0, tiled=True)  8.78 us
  transfers between devices with their start and end apart: 23, of which 4 were waited for; matrix products, arithmetic and copies ran while one was open for 34% of the time, Pallas kernels for 0%

commit v1 on v0

v1 whole, which is shorter than its diff:
```python
import functools

import jax
import jax.numpy as jnp
from jax import lax
from jax.experimental import pallas as pl
from jax.experimental.pallas import tpu as pltpu
from jax.sharding import PartitionSpec as P

TIME_STEP_SQ = 0.15
BETA_ONE = 0.9
BETA_TWO = 0.999
LEARN_RATE = 0.05
ADAM_EPS = 1e-08
ADAM_TICKS = 10.0

NZ = 16
ROWS = 8
XT = 8
LANES = 128
STEPS = 4
REACH = STEPS + 1
EXT = ROWS + 2 * REACH
SIDE_A = 3 * REACH - 1
SIDE_B = 2 * REACH - 1
SURF = STEPS * (STEPS + 1) // 2
HALF = 0.5 * TIME_STEP_SQ

f32 = jnp.float32
VMEM = pl.BlockSpec(memory_space=pltpu.VMEM)
SMEM = pl.BlockSpec(memory_space=pltpu.SMEM)


def native(block):
    planes = block.shape[0]
    return block.reshape(planes, ROWS, XT, LANES).transpose(0, 2, 1, 3).reshape(planes, XT * ROWS, LANES)


def from_native(block):
    planes = block.shape[0]
    return block.reshape(planes, XT, ROWS, LANES).transpose(0, 2, 1, 3).reshape(planes, ROWS, XT * LANES)


def row_of(ref, z, y):
    return ref[z, pl.ds(y, XT, stride=ROWS), :]


def x_next(f, lane):
    r = pltpu.roll(f, LANES - 1, 1)
    return jnp.where(lane == LANES - 1, pltpu.roll(r, XT - 1, 0), r)


def x_prev(f, lane):
    r = pltpu.roll(f, 1, 1)
    return jnp.where(lane == 0, pltpu.roll(r, 1, 0), r)


def iotas():
    lane = lax.broadcasted_iota(jnp.int32, (XT, LANES), 1)
    tile = lax.broadcasted_iota(jnp.int32, (XT, LANES), 0)
    return lane, tile


def pack_kernel(widths, *refs):
    fields, (low, high) = refs[: len(widths)], refs[len(widths) :]

    def plane(z, carry):
        at = 0
        for ref, width in zip(fields, widths, strict=True):
            for k in range(width):
                low[at + k, z] = row_of(ref, z, k)
                high[at + k, z] = row_of(ref, z, ROWS - width + k)
            at += width
        return carry

    lax.fori_loop(0, NZ, plane, 0)


def pack(fields, widths):
    rows = sum(widths)
    shape = jax.ShapeDtypeStruct((rows, NZ, XT, LANES), f32)
    return pl.pallas_call(
        functools.partial(pack_kernel, widths),
        out_shape=(shape, shape),
        in_specs=[VMEM] * len(fields),
        out_specs=(VMEM, VMEM),
        cost_estimate=pl.CostEstimate(flops=0, bytes_accessed=1 << 21, transcendentals=0),
    )(*fields)


def fill(ext, own, low, high, at, width):
    def plane(z, carry):
        for k in range(ROWS):
            ext[REACH + k, z] = row_of(own, z, k)
        return carry

    lax.fori_loop(0, NZ, plane, 0)
    ext[REACH - width : REACH] = low[at : at + width]
    ext[REACH + ROWS : REACH + ROWS + width] = high[at : at + width]


def coefficients(stiff, diag, cx, cy, cz, first, last, lane, tile):
    x_end = (lane == LANES - 1) & (tile == XT - 1)
    x_side = x_end | ((lane == 0) & (tile == 0))

    def rows_y(e, carry):
        for z in range(NZ):
            cy[e, z] = HALF * (stiff[e, z] + stiff[e + 1, z])
        return carry

    lax.fori_loop(0, EXT - 1, rows_y, 0)

    def rows(e, carry):
        below = None
        for z in range(NZ):
            s = stiff[e, z]
            face = jnp.where(x_end, 0.0, HALF * (s + x_next(s, lane)))
            total = face + x_prev(face, lane) + jnp.where(x_side, HALF * s, 0.0)
            above = HALF * (s + stiff[e, z + 1]) if z < NZ - 1 else HALF * s
            total = total + above + (below if z > 0 else HALF * s) + cy[e, z] + cy[e - 1, z]
            cx[e, z] = face
            cz[e, z] = above
            diag[e, z] = 2.0 - total
            below = above
        return carry

    lax.fori_loop(1, EXT - 1, rows, 0)

    @pl.when(first)
    def _():
        cy[REACH - 1] = jnp.zeros((NZ, XT, LANES), f32)

    @pl.when(last)
    def _():
        cy[REACH + ROWS - 1] = jnp.zeros((NZ, XT, LANES), f32)


def leap(now, before, after, diag, cx, cy, cz, lo, hi, lane):
    def rows(e, carry):
        for z in range(NZ):
            u = now[e, z]
            c = cx[e, z]
            acc = diag[e, z] * u - before[e, z]
            acc = acc + c * x_next(u, lane) + x_prev(c * u, lane)
            acc = acc + cy[e, z] * now[e + 1, z] + cy[e - 1, z] * now[e - 1, z]
            if z < NZ - 1:
                acc = acc + cz[e, z] * now[e, z + 1]
            if z > 0:
                acc = acc + cz[e, z - 1] * now[e, z - 1]
            after[e, z] = acc
        return carry

    lax.fori_loop(lo, hi, rows, 0)


def forward_kernel(
    place, source_pos, source_wave, u0, u1, s, low, high, receivers, observed,
    waves, diag, cx, cy, cz, surf, surf_low, surf_high,
    stiff, before,
):
    lane, tile = iotas()
    fill(stiff, s, low, high, 0, REACH)
    fill(waves.at[0], u1, low, high, REACH, REACH)
    fill(before, u0, low, high, 2 * REACH, REACH - 1)
    coefficients(stiff, diag, cx, cy, cz, place[1] == 1, place[2] == 1, lane, tile)
    z_src = source_pos[0, 0]
    e_src = source_pos[0, 1] - place[0] + REACH
    x_src = source_pos[0, 2]
    spot = (tile * LANES + lane) == x_src
    for k in range(STEPS):
        older = before if k == 0 else waves.at[k - 1]
        leap(waves.at[k], older, waves.at[k + 1], diag, cx, cy, cz, k + 1, EXT - 1 - k, lane)

        @pl.when((e_src >= k + 1) & (e_src < EXT - 1 - k))
        def _():
            add = jnp.where(spot, TIME_STEP_SQ * source_wave[0, k], 0.0)
            waves[k + 1, e_src, z_src] = waves[k + 1, e_src, z_src] + add

    column = lax.broadcasted_iota(jnp.int32, (LANES, LANES), 0)
    for y in range(ROWS):
        at = receivers[y : y + 1, :]
        pick = jnp.where(column == (at & (LANES - 1)), 1.0, 0.0)
        held = jnp.where(tile == (at >> 7), 1.0, 0.0)
        top = jnp.concatenate([waves[k, REACH + y, 0] for k in range(1, STEPS + 1)], 0)
        lanes_of = jnp.dot(top, pick, precision=lax.Precision.HIGHEST, preferred_element_type=f32)
        parts = []
        for k in range(STEPS):
            record = jnp.sum(lanes_of[k * XT : (k + 1) * XT] * held, axis=0, keepdims=True)
            parts.append(held * (record - observed[k, y : y + 1, :]))
        back = lax.dot_general(
            jnp.concatenate(parts, 0), pick, (((1,), (1,)), ((), ())),
            precision=lax.Precision.HIGHEST, preferred_element_type=f32,
        )
        for k in range(STEPS):
            surf[k, y] = back[k * XT : (k + 1) * XT]
    at = 0
    for k in range(STEPS - 1, -1, -1):
        width = k + 1
        surf_low[at : at + width] = surf[k, :width]
        surf_high[at : at + width] = surf[k, ROWS - width :]
        at += width


def forward(place, source_pos, source_wave, u0, u1, s, low, high, receivers, observed):
    field = (EXT, NZ, XT, LANES)
    one = jax.ShapeDtypeStruct(field, f32)
    edge = jax.ShapeDtypeStruct((SURF, XT, LANES), f32)
    return pl.pallas_call(
        forward_kernel,
        out_shape=(
            jax.ShapeDtypeStruct((STEPS + 1, *field), f32),
            one, one, one, one,
            jax.ShapeDtypeStruct((STEPS, ROWS, XT, LANES), f32),
            edge, edge,
        ),
        in_specs=[SMEM] * 3 + [VMEM] * 7,
        out_specs=(VMEM,) * 8,
        scratch_shapes=[pltpu.VMEM(field, f32)] * 2,
        compiler_params=pltpu.CompilerParams(vmem_limit_bytes=40 << 20),
        cost_estimate=pl.CostEstimate(flops=1 << 25, bytes_accessed=1 << 24, transcendentals=0),
    )(place, source_pos, source_wave, u0, u1, s, low, high, receivers, observed)


def adjoint_kernel(
    place, l6, l7, low, high, waves, diag, cx, cy, cz, surf, surf_low, surf_high,
    keep, send,
    lams, before, face_y, grad,
):
    lane, tile = iotas()
    x_end = (lane == LANES - 1) & (tile == XT - 1)
    x_side = x_end | ((lane == 0) & (tile == 0))
    fill(lams.at[0], l6, low, high, 0, REACH)
    fill(before, l7, low, high, REACH, REACH - 1)
    at = 0
    for k in range(STEPS):
        older = before if k == 0 else lams.at[k - 1]
        leap(lams.at[k], older, lams.at[k + 1], diag, cx, cy, cz, k + 1, EXT - 1 - k, lane)
        width = STEPS - k
        for j in range(width):
            e = REACH - width + j
            lams[k + 1, e, 0] = lams[k + 1, e, 0] + surf_low[at + j]
            e = REACH + ROWS + j
            lams[k + 1, e, 0] = lams[k + 1, e, 0] + surf_high[at + j]
        for j in range(ROWS):
            e = REACH + j
            lams[k + 1, e, 0] = lams[k + 1, e, 0] + surf[STEPS - 1 - k, j]
        at += width

    levels = STEPS + 1

    def edge_rows(z, carry):
        total = None
        for n in range(levels):
            m = STEPS - n
            part = (waves[n, REACH, z] - waves[n, REACH - 1, z]) * (lams[m, REACH, z] - lams[m, REACH - 1, z])
            total = part if total is None else total + part
        face_y[z] = total
        return carry

    lax.fori_loop(0, NZ, edge_rows, 0)

    def rows(y, carry):
        e = y + REACH
        below = None
        us = [waves[n, e, 0] for n in range(levels)]
        ls = [lams[STEPS - n, e, 0] for n in range(levels)]
        for z in range(NZ):
            fx = fy = fz = cell = None
            next_us, next_ls = [], []
            for n in range(levels):
                m = STEPS - n
                u, l = us[n], ls[n]
                px = (x_next(u, lane) - u) * (x_next(l, lane) - l)
                py = (waves[n, e + 1, z] - u) * (lams[m, e + 1, z] - l)
                both = u * l
                if z < NZ - 1:
                    un, ln = waves[n, e, z + 1], lams[m, e, z + 1]
                    next_us.append(un)
                    next_ls.append(ln)
                    pz = (un - u) * (ln - l)
                else:
                    pz = both
                fx = px if fx is None else fx + px
                fy = py if fy is None else fy + py
                fz = pz if fz is None else fz + pz
                cell = both if cell is None else cell + both
            us, ls = next_us, next_ls
            fx = jnp.where(x_end, 0.0, fx)
            total = fx + x_prev(fx, lane) + jnp.where(x_side, cell, 0.0)
            total = total + fy + face_y[z] + fz + (cell if z == 0 else below)
            face_y[z] = fy
            below = fz
            grad[z, pl.ds(y, XT, stride=ROWS), :] = -HALF * total
        return carry

    lax.fori_loop(0, ROWS, rows, 0)
    core = place[3]
    for group in range(2):
        keep[group] = grad[pl.ds(8 * group + 4 * core, 4)]
        send[group] = grad[pl.ds(8 * group + 4 * (1 - core), 4)]


def adjoint(place, l6, l7, low, high, waves, diag, cx, cy, cz, surf, surf_low, surf_high):
    field = (EXT, NZ, XT, LANES)
    part = jax.ShapeDtypeStruct((2, 4, XT * ROWS, LANES), f32)
    return pl.pallas_call(
        adjoint_kernel,
        out_shape=(part, part),
        in_specs=[SMEM] + [VMEM] * 12,
        out_specs=(VMEM, VMEM),
        scratch_shapes=[
            pltpu.VMEM((STEPS + 1, *field), f32),
            pltpu.VMEM(field, f32),
            pltpu.VMEM((NZ, XT, LANES), f32),
            pltpu.VMEM((NZ, XT * ROWS, LANES), f32),
        ],
        compiler_params=pltpu.CompilerParams(vmem_limit_bytes=40 << 20),
        cost_estimate=pl.CostEstimate(flops=1 << 25, bytes_accessed=1 << 24, transcendentals=0),
    )(place, l6, l7, low, high, waves, diag, cx, cy, cz, surf, surf_low, surf_high)


def to_next(block):
    count = lax.axis_size("gy")
    return lax.ppermute(block, "gy", [(i, i + 1) for i in range(count - 1)])


def to_prev(block):
    count = lax.axis_size("gy")
    return lax.ppermute(block, "gy", [(i + 1, i) for i in range(count - 1)])


def swap_core(block):
    return lax.ppermute(block, "shot", [(0, 1), (1, 0), (2, 3), (3, 2)])


def swap_far(block):
    return lax.ppermute(block, "shot", [(0, 2), (2, 0), (1, 3), (3, 1)])


def body(
    stiffness,
    first_moment,
    second_moment,
    wave_prev,
    wave_now,
    adjoint_next,
    adjoint_now,
    observed,
    receiver_x,
    source_pos,
    source_wave,
):
    gy = lax.axis_index("gy")
    shot = lax.axis_index("shot")
    core, far = shot % 2, shot // 2
    place = jnp.stack([gy * ROWS, gy == 0, gy == lax.axis_size("gy") - 1, core]).astype(jnp.int32)
    s = native(stiffness)
    u0, u1 = native(wave_prev[0]), native(wave_now[0])
    l6, l7 = native(adjoint_now[0]), native(adjoint_next[0])
    first, second = native(first_moment), native(second_moment)

    a_low, a_high = pack((s, u1, u0), (REACH, REACH, REACH - 1))
    a_high, a_low = to_next(a_high), to_prev(a_low)
    b_low, b_high = pack((l6, l7), (REACH, REACH - 1))
    b_high, b_low = to_next(b_high), to_prev(b_low)
    moments = swap_far(jnp.stack([first, second]))

    waves, diag, cx, cy, cz, surf, surf_low, surf_high = forward(
        place, source_pos, source_wave, u0, u1, s, a_high, a_low, receiver_x[0], observed[0]
    )
    surf_high, surf_low = to_next(surf_high), to_prev(surf_low)
    keep, send = adjoint(
        place, l6, l7, b_high, b_low, waves, diag, cx, cy, cz, surf, surf_high, surf_low
    )
    chip_sum = keep + swap_core(send)
    share = chip_sum + swap_far(chip_sum)

    is_far = (jnp.arange(2) == far)[:, None, None, None]
    first_two = jnp.where(is_far, first[None], moments[0][None])
    second_two = jnp.where(is_far, second[None], moments[1][None])
    stiff_two = jnp.where(core == 0, s.reshape(2, 2, 4, XT * ROWS, LANES)[:, 0], s.reshape(2, 2, 4, XT * ROWS, LANES)[:, 1])
    first_new = BETA_ONE * first_two + (1.0 - BETA_ONE) * share
    second_new = BETA_TWO * second_two + (1.0 - BETA_TWO) * share * share
    updated = stiff_two - LEARN_RATE * (first_new / (1.0 - BETA_ONE**ADAM_TICKS)) / (
        jnp.sqrt(second_new / (1.0 - BETA_TWO**ADAM_TICKS)) + ADAM_EPS
    )
    other = swap_core(updated)
    even = jnp.where(core == 0, updated, other)
    odd = jnp.where(core == 0, other, updated)
    stiffness_new = jnp.stack([even, odd], 1).reshape(NZ, XT * ROWS, LANES)
    first_out = jnp.where(far == 0, first_new[0], first_new[1])
    second_out = jnp.where(far == 0, second_new[0], second_new[1])
    return (from_native(stiffness_new), from_native(first_out), from_native(second_out))


def solution(mesh):
    return jax.shard_map(
        body,
        mesh=mesh,
        in_specs=(
            P(None, "gy", None),
            P("shot", "gy", None),
            P("shot", "gy", None),
            P("shot", None, "gy", None),
            P("shot", None, "gy", None),
            P("shot", None, "gy", None),
            P("shot", None, "gy", None),
            P("shot", None, "gy", None),
            P("shot", "gy", None),
            P("shot", None),
            P("shot", None),
        ),
        out_specs=(P(None, "gy", None), P("shot", "gy", None), P("shot", "gy", None)),
        check_vma=False,
    )
```

time: 323 us -> 100 us (0.31)
  the two profiles are of different devices: /device:TPU:97 before, /device:TPU:127 now
where the time goes in v1:
time: 100 us
  Pallas kernels  36.1 us (36%)
  waiting for transfers between devices  31.4 us (31%)
  starting transfers between devices  29.8 us (30%)
  other arithmetic  1.22 us (1%)
    pallas_call x1, Pallas kernels, adjoint(): pl.pallas_call(adjoint_kernel, out_shape=(part, part), in_specs=[SMEM] +...  15.3 us
    pallas_call x1, Pallas kernels, forward(): pl.pallas_call(forward_kernel, out_shape=(jax.ShapeDtypeStruct((STEPS + 1...  15.2 us
    ppermute x3, starting transfers between devices, to_next(): return lax.ppermute(block, 'gy', [(i, i + 1) for i in range(count - 1)])  14.2 us
    ppermute x3, waiting for transfers between devices, to_prev(): return lax.ppermute(block, 'gy', [(i + 1, i) for i in range(count - 1)])  13.5 us
    ppermute x2, waiting for transfers between devices, swap_far(): return lax.ppermute(block, 'shot', [(0, 2), (2, 0), (1, 3), (3, 1)])  11.9 us
    ppermute x3, starting transfers between devices, to_prev(): return lax.ppermute(block, 'gy', [(i + 1, i) for i in range(count - 1)])  7.2 us
    pallas_call x2, Pallas kernels, pack(): pl.pallas_call(functools.partial(pack_kernel, widths), out_shape=(shape,...  5.5 us
    ppermute x2, starting transfers between devices, swap_core(): return lax.ppermute(block, 'shot', [(0, 1), (1, 0), (2, 3), (3, 2)])  5.47 us
  transfers between devices with their start and end apart: 10, of which 7 were waited for; matrix products, arithmetic and copies ran while one was open for 1% of the time, Pallas kernels for 18%

profile of v1, /device:TPU:127, one launch (start us, length us, event | category | flops | bytes accessed | tf_op | source)
XLA Modules:
  0.0 100.2 jit_solution(9897956605057414866)
XLA Ops:
  0.7 3.1 %shard_map.131 = (f32[14,16,8,128]{3,2,1,0:T(8,128)}, f32[14,16,8,128]{3,2,1,0:T(8,128)}) custom-call(f32[16,64,128]{2,1,0:T(8,128)} %bitcast.88, f32[16,64,128]{2,1,0:T(8,128)} %bitcast.97, f32[16,64,128]{2,1,0:T(8,128)} %bitcast.95), custom_call_target="tpu_custom_call" | custom-call | bytes 2097152 | tf_op jit(solution)/shard_map/pallas_call | solution.py:82
  3.8 4.7 %collective-permute-start.3 = (f32[14,16,8,128]{3,2,1,0:T(8,128)}, f32[14,16,8,128]{3,2,1,0:T(8,128)S(1)}, u32[]{:S(2)}, u32[]{:S(2)}) collective-permute-start(f32[14,16,8,128]{3,2,1,0:T(8,128)} %get-tuple-element.19), channel_id=1, source_target_pairs={{0,1},{1,2},{2,3},{3,4},{4,5},{5,6},{6,7},{7,8},{8,9},{9,10},{10,1... | collective-permute-start | bytes 2752520 | tf_op jit(solution)/shard_map/ppermute | solution.py:324
  8.4 1.9 %collective-permute-start.4 = (f32[14,16,8,128]{3,2,1,0:T(8,128)}, f32[14,16,8,128]{3,2,1,0:T(8,128)S(1)}, u32[]{:S(2)}, u32[]{:S(2)}) collective-permute-start(f32[14,16,8,128]{3,2,1,0:T(8,128)} %get-tuple-element.20), channel_id=1, source_target_pairs={{1,0},{2,1},{3,2},{4,3},{5,4},{6,5},{7,6},{8,7},{9,8},{10,9},{11,1... | collective-permute-start | bytes 2752520 | tf_op jit(solution)/shard_map/ppermute | solution.py:329
  10.4 2.4 %shard_map.130 = (f32[9,16,8,128]{3,2,1,0:T(8,128)}, f32[9,16,8,128]{3,2,1,0:T(8,128)}) custom-call(f32[16,64,128]{2,1,0:T(8,128)} %bitcast.91, f32[16,64,128]{2,1,0:T(8,128)} %bitcast.93), custom_call_target="tpu_custom_call" | custom-call | bytes 2097152 | tf_op jit(solution)/shard_map/pallas_call | solution.py:82
  12.8 7.6 %collective-permute-start.1 = (f32[9,16,8,128]{3,2,1,0:T(8,128)}, f32[9,16,8,128]{3,2,1,0:T(8,128)}, u32[]{:S(2)}, u32[]{:S(2)}) collective-permute-start(f32[9,16,8,128]{3,2,1,0:T(8,128)} %get-tuple-element.17), channel_id=1, source_target_pairs={{0,1},{1,2},{2,3},{3,4},{4,5},{5,6},{6,7},{7,8},{8,9},{9,10},{10,1... | collective-permute-start | bytes 1769480 | tf_op jit(solution)/shard_map/ppermute | solution.py:324
  20.4 1.9 %collective-permute-start.2 = (f32[9,16,8,128]{3,2,1,0:T(8,128)}, f32[9,16,8,128]{3,2,1,0:T(8,128)}, u32[]{:S(2)}, u32[]{:S(2)}) collective-permute-start(f32[9,16,8,128]{3,2,1,0:T(8,128)} %get-tuple-element.18), channel_id=1, source_target_pairs={{1,0},{2,1},{3,2},{4,3},{5,4},{6,5},{7,6},{8,7},{9,8},{10,9},{11,1... | collective-permute-start | bytes 1769480 | tf_op jit(solution)/shard_map/ppermute | solution.py:329
  22.4 5.3 %collective-permute-done.3.low = f32[14,16,8,128]{3,2,1,0:T(8,128)S(1)} collective-permute-done((f32[14,16,8,128]{3,2,1,0:T(8,128)}, f32[14,16,8,128]{3,2,1,0:T(8,128)S(1)}, u32[]{:S(2)}, u32[]{:S(2)}) %collective-permute-start.3) | collective-permute-done | bytes 917536 | tf_op jit(solution)/shard_map/ppermute | solution.py:324
  27.7 7.9 %collective-permute-done.4.high = f32[14,16,8,128]{3,2,1,0:T(8,128)S(1)} collective-permute-done((f32[14,16,8,128]{3,2,1,0:T(8,128)}, f32[14,16,8,128]{3,2,1,0:T(8,128)S(1)}, u32[]{:S(2)}, u32[]{:S(2)}) %collective-permute-start.4) | collective-permute-done | bytes 917536 | tf_op jit(solution)/shard_map/ppermute | solution.py:329
  35.7 15.2 %shard_map.132 = (f32[5,18,16,8,128]{4,3,2,1,0:T(8,128)S(1)}, f32[18,16,8,128]{3,2,1,0:T(8,128)S(1)}, f32[18,16,8,128]{3,2,1,0:T(8,128)S(1)}, f32[18,16,8,128]{3...) custom-call(s32[4]{0:T(128)S(1)} %pad_add_fusion.place, ...), custom_call_target="tpu_custom_call" | custom-call | flops 33554432 | bytes 16777216 | tf_op jit(solution)/shard_map/pallas_call | solution.py:208
  50.9 1.9 %collective-permute-start.5 = (f32[10,8,128]{2,1,0:T(8,128)S(1)}, f32[10,8,128]{2,1,0:T(8,128)S(1)}, u32[]{:S(2)}, u32[]{:S(2)}) collective-permute-start(f32[10,8,128]{2,1,0:T(8,128)S(1)} %get-tuple-element.27), channel_id=1, source_target_pairs={{0,1},{1,2},{2,3},{3,4},{4,5},{5,6},{6,7},{7,8},{8,9},{9,10},{10,1... | collective-permute-start | bytes 122888 | tf_op jit(solution)/shard_map/ppermute | solution.py:324
  52.9 3.4 %collective-permute-start.6 = (f32[10,8,128]{2,1,0:T(8,128)S(1)}, f32[10,8,128]{2,1,0:T(8,128)S(1)}, u32[]{:S(2)}, u32[]{:S(2)}) collective-permute-start(f32[10,8,128]{2,1,0:T(8,128)S(1)} %get-tuple-element.28), channel_id=1, source_target_pairs={{1,0},{2,1},{3,2},{4,3},{5,4},{6,5},{7,6},{8,7},{9,8},{10,9},{11,1... | collective-permute-start | bytes 122888 | tf_op jit(solution)/shard_map/ppermute | solution.py:329
  56.3 5.6 %collective-permute-done.6.surf_high = f32[10,8,128]{2,1,0:T(8,128)S(1)} collective-permute-done((f32[10,8,128]{2,1,0:T(8,128)S(1)}, f32[10,8,128]{2,1,0:T(8,128)S(1)}, u32[]{:S(2)}, u32[]{:S(2)}) %collective-permute-start.6) | collective-permute-done | bytes 40992 | tf_op jit(solution)/shard_map/ppermute | solution.py:329
  61.9 15.3 %shard_map.133 = (f32[2,4,64,128]{3,2,1,0:T(8,128)S(1)}, f32[2,4,64,128]{3,2,1,0:T(8,128)S(1)}) custom-call(s32[4]{0:T(128)S(1)} %pad_add_fusion.place, f32[16,64,128]{2,1,0:T(8,128)S(1)} %bitcast.92, f32[16,64,128]{2,1,0:T(8,128)S(1)} %bitcast.94, f32[9,16,8,128]{3,2,1,0:T(8,128)} %collective-permute-done.1.low, ...), custom_call_target="tpu_custom_call" | custom-call | flops 33554432 | bytes 16777216 | tf_op jit(solution)/shard_map/pallas_call | solution.py:306
  77.2 4.6 %collective-permute-start.7 = (f32[2,4,64,128]{3,2,1,0:T(8,128)S(1)}, f32[2,4,64,128]{3,2,1,0:T(8,128)S(1)}, u32[]{:S(2)}, u32[]{:S(2)}) collective-permute-start(f32[2,4,64,128]{3,2,1,0:T(8,128)S(1)} %get-tuple-element.30), channel_id=1, source_target_pairs={{0,64},{64,0},{128,192},{192,128},{1,65},{65,1},{129,193},{193,129... | collective-permute-start | bytes 786440 | tf_op jit(solution)/shard_map/ppermute | solution.py:333
  81.8 0.9 collective-permute-start
  82.7 0.2 collective-permute-done.7
  83.0 2.0 %collective-permute-start.8 = (f32[2,4,64,128]{3,2,1,0:T(8,128)S(1)}, f32[2,4,64,128]{3,2,1,0:T(8,128)S(1)}, u32[]{:S(2)}, u32[]{:S(2)}) collective-permute-start(f32[2,4,64,128]{3,2,1,0:T(8,128)S(1)} %add.24), channel_id=1, source_target_pairs={{0,128},{128,0},{64,192},{192,64},{1,129},{129,1},{65,193},{193,65... | collective-permute-start | bytes 786440 | tf_op jit(solution)/shard_map/ppermute | solution.py:337
  85.0 6.3 %collective-permute-done = f32[2,4,64,128]{3,2,1,0:T(8,128)S(1)} collective-permute-done((f32[2,4,64,128]{3,2,1,0:T(8,128)S(1)}, f32[2,4,64,128]{3,2,1,0:T(8,128)S(1)}, u32[]{:S(2)}, u32[]{:S(2)}) %collective-permute-start) | collective-permute-done | bytes 262176 | tf_op jit(solution)/shard_map/ppermute | solution.py:337
  91.3 5.6 %collective-permute-done.8 = f32[2,4,64,128]{3,2,1,0:T(8,128)S(1)} collective-permute-done((f32[2,4,64,128]{3,2,1,0:T(8,128)S(1)}, f32[2,4,64,128]{3,2,1,0:T(8,128)S(1)}, u32[]{:S(2)}, u32[]{:S(2)}) %collective-permute-start.8) | collective-permute-done | bytes 262176 | tf_op jit(solution)/shard_map/ppermute | solution.py:337
  96.9 0.3 fusion.3
  97.2 0.9 collective-permute-start.9
  98.1 0.7 fusion.4
  98.8 0.4 collective-permute-done.9
  99.4 0.8 copy.16
  (32 shorter events, 0.3 us)
Async XLA Ops:
  0.6 35.0 %copy-start = (f32[16,8,1024]{2,1,0:T(8,128)S(1)}, f32[16,8,1024]{2,1,0:T(8,128)}, u32[]{:S(2)}) copy-start(f32[16,8,1024]{2,1,0:T(8,128)} %param.11) | copy-start | bytes 1572868
  0.6 35.0 %copy-start.3 = (f32[1,16,8,1024]{3,2,1,0:T(8,128)S(1)}, f32[1,16,8,1024]{3,2,1,0:T(8,128)}, u32[]{:S(2)}) copy-start(f32[1,16,8,1024]{3,2,1,0:T(8,128)} %param.14) | copy-start | bytes 1572868
  0.7 35.0 %copy-start.4 = (f32[1,16,8,1024]{3,2,1,0:T(8,128)S(1)}, f32[1,16,8,1024]{3,2,1,0:T(8,128)}, u32[]{:S(2)}) copy-start(f32[1,16,8,1024]{3,2,1,0:T(8,128)} %param.15) | copy-start | bytes 1572868
  0.7 35.0 %copy-start.5 = (f32[1,4,8,128]{3,2,1,0:T(8,128)S(1)}, f32[1,4,8,128]{3,2,1,0:T(8,128)}, u32[]{:S(2)}) copy-start(f32[1,4,8,128]{3,2,1,0:T(8,128)} %param.18) | copy-start | bytes 49156
  0.7 35.0 %copy-start.6 = (s32[1,8,128]{2,1,0:T(8,128)S(1)}, s32[1,8,128]{2,1,0:T(8,128)}, u32[]{:S(2)}) copy-start(s32[1,8,128]{2,1,0:T(8,128)} %param.19) | copy-start | bytes 12292
  0.7 35.0 %copy-start.7 = (s32[1,3]{1,0:T(1,128)S(1)}, s32[1,3]{1,0:T(1,128)}, u32[]{:S(2)}) copy-start(s32[1,3]{1,0:T(1,128)} %source_pos.1) | copy-start | bytes 40
  0.7 35.0 %copy-start.8 = (f32[1,4]{1,0:T(1,128)S(1)}, f32[1,4]{1,0:T(1,128)}, u32[]{:S(2)}) copy-start(f32[1,4]{1,0:T(1,128)} %source_wave.1) | copy-start | bytes 52
  3.8 24.0 %collective-permute-start.3 = (f32[14,16,8,128]{3,2,1,0:T(8,128)}, f32[14,16,8,128]{3,2,1,0:T(8,128)S(1)}, u32[]{:S(2)}, u32[]{:S(2)}) collective-permute-start(f32[14,16,8,128]{3,2,1,0:T(8,128)} %get-tuple-element.19), channel_id=1, source_target_pairs={{0,1},{1,2},{2,3},{3,4},{4,5},{5,6},{6,7},{7,8},{8,9},{9,10},{10,1... | collective-permute-start | bytes 2752520 | tf_op jit(solution)/shard_map/ppermute | solution.py:324
  8.4 27.2 %collective-permute-start.4 = (f32[14,16,8,128]{3,2,1,0:T(8,128)}, f32[14,16,8,128]{3,2,1,0:T(8,128)S(1)}, u32[]{:S(2)}, u32[]{:S(2)}) collective-permute-start(f32[14,16,8,128]{3,2,1,0:T(8,128)} %get-tuple-element.20), channel_id=1, source_target_pairs={{1,0},{2,1},{3,2},{4,3},{5,4},{6,5},{7,6},{8,7},{9,8},{10,9},{11,1... | collective-permute-start | bytes 2752520 | tf_op jit(solution)/shard_map/ppermute | solution.py:329
  12.8 43.5 %collective-permute-start.1 = (f32[9,16,8,128]{3,2,1,0:T(8,128)}, f32[9,16,8,128]{3,2,1,0:T(8,128)}, u32[]{:S(2)}, u32[]{:S(2)}) collective-permute-start(f32[9,16,8,128]{3,2,1,0:T(8,128)} %get-tuple-element.17), channel_id=1, source_target_pairs={{0,1},{1,2},{2,3},{3,4},{4,5},{5,6},{6,7},{7,8},{8,9},{9,10},{10,1... | collective-permute-start | bytes 1769480 | tf_op jit(solution)/shard_map/ppermute | solution.py:324
  20.4 35.9 %collective-permute-start.2 = (f32[9,16,8,128]{3,2,1,0:T(8,128)}, f32[9,16,8,128]{3,2,1,0:T(8,128)}, u32[]{:S(2)}, u32[]{:S(2)}) collective-permute-start(f32[9,16,8,128]{3,2,1,0:T(8,128)} %get-tuple-element.18), channel_id=1, source_target_pairs={{1,0},{2,1},{3,2},{4,3},{5,4},{6,5},{7,6},{8,7},{9,8},{10,9},{11,1... | collective-permute-start | bytes 1769480 | tf_op jit(solution)/shard_map/ppermute | solution.py:329
  35.7 26.1 %copy-start.1 = (f32[1,16,8,1024]{3,2,1,0:T(8,128)S(1)}, f32[1,16,8,1024]{3,2,1,0:T(8,128)}, u32[]{:S(2)}) copy-start(f32[1,16,8,1024]{3,2,1,0:T(8,128)} %param.17) | copy-start | bytes 1572868
  35.7 26.1 %copy-start.2 = (f32[1,16,8,1024]{3,2,1,0:T(8,128)S(1)}, f32[1,16,8,1024]{3,2,1,0:T(8,128)}, u32[]{:S(2)}) copy-start(f32[1,16,8,1024]{3,2,1,0:T(8,128)} %param.16) | copy-start | bytes 1572868
  50.9 5.3 %collective-permute-start.5 = (f32[10,8,128]{2,1,0:T(8,128)S(1)}, f32[10,8,128]{2,1,0:T(8,128)S(1)}, u32[]{:S(2)}, u32[]{:S(2)}) collective-permute-start(f32[10,8,128]{2,1,0:T(8,128)S(1)} %get-tuple-element.27), channel_id=1, source_target_pairs={{0,1},{1,2},{2,3},{3,4},{4,5},{5,6},{6,7},{7,8},{8,9},{9,10},{10,1... | collective-permute-start | bytes 122888 | tf_op jit(solution)/shard_map/ppermute | solution.py:324
  52.9 9.0 %collective-permute-start.6 = (f32[10,8,128]{2,1,0:T(8,128)S(1)}, f32[10,8,128]{2,1,0:T(8,128)S(1)}, u32[]{:S(2)}, u32[]{:S(2)}) collective-permute-start(f32[10,8,128]{2,1,0:T(8,128)S(1)} %get-tuple-element.28), channel_id=1, source_target_pairs={{1,0},{2,1},{3,2},{4,3},{5,4},{6,5},{7,6},{8,7},{9,8},{10,9},{11,1... | collective-permute-start | bytes 122888 | tf_op jit(solution)/shard_map/ppermute | solution.py:329
  61.9 19.9 %copy-start.9 = (f32[4,8,1024]{2,1,0:T(8,128)S(1)}, f32[4,8,1024]{2,1,0:T(8,128)}, u32[]{:S(2)}) copy-start(f32[4,8,1024]{2,1,0:T(8,128)} %param.13) | copy-start | bytes 393220
  61.9 19.9 %copy-start.10 = (f32[4,8,1024]{2,1,0:T(8,128)S(1)}, f32[4,8,1024]{2,1,0:T(8,128)}, u32[]{:S(2)}) copy-start(f32[4,8,1024]{2,1,0:T(8,128)} %param.12) | copy-start | bytes 393220
  77.2 5.7 %collective-permute-start.7 = (f32[2,4,64,128]{3,2,1,0:T(8,128)S(1)}, f32[2,4,64,128]{3,2,1,0:T(8,128)S(1)}, u32[]{:S(2)}, u32[]{:S(2)}) collective-permute-start(f32[2,4,64,128]{3,2,1,0:T(8,128)S(1)} %get-tuple-element.30), channel_id=1, source_target_pairs={{0,64},{64,0},{128,192},{192,128},{1,65},{65,1},{129,193},{193,129... | collective-permute-start | bytes 786440 | tf_op jit(solution)/shard_map/ppermute | solution.py:333
  81.8 9.5 %collective-permute-start = (f32[2,4,64,128]{3,2,1,0:T(8,128)S(1)}, f32[2,4,64,128]{3,2,1,0:T(8,128)S(1)}, u32[]{:S(2)}, u32[]{:S(2)}) collective-permute-start(f32[2,4,64,128]{3,2,1,0:T(8,128)S(1)} %pad_maximum_fusion.1), channel_id=1, source_target_pairs={{0,128},{128,0},{64,192},{192,64},{1,129},{129,1},{65,193},{193,65... | collective-permute-start | bytes 786440 | tf_op jit(solution)/shard_map/ppermute | solution.py:337
  83.0 13.9 %collective-permute-start.8 = (f32[2,4,64,128]{3,2,1,0:T(8,128)S(1)}, f32[2,4,64,128]{3,2,1,0:T(8,128)S(1)}, u32[]{:S(2)}, u32[]{:S(2)}) collective-permute-start(f32[2,4,64,128]{3,2,1,0:T(8,128)S(1)} %add.24), channel_id=1, source_target_pairs={{0,128},{128,0},{64,192},{192,64},{1,129},{129,1},{65,193},{193,65... | collective-permute-start | bytes 786440 | tf_op jit(solution)/shard_map/ppermute | solution.py:337
  97.2 2.1 %collective-permute-start.9 = (f32[2,4,64,128]{3,2,1,0:T(8,128)S(1)}, f32[2,4,64,128]{3,2,1,0:T(8,128)S(1)}, u32[]{:S(2)}, u32[]{:S(2)}) collective-permute-start(f32[2,4,64,128]{3,2,1,0:T(8,128)S(1)} %get-tuple-element.31), channel_id=1, source_target_pairs={{0,64},{64,0},{128,192},{192,128},{1,65},{65,1},{129,193},{193,129... | collective-permute-start | bytes 786440 | tf_op jit(solution)/shard_map/ppermute | solution.py:333

commit v2 on v1

v2 whole, which is shorter than its diff:
```python
import functools

import jax
import jax.numpy as jnp
from jax import lax
from jax.experimental import pallas as pl
from jax.experimental.pallas import tpu as pltpu
from jax.sharding import PartitionSpec as P

TIME_STEP_SQ = 0.15
BETA_ONE = 0.9
BETA_TWO = 0.999
LEARN_RATE = 0.05
ADAM_EPS = 1e-08
ADAM_TICKS = 10.0

NZ = 16
ROWS = 8
XT = 8
LANES = 128
STEPS = 4
REACH = STEPS + 1
EDGE = STEPS
CONE = STEPS - 1
OFF = ROWS
EXT = ROWS + 2 * OFF
FIELD = (EXT, NZ, XT, LANES)
SURF_ROWS = ROWS + 2 * EDGE
TILE_A = (3 * REACH - 1) * NZ + CONE * (3 * REACH - 1) + 2
TILE_B = (2 * REACH - 1) * NZ
HALF = 0.5 * TIME_STEP_SQ

f32 = jnp.float32
VMEM = pl.BlockSpec(memory_space=pltpu.VMEM)
SMEM = pl.BlockSpec(memory_space=pltpu.SMEM)


def native(block):
    planes = block.shape[0]
    return block.reshape(planes, ROWS, XT, LANES).transpose(0, 2, 1, 3).reshape(planes, XT * ROWS, LANES)


def from_native(block):
    planes = block.shape[0]
    return block.reshape(planes, XT, ROWS, LANES).transpose(0, 2, 1, 3).reshape(planes, ROWS, XT * LANES)


def row_of(ref, z, y):
    return ref[z, pl.ds(y, XT, stride=ROWS), :]


def x_next(f, lane):
    r = pltpu.roll(f, LANES - 1, 1)
    return jnp.where(lane == LANES - 1, pltpu.roll(r, XT - 1, 0), r)


def x_prev(f, lane):
    r = pltpu.roll(f, 1, 1)
    return jnp.where(lane == 0, pltpu.roll(r, 1, 0), r)


def iotas():
    lane = lax.broadcasted_iota(jnp.int32, (XT, LANES), 1)
    tile = lax.broadcasted_iota(jnp.int32, (XT, LANES), 0)
    return lane, tile


def in_blocks(lo, hi, size, rows):
    whole = (hi - lo) // size
    if whole:
        lax.fori_loop(0, whole, lambda i, c: (rows(lo + i * size, size), c)[1], 0)
    if (hi - lo) % size:
        rows(lo + whole * size, (hi - lo) % size)


def pack_fields(fields, widths, low, high, at):
    def plane(z, carry):
        first = at
        for ref, width in zip(fields, widths, strict=True):
            for k in range(width):
                low[first + k * NZ + z] = row_of(ref, z, k)
                high[first + k * NZ + z] = row_of(ref, z, ROWS - width + k)
            first += width * NZ
        return carry

    lax.fori_loop(0, NZ, plane, 0)
    return at + sum(widths) * NZ


def pack_first_kernel(s, u1, u0, receivers, observed, low, high):
    widths = (REACH, REACH, REACH - 1)
    at = pack_fields((s, u1, u0), widths, low, high, 0)
    for ref, width in zip((s, u1, u0), widths, strict=True):
        for k in range(CONE):
            for z in range(width):
                low[at + z] = row_of(ref, z, width + k)
                high[at + z] = row_of(ref, z, ROWS - width - CONE + k)
            at += width
    where = receivers[...].astype(f32)
    empty = jnp.zeros((2, LANES), f32)
    for side, rows in ((low, lambda n: slice(0, n)), (high, lambda n: slice(ROWS - n, ROWS))):
        parts = [where[rows(EDGE)]]
        for k in range(STEPS - 1, -1, -1):
            parts.append(observed[k][rows(k + 1)])
        parts.append(empty)
        both = jnp.concatenate(parts, 0)
        side[at] = both[:XT]
        side[at + 1] = both[XT:]


def pack_first(s, u1, u0, receivers, observed):
    shape = jax.ShapeDtypeStruct((TILE_A, XT, LANES), f32)
    return pl.pallas_call(
        pack_first_kernel,
        out_shape=(shape, shape),
        in_specs=[VMEM] * 5,
        out_specs=(VMEM, VMEM),
        cost_estimate=pl.CostEstimate(flops=0, bytes_accessed=1 << 21, transcendentals=0),
        name="pack_first",
    )(s, u1, u0, receivers, observed)


def pack_second_kernel(l6, l7, low, high):
    pack_fields((l6, l7), (REACH, REACH - 1), low, high, 0)


def pack_second(l6, l7):
    shape = jax.ShapeDtypeStruct((TILE_B, XT, LANES), f32)
    return pl.pallas_call(
        pack_second_kernel,
        out_shape=(shape, shape),
        in_specs=[VMEM] * 2,
        out_specs=(VMEM, VMEM),
        cost_estimate=pl.CostEstimate(flops=0, bytes_accessed=1 << 21, transcendentals=0),
        name="pack_second",
    )(l6, l7)


def fill(ext, own, low, high, at, width):
    def plane(z, carry):
        for k in range(ROWS):
            ext[OFF + k, z] = row_of(own, z, k)
        return carry

    lax.fori_loop(0, NZ, plane, 0)
    for k in range(width):
        ext[OFF - width + k] = low[at + k * NZ : at + (k + 1) * NZ]
        ext[OFF + ROWS + k] = high[at + k * NZ : at + (k + 1) * NZ]


def fill_cone(ext, low, high, at, width):
    for k in range(CONE):
        ext[OFF - width - CONE + k, :width] = low[at + k * width : at + (k + 1) * width]
        ext[OFF + ROWS + width + k, :width] = high[at + k * width : at + (k + 1) * width]


def coefficients(stiff, diag, cx, cy, cz, lo, hi, planes, lane, tile):
    x_end = (lane == LANES - 1) & (tile == XT - 1)
    x_start = (lane == 0) & (tile == 0)

    def faces(first, count):
        for e in (first + r for r in range(count)):
            for z in range(planes):
                cy[e, z] = HALF * (stiff[e, z] + stiff[e + 1, z])

    def rows(first, count):
        for e in (first + r for r in range(count)):
            below = None
            following = HALF * stiff[e, 0]
            for z in range(planes):
                s = following
                face = s + jnp.where(x_end, 0.0, x_next(s, lane))
                total = face + (s + jnp.where(x_start, 0.0, x_prev(s, lane)))
                if z < NZ - 1:
                    following = HALF * stiff[e, z + 1]
                    above = s + following
                else:
                    above = s
                total = total + above + (below if z > 0 else s) + cy[e, z] + cy[e - 1, z]
                cx[e, z] = jnp.where(x_end, 0.0, face)
                cz[e, z] = above
                diag[e, z] = 2.0 - total
                below = above

    in_blocks(lo - 1, hi, 4, faces)
    in_blocks(lo, hi, 4, rows)


def leap(now, before, after, diag, cx, cy, cz, lo, hi, planes, lane):
    def rows(first, count):
        for e in (first + r for r in range(count)):
            for z in range(planes):
                u = now[e, z]
                c = cx[e, z]
                acc = diag[e, z] * u - before[e, z]
                acc = acc + c * x_next(u, lane) + x_prev(c * u, lane)
                acc = acc + cy[e, z] * now[e + 1, z] + cy[e - 1, z] * now[e - 1, z]
                if z < NZ - 1:
                    acc = acc + cz[e, z] * now[e, z + 1]
                if z > 0:
                    acc = acc + cz[e, z - 1] * now[e, z - 1]
                after[e, z] = acc

    in_blocks(lo, hi, 4, rows)


def forward_kernel(
    place, source_pos, source_wave, u0, u1, s, low, high, receivers, observed,
    w1, w2, w3, w4, w5, diag, cx, cy, cz, surf,
    stiff, before,
):
    lane, tile = iotas()
    waves = (w1, w2, w3, w4, w5)
    at = 0
    for ext, own, width in ((stiff, s, REACH), (w1, u1, REACH), (before, u0, REACH - 1)):
        fill(ext, own, low, high, at, width)
        at += width * NZ
    for ext, width in ((stiff, REACH), (w1, REACH), (before, REACH - 1)):
        fill_cone(ext, low, high, at, width)
        at += width * CONE
    top, bottom = OFF - REACH, OFF + ROWS + REACH
    for lo, hi, planes in (
        (top + 1, bottom - 1, NZ),
        (top + 1 - CONE, top + 1, STEPS),
        (bottom - 1, bottom - 1 + CONE, STEPS),
    ):
        coefficients(stiff, diag, cx, cy, cz, lo, hi, planes, lane, tile)

    @pl.when(place[1] == 1)
    def _():
        cy[OFF - 1] = jnp.zeros((NZ, XT, LANES), f32)

    @pl.when(place[2] == 1)
    def _():
        cy[OFF + ROWS - 1] = jnp.zeros((NZ, XT, LANES), f32)

    z_src = source_pos[0, 0]
    e_src = source_pos[0, 1] - place[0] + OFF
    x_src = source_pos[0, 2]
    spot = (tile * LANES + lane) == x_src
    for k in range(STEPS):
        older = before if k == 0 else waves[k - 1]
        after = waves[k + 1]
        lo, hi = top + 1 + k, bottom - 1 - k
        leap(waves[k], older, after, diag, cx, cy, cz, lo, hi, NZ, lane)
        leap(waves[k], older, after, diag, cx, cy, cz, lo - CONE, lo, STEPS - k, lane)
        leap(waves[k], older, after, diag, cx, cy, cz, hi, hi + CONE, STEPS - k, lane)

        @pl.when((e_src >= lo - CONE) & (e_src < hi + CONE))
        def _():
            add = jnp.where(spot, TIME_STEP_SQ * source_wave[0, k], 0.0)
            after[e_src, z_src] = after[e_src, z_src] + add

    column = lax.broadcasted_iota(jnp.int32, (LANES, LANES), 0)
    sides = []
    for ref in (low, high):
        rows = jnp.concatenate([ref[TILE_A - 2], ref[TILE_A - 1]], 0)
        sides.append((rows[:EDGE].astype(jnp.int32), rows[EDGE:]))
    for j in range(SURF_ROWS):
        y = j - EDGE
        if y < 0:
            used = range(-y - 1, STEPS)
            at = sides[0][0][j : j + 1]
        elif y < ROWS:
            used = range(STEPS)
            at = receivers[y : y + 1, :]
        else:
            used = range(y - ROWS, STEPS)
            at = sides[1][0][y - ROWS : y - ROWS + 1]
        pick = jnp.where(column == (at & (LANES - 1)), 1.0, 0.0)
        held = jnp.where(tile == (at >> 7), 1.0, 0.0)
        surface = jnp.concatenate([waves[k + 1][OFF + y, 0] for k in used], 0)
        lanes_of = jnp.dot(surface, pick, precision=lax.Precision.HIGHEST, preferred_element_type=f32)
        parts = []
        for i, k in enumerate(used):
            record = jnp.sum(lanes_of[i * XT : (i + 1) * XT] * held, axis=0, keepdims=True)
            if 0 <= y < ROWS:
                trace = observed[k, y : y + 1, :]
            else:
                skip = sum(m + 1 for m in range(k + 1, STEPS))
                r = skip + (y + k + 1 if y < 0 else y - ROWS)
                trace = sides[0 if y < 0 else 1][1][r : r + 1]
            parts.append(held * (record - trace))
        back = lax.dot_general(
            jnp.concatenate(parts, 0), pick, (((1,), (1,)), ((), ())),
            precision=lax.Precision.HIGHEST, preferred_element_type=f32,
        )
        for i, k in enumerate(used):
            surf[k, j] = back[i * XT : (i + 1) * XT]


def forward(place, source_pos, source_wave, u0, u1, s, low, high, receivers, observed):
    one = jax.ShapeDtypeStruct(FIELD, f32)
    return pl.pallas_call(
        forward_kernel,
        out_shape=(one,) * (STEPS + 5) + (jax.ShapeDtypeStruct((STEPS, SURF_ROWS, XT, LANES), f32),),
        in_specs=[SMEM] * 3 + [VMEM] * 7,
        out_specs=(VMEM,) * (STEPS + 6),
        scratch_shapes=[pltpu.VMEM(FIELD, f32)] * 2,
        compiler_params=pltpu.CompilerParams(vmem_limit_bytes=26 << 20),
        cost_estimate=pl.CostEstimate(flops=1 << 25, bytes_accessed=1 << 24, transcendentals=0),
        name="forward",
    )(place, source_pos, source_wave, u0, u1, s, low, high, receivers, observed)


def adjoint_kernel(
    place, l6, l7, low, high, w1, w2, w3, w4, w5, diag, cx, cy, cz, surf,
    keep, send,
    m6, m5, m4, m3, m2, before, face_y, grad,
):
    lane, tile = iotas()
    x_end = (lane == LANES - 1) & (tile == XT - 1)
    x_side = x_end | ((lane == 0) & (tile == 0))
    lams = (m6, m5, m4, m3, m2)
    fill(m6, l6, low, high, 0, REACH)
    fill(before, l7, low, high, REACH * NZ, REACH - 1)
    for k in range(STEPS):
        older = before if k == 0 else lams[k - 1]
        after = lams[k + 1]
        lo, hi = OFF - REACH + 1 + k, OFF + ROWS + REACH - 1 - k
        leap(lams[k], older, after, diag, cx, cy, cz, lo, hi, NZ, lane)
        for e in range(lo, hi):
            after[e, 0] = after[e, 0] + surf[STEPS - 1 - k, e - OFF + EDGE]

    pairs = tuple(zip((w5, w4, w3, w2, w1), lams, strict=True))
    for z in range(NZ):
        total = None
        for w, m in pairs:
            part = (w[OFF, z] - w[OFF - 1, z]) * (m[OFF, z] - m[OFF - 1, z])
            total = part if total is None else total + part
        face_y[z] = total

    def row(y, carry):
        e = y + OFF
        below = None
        us = [w[e, 0] for w, _ in pairs]
        ls = [m[e, 0] for _, m in pairs]
        for z in range(NZ):
            fx = fy = fz = cell = None
            next_us, next_ls = [], []
            for (w, m), u, l in zip(pairs, us, ls, strict=True):
                px = (x_next(u, lane) - u) * (x_next(l, lane) - l)
                py = (w[e + 1, z] - u) * (m[e + 1, z] - l)
                both = u * l
                if z < NZ - 1:
                    un, ln = w[e, z + 1], m[e, z + 1]
                    next_us.append(un)
                    next_ls.append(ln)
                    pz = (un - u) * (ln - l)
                else:
                    pz = both
                fx = px if fx is None else fx + px
                fy = py if fy is None else fy + py
                fz = pz if fz is None else fz + pz
                cell = both if cell is None else cell + both
            us, ls = next_us, next_ls
            fx = jnp.where(x_end, 0.0, fx)
            total = fx + x_prev(fx, lane) + jnp.where(x_side, cell, 0.0)
            total = total + fy + face_y[z] + fz + (cell if z == 0 else below)
            face_y[z] = fy
            below = fz
            grad[z, pl.ds(y, XT, stride=ROWS), :] = -HALF * total
        return carry

    lax.fori_loop(0, ROWS, row, 0)
    core = place[3]
    for group in range(2):
        keep[group] = grad[pl.ds(8 * group + 4 * core, 4)]
        send[group] = grad[pl.ds(8 * group + 4 * (1 - core), 4)]


def adjoint(place, l6, l7, low, high, *rest):
    part = jax.ShapeDtypeStruct((2, 4, XT * ROWS, LANES), f32)
    return pl.pallas_call(
        adjoint_kernel,
        out_shape=(part, part),
        in_specs=[SMEM] + [VMEM] * (4 + len(rest)),
        out_specs=(VMEM, VMEM),
        scratch_shapes=[pltpu.VMEM(FIELD, f32)] * (STEPS + 2)
        + [
            pltpu.VMEM((NZ, XT, LANES), f32),
            pltpu.VMEM((NZ, XT * ROWS, LANES), f32),
        ],
        compiler_params=pltpu.CompilerParams(vmem_limit_bytes=30 << 20),
        cost_estimate=pl.CostEstimate(flops=1 << 25, bytes_accessed=1 << 24, transcendentals=0),
        name="adjoint",
    )(place, l6, l7, low, high, *rest)


def to_next(block):
    count = lax.axis_size("gy")
    return lax.ppermute(block, "gy", [(i, i + 1) for i in range(count - 1)])


def to_prev(block):
    count = lax.axis_size("gy")
    return lax.ppermute(block, "gy", [(i + 1, i) for i in range(count - 1)])


def swap_core(block):
    return lax.ppermute(block, "shot", [(0, 1), (1, 0), (2, 3), (3, 2)])


def swap_far(block):
    return lax.ppermute(block, "shot", [(0, 2), (2, 0), (1, 3), (3, 1)])


def body(
    stiffness,
    first_moment,
    second_moment,
    wave_prev,
    wave_now,
    adjoint_next,
    adjoint_now,
    observed,
    receiver_x,
    source_pos,
    source_wave,
):
    gy = lax.axis_index("gy")
    shot = lax.axis_index("shot")
    core, far = shot % 2, shot // 2
    place = jnp.stack([gy * ROWS, gy == 0, gy == lax.axis_size("gy") - 1, core]).astype(jnp.int32)
    s = native(stiffness)
    u0, u1 = native(wave_prev[0]), native(wave_now[0])
    l6, l7 = native(adjoint_now[0]), native(adjoint_next[0])
    first, second = native(first_moment), native(second_moment)

    a_low, a_high = pack_first(s, u1, u0, receiver_x[0], observed[0])
    a_high, a_low = to_next(a_high), to_prev(a_low)
    b_low, b_high = pack_second(l6, l7)
    b_high, b_low = to_next(b_high), to_prev(b_low)
    moments = swap_far(jnp.stack([first, second]))
    a_high, a_low, moments = lax.optimization_barrier((a_high, a_low, moments))

    fields = forward(
        place, source_pos, source_wave, u0, u1, s, a_high, a_low, receiver_x[0], observed[0]
    )
    keep, send = adjoint(place, l6, l7, b_high, b_low, *fields)
    chip_sum = keep + swap_core(send)
    share = chip_sum + swap_far(chip_sum)

    is_far = (jnp.arange(2) == far)[:, None, None, None]
    first_two = jnp.where(is_far, first[None], moments[0][None])
    second_two = jnp.where(is_far, second[None], moments[1][None])
    stiff_two = jnp.where(core == 0, s.reshape(2, 2, 4, XT * ROWS, LANES)[:, 0], s.reshape(2, 2, 4, XT * ROWS, LANES)[:, 1])
    first_new = BETA_ONE * first_two + (1.0 - BETA_ONE) * share
    second_new = BETA_TWO * second_two + (1.0 - BETA_TWO) * share * share
    updated = stiff_two - LEARN_RATE * (first_new / (1.0 - BETA_ONE**ADAM_TICKS)) / (
        jnp.sqrt(second_new / (1.0 - BETA_TWO**ADAM_TICKS)) + ADAM_EPS
    )
    other = swap_core(updated)
    even = jnp.where(core == 0, updated, other)
    odd = jnp.where(core == 0, other, updated)
    stiffness_new = jnp.stack([even, odd], 1).reshape(NZ, XT * ROWS, LANES)
    first_out = jnp.where(far == 0, first_new[0], first_new[1])
    second_out = jnp.where(far == 0, second_new[0], second_new[1])
    return (from_native(stiffness_new), from_native(first_out), from_native(second_out))


def solution(mesh):
    return jax.shard_map(
        body,
        mesh=mesh,
        in_specs=(
            P(None, "gy", None),
            P("shot", "gy", None),
            P("shot", "gy", None),
            P("shot", None, "gy", None),
            P("shot", None, "gy", None),
            P("shot", None, "gy", None),
            P("shot", None, "gy", None),
            P("shot", None, "gy", None),
            P("shot", "gy", None),
            P("shot", None),
            P("shot", None),
        ),
        out_specs=(P(None, "gy", None), P("shot", "gy", None), P("shot", "gy", None)),
        check_vma=False,
    )
```

time: 100 us -> 96.4 us (0.964)
  the two profiles are of different devices: /device:TPU:127 before, /device:TPU:97 now
where the time goes in v2:
time: 96.4 us; the launch traced here: 96.1 us
  waiting for transfers between devices  44.8 us (46%)
  Pallas kernels  25.1 us (26%)
  starting transfers between devices  21.5 us (22%)
  other arithmetic  1.91 us (2%)
  local copies, waits for them, and re-layouts  1.87 us (2%)
    ppermute x2, waiting for transfers between devices, swap_far(): return lax.ppermute(block, 'shot', [(0, 2), (2, 0), (1, 3), (3, 1)])  43.2 us
    ppermute x2, starting transfers between devices, to_prev(): return lax.ppermute(block, 'gy', [(i + 1, i) for i in range(count - 1)])  11.5 us
    pallas_call x1, Pallas kernels, forward(): pl.pallas_call(forward_kernel, out_shape=(one,) * (STEPS + 5) + (jax.Shap...  10.2 us
    pallas_call x1, Pallas kernels, adjoint(): pl.pallas_call(adjoint_kernel, out_shape=(part, part), in_specs=[SMEM] +...  9.13 us
    ppermute x2, starting transfers between devices, to_next(): return lax.ppermute(block, 'gy', [(i, i + 1) for i in range(count - 1)])  5.1 us
    pallas_call x1, Pallas kernels, pack_first(): pl.pallas_call(pack_first_kernel, out_shape=(shape, shape), in_specs=[VME...  3.28 us
    ppermute x2, starting transfers between devices, swap_far(): return lax.ppermute(block, 'shot', [(0, 2), (2, 0), (1, 3), (3, 1)])  3.06 us
    pallas_call x1, Pallas kernels, pack_second(): pl.pallas_call(pack_second_kernel, out_shape=(shape, shape), in_specs=[VM...  2.46 us
  transfers between devices with their start and end apart: 8, of which 4 were waited for; matrix products, arithmetic and copies ran while one was open for 3% of the time, Pallas kernels for 13%

profile of v2, /device:TPU:97, one launch (start us, length us, event | category | flops | bytes accessed | tf_op | source)
XLA Modules:
  0.0 96.1 jit_solution(6246333593395081496)
XLA Ops:
  0.7 3.3 %pack_first.1 = (f32[268,8,128]{2,1,0:T(8,128)}, f32[268,8,128]{2,1,0:T(8,128)}) custom-call(f32[16,64,128]{2,1,0:T(8,128)} %bitcast.88, f32[16,64,128]{2,1,0:T(8,128)} %bitcast.97, f32[16,64,128]{2,1,0:T(8,128)} %bitcast.95, s32[8,128]{1,0:T(8,128)} %bitcast.101, f32[4,8,128]{2,1,0:T(8,128)} %bitcast.99), custom_call_target="tpu_custom_call" | custom-call | bytes 2097152 | tf_op jit(solution)/shard_map/pack_first/pallas_call | solution.py:113
  4.0 3.2 %collective-permute-start = (f32[268,8,128]{2,1,0:T(8,128)}, f32[268,8,128]{2,1,0:T(8,128)S(1)}, u32[]{:S(2)}, u32[]{:S(2)}) collective-permute-start(f32[268,8,128]{2,1,0:T(8,128)} %get-tuple-element.22), channel_id=1, source_target_pairs={{0,1},{1,2},{2,3},{3,4},{4,5},{5,6},{6,7},{7,8},{8,9},{9,10},{10,1... | collective-permute-start | bytes 3293192 | tf_op jit(solution)/shard_map/ppermute | solution.py:392
  7.2 5.1 %collective-permute-start.1 = (f32[268,8,128]{2,1,0:T(8,128)}, f32[268,8,128]{2,1,0:T(8,128)}, u32[]{:S(2)}, u32[]{:S(2)}) collective-permute-start(f32[268,8,128]{2,1,0:T(8,128)} %get-tuple-element.23), channel_id=1, source_target_pairs={{1,0},{2,1},{3,2},{4,3},{5,4},{6,5},{7,6},{8,7},{9,8},{10,9},{11,1... | collective-permute-start | bytes 3293192 | tf_op jit(solution)/shard_map/ppermute | solution.py:397
  12.3 2.5 %pack_second.1 = (f32[144,8,128]{2,1,0:T(8,128)}, f32[144,8,128]{2,1,0:T(8,128)}) custom-call(f32[16,64,128]{2,1,0:T(8,128)} %bitcast.91, f32[16,64,128]{2,1,0:T(8,128)} %bitcast.93), custom_call_target="tpu_custom_call" | custom-call | bytes 2097152 | tf_op jit(solution)/shard_map/pack_second/pallas_call | solution.py:129
  14.8 1.9 %collective-permute-start.3 = (f32[144,8,128]{2,1,0:T(8,128)}, f32[144,8,128]{2,1,0:T(8,128)S(1)}, u32[]{:S(2)}, u32[]{:S(2)}) collective-permute-start(f32[144,8,128]{2,1,0:T(8,128)} %get-tuple-element.25), channel_id=1, source_target_pairs={{0,1},{1,2},{2,3},{3,4},{4,5},{5,6},{6,7},{7,8},{8,9},{9,10},{10,1... | collective-permute-start | bytes 1769480 | tf_op jit(solution)/shard_map/ppermute | solution.py:392
  16.7 6.4 %collective-permute-start.4 = (f32[144,8,128]{2,1,0:T(8,128)}, f32[144,8,128]{2,1,0:T(8,128)}, u32[]{:S(2)}, u32[]{:S(2)}) collective-permute-start(f32[144,8,128]{2,1,0:T(8,128)} %get-tuple-element.26), channel_id=1, source_target_pairs={{1,0},{2,1},{3,2},{4,3},{5,4},{6,5},{7,6},{8,7},{9,8},{10,9},{11,1... | collective-permute-start | bytes 1769480 | tf_op jit(solution)/shard_map/ppermute | solution.py:397
  23.1 0.7 pad_maximum_fusion.1
  23.8 2.7 %collective-permute-start.2 = (f32[2,4,64,128]{3,2,1,0:T(8,128)}, f32[2,4,64,128]{3,2,1,0:T(8,128)}, u32[]{:S(2)}, u32[]{:S(2)}) collective-permute-start(f32[2,4,64,128]{3,2,1,0:T(8,128)} %pad_maximum_fusion.1), channel_id=1, source_target_pairs={{0,128},{128,0},{64,192},{192,64},{1,129},{129,1},{65,193},{193,65... | collective-permute-start | bytes 786440 | tf_op jit(solution)/shard_map/ppermute | solution.py:405
  26.5 0.1 pad_add_fusion.place
  26.6 35.4 %collective-permute-done.2 = f32[2,4,64,128]{3,2,1,0:T(8,128)} collective-permute-done((f32[2,4,64,128]{3,2,1,0:T(8,128)}, f32[2,4,64,128]{3,2,1,0:T(8,128)}, u32[]{:S(2)}, u32[]{:S(2)}) %collective-permute-start.2) | collective-permute-done | bytes 262176 | tf_op jit(solution)/shard_map/ppermute | solution.py:405
  62.1 10.2 %forward.1 = (f32[24,16,8,128]{3,2,1,0:T(8,128)S(1)}, f32[24,16,8,128]{3,2,1,0:T(8,128)S(1)}, f32[24,16,8,128]{3,2,1,0:T(8,128)S(1)}, f32[24,16,8,128]{3,2,1,0:T...) custom-call(s32[4]{0:T(128)S(1)} %pad_add_fusion.place, ...), custom_call_target="tpu_custom_call" | custom-call | flops 33554432 | bytes 16777216 | tf_op jit(solution)/shard_map/forward/pallas_call | solution.py:294
  72.3 0.0 collective-permute-done.3.low
  72.3 0.0 collective-permute-done.4.high
  72.4 9.1 %adjoint.1 = (f32[2,4,64,128]{3,2,1,0:T(8,128)S(1)}, f32[2,4,64,128]{3,2,1,0:T(8,128)S(1)}) custom-call(s32[4]{0:T(128)S(1)} %pad_add_fusion.place, f32[16,64,128]{2,1,0:T(8,128)S(1)} %bitcast.92, f32[16,64,128]{2,1,0:T(8,128)S(1)} %bitcast.94, f32[144,8,128]{2,1,0:T(8,128)S(1)} %collective-permute-done.3.low, f32[144,8,128]{2,1,0:T(8,128)} %collective-permute-done.4.high, ...), custom_call_target="tpu_custom_call" | custom-call | flops 33554432 | bytes 16777216 | tf_op jit(solution)/shard_map/adjoint/pallas_call | solution.py:374
  81.5 0.6 collective-permute-start.5
  82.1 1.2 %collective-permute-done.5 = f32[2,4,64,128]{3,2,1,0:T(8,128)S(1)} collective-permute-done((f32[2,4,64,128]{3,2,1,0:T(8,128)S(1)}, f32[2,4,64,128]{3,2,1,0:T(8,128)S(1)}, u32[]{:S(2)}, u32[]{:S(2)}) %collective-permute-start.5) | collective-permute-done | bytes 262176 | tf_op jit(solution)/shard_map/ppermute | solution.py:401
  83.3 0.3 collective-permute-start.6
  83.6 1.0 %slice_bitcast_fusion.2 = (f32[4,64,128]{2,1,0:T(8,128)S(1)}, f32[4,64,128]{2,1,0:T(8,128)S(1)}) fusion(f32[2,4,64,128]{3,2,1,0:T(8,128)} %collective-permute-done.2), kind=kLoop, calls=%fused_computation.16 | loop fusion | bytes 524288 | tf_op jit(solution)/shard_map/jit(_where)/broadcast_in_dim | solution.py:446
  84.6 7.8 %collective-permute-done.6 = f32[2,4,64,128]{3,2,1,0:T(8,128)S(1)} collective-permute-done((f32[2,4,64,128]{3,2,1,0:T(8,128)S(1)}, f32[2,4,64,128]{3,2,1,0:T(8,128)S(1)}, u32[]{:S(2)}, u32[]{:S(2)}) %collective-permute-start.6) | collective-permute-done | bytes 262176 | tf_op jit(solution)/shard_map/ppermute | solution.py:405
  92.4 0.3 fusion.3
  92.7 1.3 %collective-permute-start.7 = (f32[2,4,64,128]{3,2,1,0:T(8,128)S(1)}, f32[2,4,64,128]{3,2,1,0:T(8,128)S(1)}, u32[]{:S(2)}, u32[]{:S(2)}) collective-permute-start(f32[2,4,64,128]{3,2,1,0:T(8,128)S(1)} %get-tuple-element.41), channel_id=1, source_target_pairs={{0,64},{64,0},{128,192},{192,128},{1,65},{65,1},{129,193},{193,129... | collective-permute-start | bytes 786440 | tf_op jit(solution)/shard_map/ppermute | solution.py:401
  94.0 0.7 fusion.4
  94.7 0.4 collective-permute-done.7
  95.2 0.8 copy.16
  (28 shorter events, 0.2 us)
Async XLA Ops:
  0.6 22.4 %copy-start.10 = (f32[4,8,1024]{2,1,0:T(8,128)S(1)}, f32[4,8,1024]{2,1,0:T(8,128)}, u32[]{:S(2)}) copy-start(f32[4,8,1024]{2,1,0:T(8,128)} %param.12) | copy-start | bytes 393220
  0.6 22.4 %copy-start.9 = (f32[4,8,1024]{2,1,0:T(8,128)S(1)}, f32[4,8,1024]{2,1,0:T(8,128)}, u32[]{:S(2)}) copy-start(f32[4,8,1024]{2,1,0:T(8,128)} %param.13) | copy-start | bytes 393220
  0.7 61.4 %copy-start = (f32[16,8,1024]{2,1,0:T(8,128)S(1)}, f32[16,8,1024]{2,1,0:T(8,128)}, u32[]{:S(2)}) copy-start(f32[16,8,1024]{2,1,0:T(8,128)} %param.11) | copy-start | bytes 1572868
  0.7 61.4 %copy-start.3 = (f32[1,16,8,1024]{3,2,1,0:T(8,128)S(1)}, f32[1,16,8,1024]{3,2,1,0:T(8,128)}, u32[]{:S(2)}) copy-start(f32[1,16,8,1024]{3,2,1,0:T(8,128)} %param.14) | copy-start | bytes 1572868
  0.7 61.4 %copy-start.4 = (f32[1,16,8,1024]{3,2,1,0:T(8,128)S(1)}, f32[1,16,8,1024]{3,2,1,0:T(8,128)}, u32[]{:S(2)}) copy-start(f32[1,16,8,1024]{3,2,1,0:T(8,128)} %param.15) | copy-start | bytes 1572868
  0.7 61.4 %copy-start.5 = (f32[1,4,8,128]{3,2,1,0:T(8,128)S(1)}, f32[1,4,8,128]{3,2,1,0:T(8,128)}, u32[]{:S(2)}) copy-start(f32[1,4,8,128]{3,2,1,0:T(8,128)} %param.18) | copy-start | bytes 49156
  0.7 61.4 %copy-start.6 = (s32[1,8,128]{2,1,0:T(8,128)S(1)}, s32[1,8,128]{2,1,0:T(8,128)}, u32[]{:S(2)}) copy-start(s32[1,8,128]{2,1,0:T(8,128)} %param.19) | copy-start | bytes 12292
  0.7 61.4 %copy-start.7 = (s32[1,3]{1,0:T(1,128)S(1)}, s32[1,3]{1,0:T(1,128)}, u32[]{:S(2)}) copy-start(s32[1,3]{1,0:T(1,128)} %source_pos.1) | copy-start | bytes 40
  0.7 61.4 %copy-start.8 = (f32[1,4]{1,0:T(1,128)S(1)}, f32[1,4]{1,0:T(1,128)}, u32[]{:S(2)}) copy-start(f32[1,4]{1,0:T(1,128)} %source_wave.1) | copy-start | bytes 52
  4.0 58.0 %collective-permute-start = (f32[268,8,128]{2,1,0:T(8,128)}, f32[268,8,128]{2,1,0:T(8,128)S(1)}, u32[]{:S(2)}, u32[]{:S(2)}) collective-permute-start(f32[268,8,128]{2,1,0:T(8,128)} %get-tuple-element.22), channel_id=1, source_target_pairs={{0,1},{1,2},{2,3},{3,4},{4,5},{5,6},{6,7},{7,8},{8,9},{9,10},{10,1... | collective-permute-start | bytes 3293192 | tf_op jit(solution)/shard_map/ppermute | solution.py:392
  7.2 54.8 %collective-permute-start.1 = (f32[268,8,128]{2,1,0:T(8,128)}, f32[268,8,128]{2,1,0:T(8,128)}, u32[]{:S(2)}, u32[]{:S(2)}) collective-permute-start(f32[268,8,128]{2,1,0:T(8,128)} %get-tuple-element.23), channel_id=1, source_target_pairs={{1,0},{2,1},{3,2},{4,3},{5,4},{6,5},{7,6},{8,7},{9,8},{10,9},{11,1... | collective-permute-start | bytes 3293192 | tf_op jit(solution)/shard_map/ppermute | solution.py:397
  14.8 57.6 %collective-permute-start.3 = (f32[144,8,128]{2,1,0:T(8,128)}, f32[144,8,128]{2,1,0:T(8,128)S(1)}, u32[]{:S(2)}, u32[]{:S(2)}) collective-permute-start(f32[144,8,128]{2,1,0:T(8,128)} %get-tuple-element.25), channel_id=1, source_target_pairs={{0,1},{1,2},{2,3},{3,4},{4,5},{5,6},{6,7},{7,8},{8,9},{9,10},{10,1... | collective-permute-start | bytes 1769480 | tf_op jit(solution)/shard_map/ppermute | solution.py:392
  16.7 55.7 %collective-permute-start.4 = (f32[144,8,128]{2,1,0:T(8,128)}, f32[144,8,128]{2,1,0:T(8,128)}, u32[]{:S(2)}, u32[]{:S(2)}) collective-permute-start(f32[144,8,128]{2,1,0:T(8,128)} %get-tuple-element.26), channel_id=1, source_target_pairs={{1,0},{2,1},{3,2},{4,3},{5,4},{6,5},{7,6},{8,7},{9,8},{10,9},{11,1... | collective-permute-start | bytes 1769480 | tf_op jit(solution)/shard_map/ppermute | solution.py:397
  23.8 38.2 %collective-permute-start.2 = (f32[2,4,64,128]{3,2,1,0:T(8,128)}, f32[2,4,64,128]{3,2,1,0:T(8,128)}, u32[]{:S(2)}, u32[]{:S(2)}) collective-permute-start(f32[2,4,64,128]{3,2,1,0:T(8,128)} %pad_maximum_fusion.1), channel_id=1, source_target_pairs={{0,128},{128,0},{64,192},{192,64},{1,129},{129,1},{65,193},{193,65... | collective-permute-start | bytes 786440 | tf_op jit(solution)/shard_map/ppermute | solution.py:405
  26.6 45.8 %copy-start.1 = (f32[1,16,8,1024]{3,2,1,0:T(8,128)S(1)}, f32[1,16,8,1024]{3,2,1,0:T(8,128)}, u32[]{:S(2)}) copy-start(f32[1,16,8,1024]{3,2,1,0:T(8,128)} %param.17) | copy-start | bytes 1572868
  26.6 45.8 %copy-start.2 = (f32[1,16,8,1024]{3,2,1,0:T(8,128)S(1)}, f32[1,16,8,1024]{3,2,1,0:T(8,128)}, u32[]{:S(2)}) copy-start(f32[1,16,8,1024]{3,2,1,0:T(8,128)} %param.16) | copy-start | bytes 1572868
  81.5 1.7 %collective-permute-start.5 = (f32[2,4,64,128]{3,2,1,0:T(8,128)S(1)}, f32[2,4,64,128]{3,2,1,0:T(8,128)S(1)}, u32[]{:S(2)}, u32[]{:S(2)}) collective-permute-start(f32[2,4,64,128]{3,2,1,0:T(8,128)S(1)} %get-tuple-element.40), channel_id=1, source_target_pairs={{0,64},{64,0},{128,192},{192,128},{1,65},{65,1},{129,193},{193,129... | collective-permute-start | bytes 786440 | tf_op jit(solution)/shard_map/ppermute | solution.py:401
  83.3 9.1 %collective-permute-start.6 = (f32[2,4,64,128]{3,2,1,0:T(8,128)S(1)}, f32[2,4,64,128]{3,2,1,0:T(8,128)S(1)}, u32[]{:S(2)}, u32[]{:S(2)}) collective-permute-start(f32[2,4,64,128]{3,2,1,0:T(8,128)S(1)} %add.24), channel_id=1, source_target_pairs={{0,128},{128,0},{64,192},{192,64},{1,129},{129,1},{65,193},{193,65... | collective-permute-start | bytes 786440 | tf_op jit(solution)/shard_map/ppermute | solution.py:405
  92.7 2.5 %collective-permute-start.7 = (f32[2,4,64,128]{3,2,1,0:T(8,128)S(1)}, f32[2,4,64,128]{3,2,1,0:T(8,128)S(1)}, u32[]{:S(2)}, u32[]{:S(2)}) collective-permute-start(f32[2,4,64,128]{3,2,1,0:T(8,128)S(1)} %get-tuple-element.41), channel_id=1, source_target_pairs={{0,64},{64,0},{128,192},{192,128},{1,65},{65,1},{129,193},{193,129... | collective-permute-start | bytes 786440 | tf_op jit(solution)/shard_map/ppermute | solution.py:401

commit v3 on v2

v3 whole, which is shorter than its diff:
```python
import functools

import jax
import jax.numpy as jnp
from jax import lax
from jax.experimental import pallas as pl
from jax.experimental.pallas import tpu as pltpu
from jax.sharding import PartitionSpec as P

TIME_STEP_SQ = 0.15
BETA_ONE = 0.9
BETA_TWO = 0.999
LEARN_RATE = 0.05
ADAM_EPS = 1e-08
ADAM_TICKS = 10.0

NZ = 16
ROWS = 8
XT = 8
LANES = 128
STEPS = 4
REACH = STEPS + 1
EDGE = STEPS
CONE = STEPS - 1
OFF = ROWS
EXT = ROWS + 2 * OFF
FIELD = (EXT, NZ, XT, LANES)
SHORT = (ROWS + 2 * REACH, NZ, XT, LANES)
SURF_ROWS = ROWS + 2 * EDGE
PART = NZ // 2
TILE_S = REACH * PART + CONE * REACH
TILE_U = (2 * REACH - 1) * (NZ + CONE) + 2
TILE_L = (2 * REACH - 1) * NZ
HALF = 0.5 * TIME_STEP_SQ

f32 = jnp.float32
VMEM = pl.BlockSpec(memory_space=pltpu.VMEM)
SMEM = pl.BlockSpec(memory_space=pltpu.SMEM)


def native(block):
    planes = block.shape[0]
    return block.reshape(planes, ROWS, XT, LANES).transpose(0, 2, 1, 3).reshape(planes, XT * ROWS, LANES)


def from_native(block):
    planes = block.shape[0]
    return block.reshape(planes, XT, ROWS, LANES).transpose(0, 2, 1, 3).reshape(planes, ROWS, XT * LANES)


def row_of(ref, z, y):
    return ref[z, pl.ds(y, XT, stride=ROWS), :]


def x_next(f, lane):
    r = pltpu.roll(f, LANES - 1, 1)
    return jnp.where(lane == LANES - 1, pltpu.roll(r, XT - 1, 0), r)


def x_prev(f, lane):
    r = pltpu.roll(f, 1, 1)
    return jnp.where(lane == 0, pltpu.roll(r, 1, 0), r)


def iotas():
    lane = lax.broadcasted_iota(jnp.int32, (XT, LANES), 1)
    tile = lax.broadcasted_iota(jnp.int32, (XT, LANES), 0)
    return lane, tile


def in_blocks(lo, hi, size, rows):
    whole = (hi - lo) // size
    if whole:
        lax.fori_loop(0, whole, lambda i, c: (rows(lo + i * size, size), c)[1], 0)
    if (hi - lo) % size:
        rows(lo + whole * size, (hi - lo) % size)


def pack_fields(fields, widths, low, high, at):
    def plane(z, carry):
        first = at
        for ref, width in zip(fields, widths, strict=True):
            for k in range(width):
                low[first + k * NZ + z] = row_of(ref, z, k)
                high[first + k * NZ + z] = row_of(ref, z, ROWS - width + k)
            first += width * NZ
        return carry

    lax.fori_loop(0, NZ, plane, 0)
    return at + sum(widths) * NZ


def core_index():
    return lax.rem(lax.axis_index("shot"), 2)


def by_parity(pair, work):
    parity = lax.rem(lax.axis_index("gy"), 2)

    @pl.when(parity == 0)
    def _():
        work(pair[1], pair[0])

    @pl.when(parity == 1)
    def _():
        work(pair[0], pair[1])


def pack_cone(ref, width, low, high, at):
    for k in range(CONE):
        for z in range(width):
            low[at + z] = row_of(ref, z, width + k)
            high[at + z] = row_of(ref, z, ROWS - width - CONE + k)
        at += width
    return at


def pack_stiffness_kernel(s, *pair):
    base = core_index() * PART

    def work(low, high):
        def plane(z, carry):
            for k in range(REACH):
                low[k * PART + z] = row_of(s, base + z, k)
                high[k * PART + z] = row_of(s, base + z, ROWS - REACH + k)
            return carry

        lax.fori_loop(0, PART, plane, 0)
        pack_cone(s, REACH, low, high, REACH * PART)

    by_parity(pair, work)


def pack_waves_kernel(u1, u0, receivers, observed, *pair):
    def work(low, high):
        at = pack_fields((u1, u0), (REACH, REACH - 1), low, high, 0)
        at = pack_cone(u1, REACH, low, high, at)
        at = pack_cone(u0, REACH - 1, low, high, at)
        where = receivers[...].astype(f32)
        empty = jnp.zeros((2, LANES), f32)
        for side, rows in ((low, lambda n: slice(0, n)), (high, lambda n: slice(ROWS - n, ROWS))):
            parts = [where[rows(EDGE)]]
            for k in range(STEPS - 1, -1, -1):
                parts.append(observed[k][rows(k + 1)])
            parts.append(empty)
            both = jnp.concatenate(parts, 0)
            side[at] = both[:XT]
            side[at + 1] = both[XT:]

    by_parity(pair, work)


def pack_adjoint_kernel(l6, l7, *pair):
    by_parity(pair, lambda low, high: pack_fields((l6, l7), (REACH, REACH - 1), low, high, 0))


def pack(kernel, name, tiles, *arrays):
    shape = pltpu.VMEM((tiles, XT, LANES), f32)
    return pl.pallas_call(
        kernel,
        out_shape=(shape, shape),
        in_specs=[VMEM] * len(arrays),
        out_specs=(VMEM, VMEM),
        compiler_params=pltpu.CompilerParams(vmem_limit_bytes=6 << 20),
        cost_estimate=pl.CostEstimate(flops=0, bytes_accessed=1 << 21, transcendentals=0),
        name=name,
    )(*arrays)


def fill(ext, own, off):
    def plane(z, carry):
        for k in range(ROWS):
            ext[off + k, z] = row_of(own, z, k)
        return carry

    lax.fori_loop(0, NZ, plane, 0)


def fill_halo(ext, off, low, high, at, width):
    for k in range(width):
        ext[off - width + k] = low[at + k * NZ : at + (k + 1) * NZ]
        ext[off + ROWS + k] = high[at + k * NZ : at + (k + 1) * NZ]


def fill_cone(ext, low, high, at, width):
    for k in range(CONE):
        ext[OFF - width - CONE + k, :width] = low[at + k * width : at + (k + 1) * width]
        ext[OFF + ROWS + width + k, :width] = high[at + k * width : at + (k + 1) * width]


def coefficients(stiff, diag, cx, cy, cz, lo, hi, planes, lane, tile):
    x_end = (lane == LANES - 1) & (tile == XT - 1)
    x_start = (lane == 0) & (tile == 0)

    def faces(first, count):
        for e in (first + r for r in range(count)):
            for z in range(planes):
                cy[e, z] = HALF * (stiff[e, z] + stiff[e + 1, z])

    def rows(first, count):
        for e in (first + r for r in range(count)):
            below = None
            following = HALF * stiff[e, 0]
            for z in range(planes):
                s = following
                face = s + jnp.where(x_end, 0.0, x_next(s, lane))
                total = face + (s + jnp.where(x_start, 0.0, x_prev(s, lane)))
                if z < NZ - 1:
                    following = HALF * stiff[e, z + 1]
                    above = s + following
                else:
                    above = s
                total = total + above + (below if z > 0 else s) + cy[e, z] + cy[e - 1, z]
                cx[e, z] = jnp.where(x_end, 0.0, face)
                cz[e, z] = above
                diag[e, z] = 2.0 - total
                below = above

    in_blocks(lo - 1, hi, 4, faces)
    in_blocks(lo, hi, 4, rows)


def leap(now, before, after, base, diag, cx, cy, cz, outer, lane, slope, inject=None):
    def cells(e, planes, slope_row):
        f = e - base
        for z in range(planes):
            u = now[f, z]
            c = cx[e, z]
            following = x_next(u, lane)
            acc = diag[e, z] * u - before[f, z]
            acc = acc + c * following + x_prev(c * u, lane)
            acc = acc + cy[e, z] * now[f + 1, z] + cy[e - 1, z] * now[f - 1, z]
            if z < NZ - 1:
                acc = acc + cz[e, z] * now[f, z + 1]
            if z > 0:
                acc = acc + cz[e, z - 1] * now[f, z - 1]
            if z == 0 and inject is not None:
                acc = acc + inject[e - OFF + EDGE]
            after[f, z] = acc
            if slope_row is not None:
                slope[slope_row, z] = following - u

    def own(i, carry):
        for r in range(4):
            cells(OFF + 4 * i + r, NZ, 4 * i + r)
        return carry

    lax.fori_loop(0, ROWS // 4, own, 0)
    for e, planes in outer:
        cells(e, planes, None)


def outer_rows(k, cone):
    whole = STEPS - k
    rows = [(OFF - whole + j, NZ) for j in range(whole)] + [(OFF + ROWS + j, NZ) for j in range(whole)]
    if cone:
        rows += [(OFF - whole - CONE + j, whole) for j in range(CONE)]
        rows += [(OFF + ROWS + whole + j, whole) for j in range(CONE)]
    return rows


def three_parts(f):
    parts = []
    for _ in range(3):
        part = f.astype(jnp.bfloat16)
        parts.append(part.astype(f32))
        f = f - parts[-1]
    return jnp.concatenate(parts, 0).astype(jnp.bfloat16)


def misfit_surfaces(waves, receivers, observed, edges, surf, lane, tile):
    column = lax.broadcasted_iota(jnp.int32, (LANES, LANES), 0)
    plan = []
    for j in range(SURF_ROWS):
        y = j - EDGE
        if y < 0:
            used, at = range(-y - 1, STEPS), edges[0][:EDGE].astype(jnp.int32)[j : j + 1]
        elif y < ROWS:
            used, at = range(STEPS), receivers[y : y + 1, :]
        else:
            used, at = range(y - ROWS, STEPS), edges[1][:EDGE].astype(jnp.int32)[y - ROWS : y - ROWS + 1]
        pick = jnp.where(column == (at & (LANES - 1)), 1.0, 0.0).astype(jnp.bfloat16)
        held = jnp.where(tile == (at >> 7), 1.0, 0.0)
        surface = jnp.concatenate([waves[k + 1][OFF + y, 0] for k in used], 0)
        lanes_of = jnp.dot(three_parts(surface), pick, preferred_element_type=f32)
        plan.append((j, used, pick, held, lanes_of))
    for j, used, pick, held, lanes_of in plan:
        y = j - EDGE
        size = len(used) * XT
        lanes_of = lanes_of[:size] + lanes_of[size : 2 * size] + lanes_of[2 * size :]
        parts = []
        for i, k in enumerate(used):
            record = jnp.sum(lanes_of[i * XT : (i + 1) * XT] * held, axis=0, keepdims=True)
            if 0 <= y < ROWS:
                trace = observed[k, y : y + 1, :]
            else:
                skip = EDGE + sum(m + 1 for m in range(k + 1, STEPS))
                r = skip + (y + k + 1 if y < 0 else y - ROWS)
                trace = edges[0 if y < 0 else 1][r : r + 1]
            parts.append(held * (record - trace))
        back = lax.dot_general(
            three_parts(jnp.concatenate(parts, 0)), pick, (((1,), (1,)), ((), ())), preferred_element_type=f32
        )
        back = back[:size] + back[size : 2 * size] + back[2 * size :]
        for i, k in enumerate(used):
            surf[k, j] = back[i * XT : (i + 1) * XT]


def forward_kernel(
    source_pos, source_wave, u0, u1, s, s_even, s_odd, s_even_other, s_odd_other, u_even, u_odd, receivers, observed,
    w1, w2, w3, w4, w5, d1, d2, d3, d4, d5, diag, cx, cy, cz, surf,
    stiff, before, edge,
):
    lane, tile = iotas()
    waves = (w1, w2, w3, w4, w5)
    slopes = (d1, d2, d3, d4)
    for ext, own in ((stiff, s), (w1, u1), (before, u0)):
        fill(ext, own, OFF)
    core = core_index()

    def stiffness_halos(low, high):
        for part, base in ((0, core * PART), (1, (1 - core) * PART)):
            for k in range(REACH):
                stiff[OFF - REACH + k, pl.ds(base, PART)] = low[part][k * PART : (k + 1) * PART]
                stiff[OFF + ROWS + k, pl.ds(base, PART)] = high[part][k * PART : (k + 1) * PART]
        fill_cone(stiff, low[0], high[0], REACH * PART, REACH)

    def wave_halos(low, high):
        fill_halo(w1, OFF, low, high, 0, REACH)
        fill_halo(before, OFF, low, high, REACH * NZ, REACH - 1)
        at = (2 * REACH - 1) * NZ
        fill_cone(w1, low, high, at, REACH)
        fill_cone(before, low, high, at + REACH * CONE, REACH - 1)
        for i, ref in enumerate((low, high)):
            edge[2 * i] = ref[TILE_U - 2]
            edge[2 * i + 1] = ref[TILE_U - 1]

    by_parity(((s_even, s_even_other), (s_odd, s_odd_other)), stiffness_halos)
    by_parity((u_even, u_odd), wave_halos)
    top, bottom = OFF - REACH, OFF + ROWS + REACH
    for lo, hi, planes in (
        (top + 1, bottom - 1, NZ),
        (top + 1 - CONE, top + 1, STEPS),
        (bottom - 1, bottom - 1 + CONE, STEPS),
    ):
        coefficients(stiff, diag, cx, cy, cz, lo, hi, planes, lane, tile)

    gy = lax.axis_index("gy")

    @pl.when(gy == 0)
    def _():
        cy[OFF - 1] = jnp.zeros((NZ, XT, LANES), f32)

    @pl.when(gy == lax.axis_size("gy") - 1)
    def _():
        cy[OFF + ROWS - 1] = jnp.zeros((NZ, XT, LANES), f32)

    z_src = source_pos[0, 0]
    e_src = source_pos[0, 1] - gy * ROWS + OFF
    x_src = source_pos[0, 2]
    spot = (tile * LANES + lane) == x_src
    for k in range(STEPS):
        older = before if k == 0 else waves[k - 1]
        after = waves[k + 1]
        leap(waves[k], older, after, 0, diag, cx, cy, cz, outer_rows(k, True), lane, slopes[k])
        reach = STEPS - k + CONE

        @pl.when((e_src >= OFF - reach) & (e_src < OFF + ROWS + reach))
        def _():
            add = jnp.where(spot, TIME_STEP_SQ * source_wave[0, k], 0.0)
            after[e_src, z_src] = after[e_src, z_src] + add

    def last_slope(i, carry):
        for y in (4 * i + r for r in range(4)):
            for z in range(NZ):
                u = w5[OFF + y, z]
                d5[y, z] = x_next(u, lane) - u
        return carry

    lax.fori_loop(0, ROWS // 4, last_slope, 0)
    edges = [jnp.concatenate([edge[2 * i], edge[2 * i + 1]], 0) for i in range(2)]
    misfit_surfaces(waves, receivers, observed, edges, surf, lane, tile)


def forward(*args):
    one = jax.ShapeDtypeStruct(FIELD, f32)
    own = jax.ShapeDtypeStruct((ROWS, NZ, XT, LANES), f32)
    surf = jax.ShapeDtypeStruct((STEPS, SURF_ROWS, XT, LANES), f32)
    outs = (one,) * (STEPS + 1) + (own,) * (STEPS + 1) + (one,) * 4 + (surf,)
    return pl.pallas_call(
        forward_kernel,
        out_shape=outs,
        in_specs=[SMEM] * 2 + [VMEM] * (len(args) - 2),
        out_specs=(VMEM,) * len(outs),
        scratch_shapes=[pltpu.VMEM(FIELD, f32)] * 2 + [pltpu.VMEM((4, XT, LANES), f32)],
        compiler_params=pltpu.CompilerParams(vmem_limit_bytes=16 << 20),
        cost_estimate=pl.CostEstimate(flops=1 << 25, bytes_accessed=1 << 24, transcendentals=0),
        name="forward",
    )(*args)


def adjoint_kernel(
    l6, l7, even, odd, w1, w2, w3, w4, w5, d1, d2, d3, d4, d5, diag, cx, cy, cz, surf,
    keep, send,
    m6, m5, m4, m3, m2, before, g6, g5, g4, g3, face_y, grad,
):
    lane, tile = iotas()
    x_end = (lane == LANES - 1) & (tile == XT - 1)
    x_side = x_end | ((lane == 0) & (tile == 0))
    lams = (m6, m5, m4, m3, m2)
    slopes = (g6, g5, g4, g3)
    fill(m6, l6, REACH)
    fill(before, l7, REACH)

    def halos(low, high):
        fill_halo(m6, REACH, low, high, 0, REACH)
        fill_halo(before, REACH, low, high, REACH * NZ, REACH - 1)

    by_parity((even, odd), halos)
    for k in range(STEPS):
        older = before if k == 0 else lams[k - 1]
        leap(
            lams[k], older, lams[k + 1], OFF - REACH, diag, cx, cy, cz, outer_rows(k, False), lane, slopes[k],
            surf.at[STEPS - 1 - k],
        )

    pairs = ((w5, m6, d5, g6), (w4, m5, d4, g5), (w3, m4, d3, g4), (w2, m3, d2, g3), (w1, m2, d1, None))
    for z in range(NZ):
        total = None
        for w, m, _, _ in pairs:
            part = (w[OFF, z] - w[OFF - 1, z]) * (m[REACH, z] - m[REACH - 1, z])
            total = part if total is None else total + part
        face_y[z] = total

    def two_rows(i, carry):
        below_y = [face_y[z] for z in range(NZ)]
        for y in (2 * i, 2 * i + 1):
            e = y + OFF
            below = None
            us = [w[e, 0] for w, _, _, _ in pairs]
            f = y + REACH
            ls = [m[f, 0] for _, m, _, _ in pairs]
            for z in range(NZ):
                fx = fy = fz = cell = None
                next_us, next_ls = [], []
                for (w, m, d, g), u, l in zip(pairs, us, ls, strict=True):
                    px = d[y, z] * (g[y, z] if g is not None else x_next(l, lane) - l)
                    py = (w[e + 1, z] - u) * (m[f + 1, z] - l)
                    both = u * l
                    if z < NZ - 1:
                        un, ln = w[e, z + 1], m[f, z + 1]
                        next_us.append(un)
                        next_ls.append(ln)
                        pz = (un - u) * (ln - l)
                    else:
                        pz = both
                    fx = px if fx is None else fx + px
                    fy = py if fy is None else fy + py
                    fz = pz if fz is None else fz + pz
                    cell = both if cell is None else cell + both
                us, ls = next_us, next_ls
                fx = jnp.where(x_end, 0.0, fx)
                total = fx + x_prev(fx, lane) + jnp.where(x_side, cell, 0.0)
                total = total + fy + below_y[z] + fz + (cell if z == 0 else below)
                below_y[z] = fy
                below = fz
                grad[z, pl.ds(y, XT, stride=ROWS), :] = -HALF * total
        for z in range(NZ):
            face_y[z] = below_y[z]
        return carry

    lax.fori_loop(0, ROWS // 2, two_rows, 0)
    core = core_index()
    for group in range(2):
        keep[group] = grad[pl.ds(8 * group + 4 * core, 4)]
        send[group] = grad[pl.ds(8 * group + 4 * (1 - core), 4)]


def adjoint(*args):
    part = jax.ShapeDtypeStruct((2, 4, XT * ROWS, LANES), f32)
    own = pltpu.VMEM((ROWS, NZ, XT, LANES), f32)
    return pl.pallas_call(
        adjoint_kernel,
        out_shape=(part, part),
        in_specs=[VMEM] * len(args),
        out_specs=(VMEM, VMEM),
        scratch_shapes=[pltpu.VMEM(SHORT, f32)] * (STEPS + 2)
        + [own] * STEPS
        + [
            pltpu.VMEM((NZ, XT, LANES), f32),
            pltpu.VMEM((NZ, XT * ROWS, LANES), f32),
        ],
        compiler_params=pltpu.CompilerParams(vmem_limit_bytes=16 << 20),
        cost_estimate=pl.CostEstimate(flops=1 << 25, bytes_accessed=1 << 24, transcendentals=0),
        name="adjoint",
    )(*args)


def finish_kernel(mine, other, out, sems):
    core = core_index()
    copies = []
    for group in range(2):
        for i, (part, base) in enumerate(((mine, core), (other, 1 - core))):
            target = out.at[pl.ds(8 * group + 4 * base, 4)]
            copies.append(pltpu.make_async_copy(part.at[group], target, sems.at[2 * group + i]))
    for copy in copies:
        copy.start()
    for copy in copies:
        copy.wait()


def finish(mine, other):
    return pl.pallas_call(
        finish_kernel,
        out_shape=jax.ShapeDtypeStruct((NZ, XT * ROWS, LANES), f32),
        in_specs=[VMEM, VMEM],
        out_specs=pl.BlockSpec(memory_space=pl.ANY),
        scratch_shapes=[pltpu.SemaphoreType.DMA((4,))],
        compiler_params=pltpu.CompilerParams(vmem_limit_bytes=2 << 20),
        name="finish",
    )(mine, other)


def swap_even(block):
    count = lax.axis_size("gy")
    pairs = [(i, i + 1) for i in range(0, count - 1, 2)]
    return lax.ppermute(block, "gy", pairs + [(j, i) for i, j in pairs])


def swap_odd(block):
    count = lax.axis_size("gy")
    pairs = [(i, i + 1) for i in range(1, count - 1, 2)]
    return lax.ppermute(block, "gy", pairs + [(j, i) for i, j in pairs])


def swap_core(block):
    return lax.ppermute(block, "shot", [(0, 1), (1, 0), (2, 3), (3, 2)])


def swap_far(block):
    return lax.ppermute(block, "shot", [(0, 2), (2, 0), (1, 3), (3, 1)])


def body(
    stiffness,
    first_moment,
    second_moment,
    wave_prev,
    wave_now,
    adjoint_next,
    adjoint_now,
    observed,
    receiver_x,
    source_pos,
    source_wave,
):
    shot = lax.axis_index("shot")
    core, far = shot % 2, shot // 2
    s = native(stiffness)
    u0, u1 = native(wave_prev[0]), native(wave_now[0])
    l6, l7 = native(adjoint_now[0]), native(adjoint_next[0])
    first, second = native(first_moment), native(second_moment)

    s_even, s_odd = pack(pack_stiffness_kernel, "pack_stiffness", TILE_S, s)
    s_even, s_odd = swap_even(s_even), swap_odd(s_odd)
    u_even, u_odd = pack(pack_waves_kernel, "pack_waves", TILE_U, u1, u0, receiver_x[0], observed[0])
    u_even, u_odd = swap_even(u_even), swap_odd(u_odd)
    s_even_other, s_odd_other = swap_core(s_even), swap_core(s_odd)
    l6_after, l7_after, s_even_other, s_odd_other = lax.optimization_barrier((l6, l7, s_even_other, s_odd_other))
    l_even, l_odd = pack(pack_adjoint_kernel, "pack_adjoint", TILE_L, l6_after, l7_after)
    l_even, l_odd = swap_even(l_even), swap_odd(l_odd)
    moments = jnp.stack([first, second])
    u_even, u_odd, moments = lax.optimization_barrier((u_even, u_odd, moments))
    moments = swap_far(moments)
    fields = forward(
        source_pos, source_wave, u0, u1, s, s_even, s_odd, s_even_other, s_odd_other, u_even, u_odd,
        receiver_x[0], observed[0],
    )
    keep, send = adjoint(l6, l7, l_even, l_odd, *fields)
    keep, send, moments = lax.optimization_barrier((keep, send, moments))
    chip_sum = keep + swap_core(send)
    share = chip_sum + swap_far(chip_sum)

    is_far = (jnp.arange(2) == far)[:, None, None, None]
    first_two = jnp.where(is_far, first[None], moments[0][None])
    second_two = jnp.where(is_far, second[None], moments[1][None])
    stiff_two = jnp.where(core == 0, s.reshape(2, 2, 4, XT * ROWS, LANES)[:, 0], s.reshape(2, 2, 4, XT * ROWS, LANES)[:, 1])
    first_new = BETA_ONE * first_two + (1.0 - BETA_ONE) * share
    second_new = BETA_TWO * second_two + (1.0 - BETA_TWO) * share * share
    updated = stiff_two - LEARN_RATE * (first_new / (1.0 - BETA_ONE**ADAM_TICKS)) / (
        jnp.sqrt(second_new / (1.0 - BETA_TWO**ADAM_TICKS)) + ADAM_EPS
    )
    other = swap_core(updated)
    stiffness_new = finish(updated, other)
    first_out = jnp.where(far == 0, first_new[0], first_new[1])
    second_out = jnp.where(far == 0, second_new[0], second_new[1])
    return (from_native(stiffness_new), from_native(first_out), from_native(second_out))


def solution(mesh):
    return jax.shard_map(
        body,
        mesh=mesh,
        in_specs=(
            P(None, "gy", None),
            P("shot", "gy", None),
            P("shot", "gy", None),
            P("shot", None, "gy", None),
            P("shot", None, "gy", None),
            P("shot", None, "gy", None),
            P("shot", None, "gy", None),
            P("shot", None, "gy", None),
            P("shot", "gy", None),
            P("shot", None),
            P("shot", None),
        ),
        out_specs=(P(None, "gy", None), P("shot", "gy", None), P("shot", "gy", None)),
        check_vma=False,
    )
```

time: 96.4 us -> 71.3 us (0.74)
  waiting for transfers between devices: 44.8 us -> 25.8 us
  Pallas kernels: 25.1 us -> 14.8 us
  local copies, waits for them, and re-layouts: 1.87 us -> 6.66 us
    ppermute x2, waiting for transfers between devices: 43.2 us -> 14.2 us  [swap_far(): return lax.ppermute(block, 'shot', [(0, 2), (2, 0), (1, 3), (3, 1)])]
    pallas_call x4 -> x6, Pallas kernels: 25.1 us -> 14.8 us  [the longest x1 7.25 us: forward(): pl.pallas_call(forward_kernel, out_shape=outs, in_specs=[SMEM] * 2 + [VME...]
    ppermute x4 -> x6, waiting for transfers between devices: 0.01 us -> 8.7 us  [the longest x3 7.59 us: swap_odd(): return lax.ppermute(block, 'gy', pairs + [(j, i) for i, j in pairs])]
    unnamed x22 -> x36, local copies, waits for them, and re-layouts: 0.05 us -> 6.64 us
    ppermute x4 -> x6, starting transfers between devices: 16.6 us -> 14.3 us  [the longest x3 12.5 us: swap_odd(): return lax.ppermute(block, 'gy', pairs + [(j, i) for i, j in pairs])]
    ppermute x2 -> x4, starting transfers between devices: 1.87 us -> 3.49 us  [swap_core(): return lax.ppermute(block, 'shot', [(0, 1), (1, 0), (2, 3), (3, 2)])]
    ppermute x2 -> x4, waiting for transfers between devices: 1.6 us -> 2.97 us  [swap_core(): return lax.ppermute(block, 'shot', [(0, 1), (1, 0), (2, 3), (3, 2)])]
    broadcast_in_dim x1, local copies, waits for them, and re-layouts: 0.99 us -> 0.02 us  [body(): second_two = jnp.where(is_far, second[None], moments[1][None])]
  transfers between devices with their start and end apart: 8 -> 12, of which waited for: 4 -> 9; matrix products, arithmetic and copies ran while one was open for 3% -> 2% of each run, Pallas kernels for 13% -> 20%
where the time goes in v3:
time: 71.3 us; the launch traced here: 70.8 us
  waiting for transfers between devices  25.8 us (36%)
  starting transfers between devices  20.6 us (29%)
  Pallas kernels  14.8 us (21%)
  local copies, waits for them, and re-layouts  6.66 us (9%)
  other arithmetic  2.02 us (3%)
  between operations  0.81 us (1%)
    ppermute x2, waiting for transfers between devices, swap_far(): return lax.ppermute(block, 'shot', [(0, 2), (2, 0), (1, 3), (3, 1)])  14.2 us
    ppermute x3, starting transfers between devices, swap_odd(): return lax.ppermute(block, 'gy', pairs + [(j, i) for i, j in pairs])  12.5 us
    ppermute x3, waiting for transfers between devices, swap_odd(): return lax.ppermute(block, 'gy', pairs + [(j, i) for i, j in pairs])  7.59 us
    pallas_call x1, Pallas kernels, forward(): pl.pallas_call(forward_kernel, out_shape=outs, in_specs=[SMEM] * 2 + [VME...  7.25 us
    unnamed x36, local copies, waits for them, and re-layouts  6.64 us
    pallas_call x1, Pallas kernels, adjoint(): pl.pallas_call(adjoint_kernel, out_shape=(part, part), in_specs=[VMEM] *...  6.14 us
    ppermute x4, starting transfers between devices, swap_core(): return lax.ppermute(block, 'shot', [(0, 1), (1, 0), (2, 3), (3, 2)])  3.49 us
    ppermute x4, waiting for transfers between devices, swap_core(): return lax.ppermute(block, 'shot', [(0, 1), (1, 0), (2, 3), (3, 2)])  2.97 us
  transfers between devices with their start and end apart: 12, of which 9 were waited for; matrix products, arithmetic and copies ran while one was open for 2% of the time, Pallas kernels for 20%

profile of v3, /device:TPU:97, one launch (start us, length us, event | category | flops | bytes accessed | tf_op | source)
XLA Modules:
  0.0 70.8 jit_solution(1260142139041044406)
XLA Ops:
  0.6 1.0 %copy-done = f32[16,8,1024]{2,1,0:T(8,128)S(1)} copy-done((f32[16,8,1024]{2,1,0:T(8,128)S(1)}, f32[16,8,1024]{2,1,0:T(8,128)}, u32[]{:S(2)}) %copy-start) | copy-done | bytes 524312
  1.8 1.4 %collective-permute-start = (f32[55,8,128]{2,1,0:T(8,128)S(1)}, f32[55,8,128]{2,1,0:T(8,128)S(1)}, u32[]{:S(2)}, u32[]{:S(2)}) collective-permute-start(f32[55,8,128]{2,1,0:T(8,128)S(1)} %get-tuple-element.36), channel_id=1, source_target_pairs={{0,1},{2,3},{4,5},{6,7},{8,9},{10,11},{12,13},{14,15},{16,17},{18,... | collective-permute-start | bytes 675848 | tf_op jit(solution)/shard_map/ppermute | solution.py:527
  3.2 4.3 %collective-permute-start.2 = (f32[55,8,128]{2,1,0:T(8,128)S(1)}, f32[55,8,128]{2,1,0:T(8,128)S(1)}, u32[]{:S(2)}, u32[]{:S(2)}) collective-permute-start(f32[55,8,128]{2,1,0:T(8,128)S(1)} %get-tuple-element.37), channel_id=1, source_target_pairs={{1,2},{3,4},{5,6},{7,8},{9,10},{11,12},{13,14},{15,16},{17,18},{19... | collective-permute-start | bytes 675848 | tf_op jit(solution)/shard_map/ppermute | solution.py:533
  7.5 1.0 %copy-done.2 = f32[1,16,8,1024]{3,2,1,0:T(8,128)S(1)} copy-done((f32[1,16,8,1024]{3,2,1,0:T(8,128)S(1)}, f32[1,16,8,1024]{3,2,1,0:T(8,128)}, u32[]{:S(2)}) %copy-start.2) | copy-done | bytes 524312
  8.5 1.0 %copy-done.4 = f32[1,16,8,1024]{3,2,1,0:T(8,128)S(1)} copy-done((f32[1,16,8,1024]{3,2,1,0:T(8,128)S(1)}, f32[1,16,8,1024]{3,2,1,0:T(8,128)}, u32[]{:S(2)}) %copy-start.4) | copy-done | bytes 524312
  11.4 4.0 %collective-permute-start.7 = (f32[173,8,128]{2,1,0:T(8,128)S(1)}, f32[173,8,128]{2,1,0:T(8,128)S(1)}, u32[]{:S(2)}, u32[]{:S(2)}) collective-permute-start(f32[173,8,128]{2,1,0:T(8,128)S(1)} %get-tuple-element.45), channel_id=1, source_target_pairs={{1,2},{3,4},{5,6},{7,8},{9,10},{11,12},{13,14},{15,16},{17,18},{19... | collective-permute-start | bytes 2125832 | tf_op jit(solution)/shard_map/ppermute | solution.py:533
  15.4 1.6 %collective-permute-start.1 = (f32[55,8,128]{2,1,0:T(8,128)S(1)}, f32[55,8,128]{2,1,0:T(8,128)S(1)}, u32[]{:S(2)}, u32[]{:S(2)}) collective-permute-start(f32[55,8,128]{2,1,0:T(8,128)S(1)} %collective-permute-done.s_even), channel_id=1, source_target_pairs={{0,64},{64,0},{128,192},{192,128},{1,65},{65,1},{129,193},{193,129... | collective-permute-start | bytes 675848 | tf_op jit(solution)/shard_map/ppermute | solution.py:537
  17.1 1.0 %collective-permute-done.1.s_even_other = f32[55,8,128]{2,1,0:T(8,128)S(1)} collective-permute-done((f32[55,8,128]{2,1,0:T(8,128)S(1)}, f32[55,8,128]{2,1,0:T(8,128)S(1)}, u32[]{:S(2)}, u32[]{:S(2)}) %collective-permute-start.1) | collective-permute-done | bytes 225312 | tf_op jit(solution)/shard_map/ppermute | solution.py:537
  18.5 1.0 %copy-done.6 = f32[1,16,8,1024]{3,2,1,0:T(8,128)S(1)} copy-done((f32[1,16,8,1024]{3,2,1,0:T(8,128)S(1)}, f32[1,16,8,1024]{3,2,1,0:T(8,128)}, u32[]{:S(2)}) %copy-start.6) | copy-done | bytes 524312
  19.5 1.0 %copy-done.8 = f32[1,16,8,1024]{3,2,1,0:T(8,128)S(1)} copy-done((f32[1,16,8,1024]{3,2,1,0:T(8,128)S(1)}, f32[1,16,8,1024]{3,2,1,0:T(8,128)}, u32[]{:S(2)}) %copy-start.8) | copy-done | bytes 524312
  21.1 4.2 %collective-permute-start.5 = (f32[144,8,128]{2,1,0:T(8,128)S(1)}, f32[144,8,128]{2,1,0:T(8,128)S(1)}, u32[]{:S(2)}, u32[]{:S(2)}) collective-permute-start(f32[144,8,128]{2,1,0:T(8,128)S(1)} %get-tuple-element.41), channel_id=1, source_target_pairs={{1,2},{3,4},{5,6},{7,8},{9,10},{11,12},{13,14},{15,16},{17,18},{19... | collective-permute-start | bytes 1769480 | tf_op jit(solution)/shard_map/ppermute | solution.py:533
  25.4 1.0 %pad_maximum_fusion = f32[2,4,64,128]{3,2,1,0:T(8,128)S(1)} fusion(f32[1,4,64,128]{3,2,1,0:T(8,128)} %bitcast.96, f32[1,4,64,128]{3,2,1,0:T(8,128)} %bitcast.98), kind=kLoop, calls=%fused_computation.7 | loop fusion | flops 65536 | bytes 524288 | tf_op jit(solution)/shard_map/stack | solution.py:572
  26.4 1.1 %collective-permute-done.6.u_even = f32[173,8,128]{2,1,0:T(8,128)S(1)} collective-permute-done((f32[173,8,128]{2,1,0:T(8,128)S(1)}, f32[173,8,128]{2,1,0:T(8,128)S(1)}, u32[]{:S(2)}, u32[]{:S(2)}) %collective-permute-start.6) | collective-permute-done | bytes 708640 | tf_op jit(solution)/shard_map/ppermute | solution.py:527
  27.5 4.7 %collective-permute-done.7.u_odd = f32[173,8,128]{2,1,0:T(8,128)S(1)} collective-permute-done((f32[173,8,128]{2,1,0:T(8,128)S(1)}, f32[173,8,128]{2,1,0:T(8,128)S(1)}, u32[]{:S(2)}, u32[]{:S(2)}) %collective-permute-start.7) | collective-permute-done | bytes 708640 | tf_op jit(solution)/shard_map/ppermute | solution.py:533
  32.2 2.5 %collective-permute-start.8 = (f32[2,4,64,128]{3,2,1,0:T(8,128)S(1)}, f32[2,4,64,128]{3,2,1,0:T(8,128)S(1)}, u32[]{:S(2)}, u32[]{:S(2)}) collective-permute-start(f32[2,4,64,128]{3,2,1,0:T(8,128)S(1)} %pad_maximum_fusion), channel_id=1, source_target_pairs={{0,128},{128,0},{64,192},{192,64},{1,129},{129,1},{65,193},{193,65... | collective-permute-start | bytes 786440 | tf_op jit(solution)/shard_map/ppermute | solution.py:541
  34.8 7.2 %forward.1 = (f32[24,16,8,128]{3,2,1,0:T(8,128)S(1)}, f32[24,16,8,128]{3,2,1,0:T(8,128)S(1)}, f32[24,16,8,128]{3,2,1,0:T(8,128)S(1)}, f32[24,16,8,128]{3,2,1,0:T...) custom-call(s32[1,3]{1,0:T(1,128)S(1)} %copy-done.14, ...), custom_call_target="tpu_custom_call" | custom-call | flops 33554432 | bytes 16777216 | tf_op jit(solution)/shard_map/forward/pallas_call | solution.py:390
  42.1 2.8 %collective-permute-done.5.odd = f32[144,8,128]{2,1,0:T(8,128)S(1)} collective-permute-done((f32[144,8,128]{2,1,0:T(8,128)S(1)}, f32[144,8,128]{2,1,0:T(8,128)S(1)}, u32[]{:S(2)}, u32[]{:S(2)}) %collective-permute-start.5) | collective-permute-done | bytes 589856 | tf_op jit(solution)/shard_map/ppermute | solution.py:533
  44.9 6.1 %adjoint.1 = (f32[2,4,64,128]{3,2,1,0:T(8,128)S(1)}, f32[2,4,64,128]{3,2,1,0:T(8,128)S(1)}) custom-call(f32[16,64,128]{2,1,0:T(8,128)S(1)} %bitcast.88, f32[16,64,128]{2,1,0:T(8,128)S(1)} %bitcast.90, f32[144,8,128]{2,1,0:T(8,128)S(1)} %collective-permute-done.4.even, f32[144,8,128]{2,1,0:T(8,128)S(1)} %collective-permute-done.5.odd, ...), custom_call_target="tpu_custom_call" | custom-call | flops 33554432 | bytes 16777216 | tf_op jit(solution)/shard_map/adjoint/pallas_call | solution.py:482
  51.1 5.4 %collective-permute-done.8 = f32[2,4,64,128]{3,2,1,0:T(8,128)S(1)} collective-permute-done((f32[2,4,64,128]{3,2,1,0:T(8,128)S(1)}, f32[2,4,64,128]{3,2,1,0:T(8,128)S(1)}, u32[]{:S(2)}, u32[]{:S(2)}) %collective-permute-start.8) | collective-permute-done | bytes 262176 | tf_op jit(solution)/shard_map/ppermute | solution.py:541
  57.0 1.2 %collective-permute-done.9 = f32[2,4,64,128]{3,2,1,0:T(8,128)S(1)} collective-permute-done((f32[2,4,64,128]{3,2,1,0:T(8,128)S(1)}, f32[2,4,64,128]{3,2,1,0:T(8,128)S(1)}, u32[]{:S(2)}, u32[]{:S(2)}) %collective-permute-start.9) | collective-permute-done | bytes 262176 | tf_op jit(solution)/shard_map/ppermute | solution.py:537
  58.5 8.8 %collective-permute-done.10 = f32[2,4,64,128]{3,2,1,0:T(8,128)S(1)} collective-permute-done((f32[2,4,64,128]{3,2,1,0:T(8,128)S(1)}, f32[2,4,64,128]{3,2,1,0:T(8,128)S(1)}, u32[]{:S(2)}, u32[]{:S(2)}) %collective-permute-start.10) | collective-permute-done | bytes 262176 | tf_op jit(solution)/shard_map/ppermute | solution.py:541
  67.5 1.3 %collective-permute-start.11 = (f32[2,4,64,128]{3,2,1,0:T(8,128)S(1)}, f32[2,4,64,128]{3,2,1,0:T(8,128)S(1)}, u32[]{:S(2)}, u32[]{:S(2)}) collective-permute-start(f32[2,4,64,128]{3,2,1,0:T(8,128)S(1)} %get-tuple-element.69.mine), channel_id=1, source_target_pairs={{0,64},{64,0},{128,192},{192,128},{1,65},{65,1},{129,193},{193,129... | collective-permute-start | bytes 786440 | tf_op jit(solution)/shard_map/ppermute | solution.py:537
  68.8 0.7 %fusion.4 = (f32[4,8,1024]{2,1,0:T(8,128)}, f32[4,8,1024]{2,1,0:T(8,128)}) fusion(f32[2,4,64,128]{3,2,1,0:T(8,128)S(1)} %get-tuple-element.71, pred[]{:T(512)S(6)} %eq.22, f32[2,4,64,128]{3,2,1,0:T(8,128)S(1)} %get-tuple-element.70), kind=kLoop, calls=%fused_computation.10 | loop fusion | flops 65536 | bytes 786433 | tf_op jit(solution)/shard_map/reshape | solution.py:48
  70.0 0.8 %finish.1 = f32[16,64,128]{2,1,0:T(8,128)} custom-call(f32[2,4,64,128]{3,2,1,0:T(8,128)S(1)} %get-tuple-element.69.mine, f32[2,4,64,128]{3,2,1,0:T(8,128)S(1)} %collective-permute-done.11.other), custom_call_target="tpu_custom_call" | custom-call | tf_op jit(solution)/shard_map/finish/pallas_call | solution.py:513
  (48 shorter events, 4.6 us)
Async XLA Ops:
  1.7 33.1 %copy-start.1 = (f32[16,8,1024]{2,1,0:T(8,128)S(1)}, f32[16,8,1024]{2,1,0:T(8,128)}, u32[]{:S(2)}) copy-start(f32[16,8,1024]{2,1,0:T(8,128)} %param.11) | copy-start | bytes 1572868
  1.7 33.1 %copy-start.13 = (s32[1,8,128]{2,1,0:T(8,128)S(1)}, s32[1,8,128]{2,1,0:T(8,128)}, u32[]{:S(2)}) copy-start(s32[1,8,128]{2,1,0:T(8,128)} %param.19) | copy-start | bytes 12292
  1.7 33.1 %copy-start.14 = (s32[1,3]{1,0:T(1,128)S(1)}, s32[1,3]{1,0:T(1,128)}, u32[]{:S(2)}) copy-start(s32[1,3]{1,0:T(1,128)} %source_pos.1) | copy-start | bytes 40
  1.7 33.1 %copy-start.15 = (f32[1,4]{1,0:T(1,128)S(1)}, f32[1,4]{1,0:T(1,128)}, u32[]{:S(2)}) copy-start(f32[1,4]{1,0:T(1,128)} %source_wave.1) | copy-start | bytes 52
  1.8 13.6 %collective-permute-start = (f32[55,8,128]{2,1,0:T(8,128)S(1)}, f32[55,8,128]{2,1,0:T(8,128)S(1)}, u32[]{:S(2)}, u32[]{:S(2)}) collective-permute-start(f32[55,8,128]{2,1,0:T(8,128)S(1)} %get-tuple-element.36), channel_id=1, source_target_pairs={{0,1},{2,3},{4,5},{6,7},{8,9},{10,11},{12,13},{14,15},{16,17},{18,... | collective-permute-start | bytes 675848 | tf_op jit(solution)/shard_map/ppermute | solution.py:527
  3.2 13.8 %collective-permute-start.2 = (f32[55,8,128]{2,1,0:T(8,128)S(1)}, f32[55,8,128]{2,1,0:T(8,128)S(1)}, u32[]{:S(2)}, u32[]{:S(2)}) collective-permute-start(f32[55,8,128]{2,1,0:T(8,128)S(1)} %get-tuple-element.37), channel_id=1, source_target_pairs={{1,2},{3,4},{5,6},{7,8},{9,10},{11,12},{13,14},{15,16},{17,18},{19... | collective-permute-start | bytes 675848 | tf_op jit(solution)/shard_map/ppermute | solution.py:533
  7.5 1.0 %copy-start.2 = (f32[1,16,8,1024]{3,2,1,0:T(8,128)S(1)}, f32[1,16,8,1024]{3,2,1,0:T(8,128)}, u32[]{:S(2)}) copy-start(f32[1,16,8,1024]{3,2,1,0:T(8,128)} %param.14) | copy-start | bytes 1572868
  11.0 23.8 %copy-start.3 = (f32[1,16,8,1024]{3,2,1,0:T(8,128)S(1)}, f32[1,16,8,1024]{3,2,1,0:T(8,128)}, u32[]{:S(2)}) copy-start(f32[1,16,8,1024]{3,2,1,0:T(8,128)} %param.14) | copy-start | bytes 1572868
  11.0 23.8 %copy-start.5 = (f32[1,16,8,1024]{3,2,1,0:T(8,128)S(1)}, f32[1,16,8,1024]{3,2,1,0:T(8,128)}, u32[]{:S(2)}) copy-start(f32[1,16,8,1024]{3,2,1,0:T(8,128)} %param.15) | copy-start | bytes 1572868
  11.0 23.8 %copy-start.11 = (f32[1,4,8,128]{3,2,1,0:T(8,128)S(1)}, f32[1,4,8,128]{3,2,1,0:T(8,128)}, u32[]{:S(2)}) copy-start(f32[1,4,8,128]{3,2,1,0:T(8,128)} %param.18) | copy-start | bytes 49156
  11.3 16.2 %collective-permute-start.6 = (f32[173,8,128]{2,1,0:T(8,128)S(1)}, f32[173,8,128]{2,1,0:T(8,128)S(1)}, u32[]{:S(2)}, u32[]{:S(2)}) collective-permute-start(f32[173,8,128]{2,1,0:T(8,128)S(1)} %get-tuple-element.44), channel_id=1, source_target_pairs={{0,1},{2,3},{4,5},{6,7},{8,9},{10,11},{12,13},{14,15},{16,17},{18,... | collective-permute-start | bytes 2125832 | tf_op jit(solution)/shard_map/ppermute | solution.py:527
  11.4 20.9 %collective-permute-start.7 = (f32[173,8,128]{2,1,0:T(8,128)S(1)}, f32[173,8,128]{2,1,0:T(8,128)S(1)}, u32[]{:S(2)}, u32[]{:S(2)}) collective-permute-start(f32[173,8,128]{2,1,0:T(8,128)S(1)} %get-tuple-element.45), channel_id=1, source_target_pairs={{1,2},{3,4},{5,6},{7,8},{9,10},{11,12},{13,14},{15,16},{17,18},{19... | collective-permute-start | bytes 2125832 | tf_op jit(solution)/shard_map/ppermute | solution.py:533
  15.4 2.7 %collective-permute-start.1 = (f32[55,8,128]{2,1,0:T(8,128)S(1)}, f32[55,8,128]{2,1,0:T(8,128)S(1)}, u32[]{:S(2)}, u32[]{:S(2)}) collective-permute-start(f32[55,8,128]{2,1,0:T(8,128)S(1)} %collective-permute-done.s_even), channel_id=1, source_target_pairs={{0,64},{64,0},{128,192},{192,128},{1,65},{65,1},{129,193},{193,129... | collective-permute-start | bytes 675848 | tf_op jit(solution)/shard_map/ppermute | solution.py:537
  17.0 1.5 %collective-permute-start.3 = (f32[55,8,128]{2,1,0:T(8,128)S(1)}, f32[55,8,128]{2,1,0:T(8,128)S(1)}, u32[]{:S(2)}, u32[]{:S(2)}) collective-permute-start(f32[55,8,128]{2,1,0:T(8,128)S(1)} %collective-permute-done.2.s_odd), channel_id=1, source_target_pairs={{0,64},{64,0},{128,192},{192,128},{1,65},{65,1},{129,193},{193,129... | collective-permute-start | bytes 675848 | tf_op jit(solution)/shard_map/ppermute | solution.py:537
  20.8 21.3 %collective-permute-start.4 = (f32[144,8,128]{2,1,0:T(8,128)S(1)}, f32[144,8,128]{2,1,0:T(8,128)S(1)}, u32[]{:S(2)}, u32[]{:S(2)}) collective-permute-start(f32[144,8,128]{2,1,0:T(8,128)S(1)} %get-tuple-element.40), channel_id=1, source_target_pairs={{0,1},{2,3},{4,5},{6,7},{8,9},{10,11},{12,13},{14,15},{16,17},{18,... | collective-permute-start | bytes 1769480 | tf_op jit(solution)/shard_map/ppermute | solution.py:527
  21.1 23.8 %collective-permute-start.5 = (f32[144,8,128]{2,1,0:T(8,128)S(1)}, f32[144,8,128]{2,1,0:T(8,128)S(1)}, u32[]{:S(2)}, u32[]{:S(2)}) collective-permute-start(f32[144,8,128]{2,1,0:T(8,128)S(1)} %get-tuple-element.41), channel_id=1, source_target_pairs={{1,2},{3,4},{5,6},{7,8},{9,10},{11,12},{13,14},{15,16},{17,18},{19... | collective-permute-start | bytes 1769480 | tf_op jit(solution)/shard_map/ppermute | solution.py:533
  26.4 18.5 %copy-start.7 = (f32[1,16,8,1024]{3,2,1,0:T(8,128)S(1)}, f32[1,16,8,1024]{3,2,1,0:T(8,128)}, u32[]{:S(2)}) copy-start(f32[1,16,8,1024]{3,2,1,0:T(8,128)} %param.17) | copy-start | bytes 1572868
  26.4 18.5 %copy-start.9 = (f32[1,16,8,1024]{3,2,1,0:T(8,128)S(1)}, f32[1,16,8,1024]{3,2,1,0:T(8,128)}, u32[]{:S(2)}) copy-start(f32[1,16,8,1024]{3,2,1,0:T(8,128)} %param.16) | copy-start | bytes 1572868
  32.2 24.2 %collective-permute-start.8 = (f32[2,4,64,128]{3,2,1,0:T(8,128)S(1)}, f32[2,4,64,128]{3,2,1,0:T(8,128)S(1)}, u32[]{:S(2)}, u32[]{:S(2)}) collective-permute-start(f32[2,4,64,128]{3,2,1,0:T(8,128)S(1)} %pad_maximum_fusion), channel_id=1, source_target_pairs={{0,128},{128,0},{64,192},{192,64},{1,129},{129,1},{65,193},{193,65... | collective-permute-start | bytes 786440 | tf_op jit(solution)/shard_map/ppermute | solution.py:541
  44.9 22.4 %copy-start.16 = (f32[4,8,1024]{2,1,0:T(8,128)S(1)}, f32[4,8,1024]{2,1,0:T(8,128)}, u32[]{:S(2)}) copy-start(f32[4,8,1024]{2,1,0:T(8,128)} %param.13) | copy-start | bytes 393220
  44.9 22.4 %copy-start.17 = (f32[4,8,1024]{2,1,0:T(8,128)S(1)}, f32[4,8,1024]{2,1,0:T(8,128)}, u32[]{:S(2)}) copy-start(f32[4,8,1024]{2,1,0:T(8,128)} %param.12) | copy-start | bytes 393220
  56.5 1.7 %collective-permute-start.9 = (f32[2,4,64,128]{3,2,1,0:T(8,128)S(1)}, f32[2,4,64,128]{3,2,1,0:T(8,128)S(1)}, u32[]{:S(2)}, u32[]{:S(2)}) collective-permute-start(f32[2,4,64,128]{3,2,1,0:T(8,128)S(1)} %get-tuple-element.68), channel_id=1, source_target_pairs={{0,64},{64,0},{128,192},{192,128},{1,65},{65,1},{129,193},{193,129... | collective-permute-start | bytes 786440 | tf_op jit(solution)/shard_map/ppermute | solution.py:537
  58.1 9.1 %collective-permute-start.10 = (f32[2,4,64,128]{3,2,1,0:T(8,128)S(1)}, f32[2,4,64,128]{3,2,1,0:T(8,128)S(1)}, u32[]{:S(2)}, u32[]{:S(2)}) collective-permute-start(f32[2,4,64,128]{3,2,1,0:T(8,128)S(1)} %add.24), channel_id=1, source_target_pairs={{0,128},{128,0},{64,192},{192,64},{1,129},{129,1},{65,193},{193,65... | collective-permute-start | bytes 786440 | tf_op jit(solution)/shard_map/ppermute | solution.py:541
  67.5 2.5 %collective-permute-start.11 = (f32[2,4,64,128]{3,2,1,0:T(8,128)S(1)}, f32[2,4,64,128]{3,2,1,0:T(8,128)S(1)}, u32[]{:S(2)}, u32[]{:S(2)}) collective-permute-start(f32[2,4,64,128]{3,2,1,0:T(8,128)S(1)} %get-tuple-element.69.mine), channel_id=1, source_target_pairs={{0,64},{64,0},{128,192},{192,128},{1,65},{65,1},{129,193},{193,129... | collective-permute-start | bytes 786440 | tf_op jit(solution)/shard_map/ppermute | solution.py:537
  (6 other events, 5.6 us)

commit v4 on v3

--- a/solution.py
+++ b/solution.py
@@ -28,10 +28,13 @@
 SHORT = (ROWS + 2 * REACH, NZ, XT, LANES)
 SURF_ROWS = ROWS + 2 * EDGE
 PART = NZ // 2
-TILE_S = REACH * PART + CONE * REACH
-TILE_U = (2 * REACH - 1) * (NZ + CONE) + 2
+TIP = CONE * (CONE + 1) // 2
+TILE_S = REACH * PART + TIP
+TILE_U = (2 * REACH - 1) * NZ + 2 * TIP + 2
+TILE_A = TILE_S + TILE_U
 TILE_L = (2 * REACH - 1) * NZ
 HALF = 0.5 * TIME_STEP_SQ
+PACK_VMEM = 56 << 20
 
 f32 = jnp.float32
 VMEM = pl.BlockSpec(memory_space=pltpu.VMEM)
@@ -108,14 +111,25 @@
 
 def pack_cone(ref, width, low, high, at):
     for k in range(CONE):
-        for z in range(width):
-            low[at + z] = row_of(ref, z, width + k)
-            high[at + z] = row_of(ref, z, ROWS - width - CONE + k)
-        at += width
+        for z in range(CONE - k):
+            low[at] = row_of(ref, z, width + k)
+            high[at] = row_of(ref, z, ROWS - 1 - width - k)
+            at += 1
     return at
 
 
-def pack_stiffness_kernel(s, *pair):
+def fetch(sources, places, sems):
+    copies = [pltpu.make_async_copy(a, b, sems.at[i]) for i, (a, b) in enumerate(zip(sources, places, strict=True))]
+    for copy in copies:
+        copy.start()
+    for copy in copies:
+        copy.wait()
+
+
+def pack_first_kernel(
+    s_far, u1_far, u0_far, receivers_far, observed_far, even, odd, s, u1, u0, receivers, observed, sems
+):
+    fetch((s_far, u1_far, u0_far, receivers_far, observed_far), (s, u1, u0, receivers, observed), sems)
     base = core_index() * PART
 
     def work(low, high):
@@ -126,14 +140,8 @@
             return carry
 
         lax.fori_loop(0, PART, plane, 0)
-        pack_cone(s, REACH, low, high, REACH * PART)
-
-    by_parity(pair, work)
-
-
-def pack_waves_kernel(u1, u0, receivers, observed, *pair):
-    def work(low, high):
-        at = pack_fields((u1, u0), (REACH, REACH - 1), low, high, 0)
+        at = pack_cone(s, REACH, low, high, REACH * PART)
+        at = pack_fields((u1, u0), (REACH, REACH - 1), low, high, at)
         at = pack_cone(u1, REACH, low, high, at)
         at = pack_cone(u0, REACH - 1, low, high, at)
         where = receivers[...].astype(f32)
@@ -147,11 +155,12 @@
             side[at] = both[:XT]
             side[at + 1] = both[XT:]
 
-    by_parity(pair, work)
-
-
-def pack_adjoint_kernel(l6, l7, *pair):
-    by_parity(pair, lambda low, high: pack_fields((l6, l7), (REACH, REACH - 1), low, high, 0))
+    by_parity((even, odd), work)
+
+
+def pack_adjoint_kernel(l6_far, l7_far, even, odd, l6, l7, sems):
+    fetch((l6_far, l7_far), (l6, l7), sems)
+    by_parity((even, odd), lambda low, high: pack_fields((l6, l7), (REACH, REACH - 1), low, high, 0))
 
 
 def pack(kernel, name, tiles, *arrays):
@@ -159,10 +168,11 @@
     return pl.pallas_call(
         kernel,
         out_shape=(shape, shape),
-        in_specs=[VMEM] * len(arrays),
+        in_specs=[pl.BlockSpec(memory_space=pl.ANY)] * len(arrays),
         out_specs=(VMEM, VMEM),
-        compiler_params=pltpu.CompilerParams(vmem_limit_bytes=6 << 20),
-        cost_estimate=pl.CostEstimate(flops=0, bytes_accessed=1 << 21, transcendentals=0),
+        scratch_shapes=[pltpu.VMEM(a.shape, a.dtype) for a in arrays] + [pltpu.SemaphoreType.DMA((len(arrays),))],
+        compiler_params=pltpu.CompilerParams(vmem_limit_bytes=PACK_VMEM),
+        cost_estimate=pl.CostEstimate(flops=0, bytes_accessed=1 << 16, transcendentals=0),
         name=name,
     )(*arrays)
 
@@ -184,40 +194,55 @@
 
 def fill_cone(ext, low, high, at, width):
     for k in range(CONE):
-        ext[OFF - width - CONE + k, :width] = low[at + k * width : at + (k + 1) * width]
-        ext[OFF + ROWS + width + k, :width] = high[at + k * width : at + (k + 1) * width]
-
-
-def coefficients(stiff, diag, cx, cy, cz, lo, hi, planes, lane, tile):
+        planes = CONE - k
+        ext[OFF - 1 - width - k, :planes] = low[at : at + planes]
+        ext[OFF + ROWS + width + k, :planes] = high[at : at + planes]
+        at += planes
+
+
+def coefficients(stiff, diag, cx, cy, cz, lane, tile):
     x_end = (lane == LANES - 1) & (tile == XT - 1)
     x_start = (lane == 0) & (tile == 0)
+    top, bottom = OFF - REACH, OFF + ROWS + REACH
+
+    def face_y(e, planes):
+        for z in range(planes):
+            cy[e, z] = HALF * (stiff[e, z] + stiff[e + 1, z])
+
+    def cells(e, planes):
+        below = None
+        following = HALF * stiff[e, 0]
+        for z in range(planes):
+            s = following
+            face = s + jnp.where(x_end, 0.0, x_next(s, lane))
+            total = face + (s + jnp.where(x_start, 0.0, x_prev(s, lane)))
+            if z < NZ - 1:
+                following = HALF * stiff[e, z + 1]
+                above = s + following
+            else:
+                above = s
+            total = total + above + (below if z > 0 else s) + cy[e, z] + cy[e - 1, z]
+            cx[e, z] = jnp.where(x_end, 0.0, face)
+            cz[e, z] = above
+            diag[e, z] = 2.0 - total
+            below = above
 
     def faces(first, count):
-        for e in (first + r for r in range(count)):
-            for z in range(planes):
-                cy[e, z] = HALF * (stiff[e, z] + stiff[e + 1, z])
+        for r in range(count):
+            face_y(first + r, NZ)
 
     def rows(first, count):
-        for e in (first + r for r in range(count)):
-            below = None
-            following = HALF * stiff[e, 0]
-            for z in range(planes):
-                s = following
-                face = s + jnp.where(x_end, 0.0, x_next(s, lane))
-                total = face + (s + jnp.where(x_start, 0.0, x_prev(s, lane)))
-                if z < NZ - 1:
-                    following = HALF * stiff[e, z + 1]
-                    above = s + following
-                else:
-                    above = s
-                total = total + above + (below if z > 0 else s) + cy[e, z] + cy[e - 1, z]
-                cx[e, z] = jnp.where(x_end, 0.0, face)
-                cz[e, z] = above
-                diag[e, z] = 2.0 - total
-                below = above
-
-    in_blocks(lo - 1, hi, 4, faces)
-    in_blocks(lo, hi, 4, rows)
+        for r in range(count):
+            cells(first + r, NZ)
+
+    in_blocks(top, bottom - 1, 4, faces)
+    for k in range(CONE):
+        face_y(top - 1 - k, CONE - k)
+        face_y(bottom - 1 + k, CONE - k)
+    in_blocks(top + 1, bottom - 1, 4, rows)
+    for k in range(CONE):
+        cells(top - k, CONE - k)
+        cells(bottom - 1 + k, CONE - k)
 
 
 def leap(now, before, after, base, diag, cx, cy, cz, outer, lane, slope, inject=None):
@@ -240,12 +265,8 @@
             if slope_row is not None:
                 slope[slope_row, z] = following - u
 
-    def own(i, carry):
-        for r in range(4):
-            cells(OFF + 4 * i + r, NZ, 4 * i + r)
-        return carry
-
-    lax.fori_loop(0, ROWS // 4, own, 0)
+    for r in range(ROWS):
+        cells(OFF + r, NZ, r)
     for e, planes in outer:
         cells(e, planes, None)
 
@@ -254,8 +275,9 @@
     whole = STEPS - k
     rows = [(OFF - whole + j, NZ) for j in range(whole)] + [(OFF + ROWS + j, NZ) for j in range(whole)]
     if cone:
-        rows += [(OFF - whole - CONE + j, whole) for j in range(CONE)]
-        rows += [(OFF + ROWS + whole + j, whole) for j in range(CONE)]
+        for j in range(CONE):
+            planes = min(CONE - j, whole)
+            rows += [(OFF - 1 - whole - j, planes), (OFF + ROWS + whole + j, planes)]
     return rows
 
 
@@ -307,7 +329,7 @@
 
 
 def forward_kernel(
-    source_pos, source_wave, u0, u1, s, s_even, s_odd, s_even_other, s_odd_other, u_even, u_odd, receivers, observed,
+    source_pos, source_wave, u0, u1, s, even, odd, even_other, odd_other, receivers, observed,
     w1, w2, w3, w4, w5, d1, d2, d3, d4, d5, diag, cx, cy, cz, surf,
     stiff, before, edge,
 ):
@@ -318,33 +340,26 @@
         fill(ext, own, OFF)
     core = core_index()
 
-    def stiffness_halos(low, high):
+    def halos(low, high):
         for part, base in ((0, core * PART), (1, (1 - core) * PART)):
             for k in range(REACH):
                 stiff[OFF - REACH + k, pl.ds(base, PART)] = low[part][k * PART : (k + 1) * PART]
                 stiff[OFF + ROWS + k, pl.ds(base, PART)] = high[part][k * PART : (k + 1) * PART]
-        fill_cone(stiff, low[0], high[0], REACH * PART, REACH)
-
-    def wave_halos(low, high):
-        fill_halo(w1, OFF, low, high, 0, REACH)
-        fill_halo(before, OFF, low, high, REACH * NZ, REACH - 1)
-        at = (2 * REACH - 1) * NZ
+        low, high = low[0], high[0]
+        fill_cone(stiff, low, high, REACH * PART, REACH)
+        at = TILE_S
+        fill_halo(w1, OFF, low, high, at, REACH)
+        at += REACH * NZ
+        fill_halo(before, OFF, low, high, at, REACH - 1)
+        at += (REACH - 1) * NZ
         fill_cone(w1, low, high, at, REACH)
-        fill_cone(before, low, high, at + REACH * CONE, REACH - 1)
+        fill_cone(before, low, high, at + TIP, REACH - 1)
         for i, ref in enumerate((low, high)):
-            edge[2 * i] = ref[TILE_U - 2]
-            edge[2 * i + 1] = ref[TILE_U - 1]
-
-    by_parity(((s_even, s_even_other), (s_odd, s_odd_other)), stiffness_halos)
-    by_parity((u_even, u_odd), wave_halos)
-    top, bottom = OFF - REACH, OFF + ROWS + REACH
-    for lo, hi, planes in (
-        (top + 1, bottom - 1, NZ),
-        (top + 1 - CONE, top + 1, STEPS),
-        (bottom - 1, bottom - 1 + CONE, STEPS),
-    ):
-        coefficients(stiff, diag, cx, cy, cz, lo, hi, planes, lane, tile)
-
+            edge[2 * i] = ref[TILE_A - 2]
+            edge[2 * i + 1] = ref[TILE_A - 1]
+
+    by_parity(((even, even_other), (odd, odd_other)), halos)
+    coefficients(stiff, diag, cx, cy, cz, lane, tile)
     gy = lax.axis_index("gy")
 
     @pl.when(gy == 0)
@@ -561,40 +576,35 @@
     l6, l7 = native(adjoint_now[0]), native(adjoint_next[0])
     first, second = native(first_moment), native(second_moment)
 
-    s_even, s_odd = pack(pack_stiffness_kernel, "pack_stiffness", TILE_S, s)
-    s_even, s_odd = swap_even(s_even), swap_odd(s_odd)
-    u_even, u_odd = pack(pack_waves_kernel, "pack_waves", TILE_U, u1, u0, receiver_x[0], observed[0])
-    u_even, u_odd = swap_even(u_even), swap_odd(u_odd)
-    s_even_other, s_odd_other = swap_core(s_even), swap_core(s_odd)
-    l6_after, l7_after, s_even_other, s_odd_other = lax.optimization_barrier((l6, l7, s_even_other, s_odd_other))
-    l_even, l_odd = pack(pack_adjoint_kernel, "pack_adjoint", TILE_L, l6_after, l7_after)
+    a_even, a_odd = pack(pack_first_kernel, "pack_first", TILE_A, s, u1, u0, receiver_x[0], observed[0])
+    l_even, l_odd = pack(pack_adjoint_kernel, "pack_adjoint", TILE_L, l6, l7)
+    a_even, a_odd = swap_even(a_even), swap_odd(a_odd)
+    l_even, l_odd, a_even = lax.optimization_barrier((l_even, l_odd, a_even))
     l_even, l_odd = swap_even(l_even), swap_odd(l_odd)
+    even_other, odd_other = swap_core(a_even[:TILE_S]), swap_core(a_odd[:TILE_S])
+    *fields, surf = forward(
+        source_pos, source_wave, u0, u1, s, a_even, a_odd, even_other, odd_other, receiver_x[0], observed[0]
+    )
     moments = jnp.stack([first, second])
-    u_even, u_odd, moments = lax.optimization_barrier((u_even, u_odd, moments))
+    l_even, moments, surf = lax.optimization_barrier((l_even, moments, surf))
     moments = swap_far(moments)
-    fields = forward(
-        source_pos, source_wave, u0, u1, s, s_even, s_odd, s_even_other, s_odd_other, u_even, u_odd,
-        receiver_x[0], observed[0],
-    )
-    keep, send = adjoint(l6, l7, l_even, l_odd, *fields)
+    keep, send = adjoint(l6, l7, l_even, l_odd, *fields, surf)
     keep, send, moments = lax.optimization_barrier((keep, send, moments))
     chip_sum = keep + swap_core(send)
     share = chip_sum + swap_far(chip_sum)
-
-    is_far = (jnp.arange(2) == far)[:, None, None, None]
-    first_two = jnp.where(is_far, first[None], moments[0][None])
-    second_two = jnp.where(is_far, second[None], moments[1][None])
-    stiff_two = jnp.where(core == 0, s.reshape(2, 2, 4, XT * ROWS, LANES)[:, 0], s.reshape(2, 2, 4, XT * ROWS, LANES)[:, 1])
+    first_two = jnp.where(far == 0, jnp.stack([first, moments[0]]), jnp.stack([moments[0], first]))
+    second_two = jnp.where(far == 0, jnp.stack([second, moments[1]]), jnp.stack([moments[1], second]))
+    halves = s.reshape(2, 2, 4, XT * ROWS, LANES)
+    stiff_two = jnp.where(core == 0, halves[:, 0], halves[:, 1])
     first_new = BETA_ONE * first_two + (1.0 - BETA_ONE) * share
     second_new = BETA_TWO * second_two + (1.0 - BETA_TWO) * share * share
     updated = stiff_two - LEARN_RATE * (first_new / (1.0 - BETA_ONE**ADAM_TICKS)) / (
         jnp.sqrt(second_new / (1.0 - BETA_TWO**ADAM_TICKS)) + ADAM_EPS
     )
-    other = swap_core(updated)
-    stiffness_new = finish(updated, other)
-    first_out = jnp.where(far == 0, first_new[0], first_new[1])
-    second_out = jnp.where(far == 0, second_new[0], second_new[1])
-    return (from_native(stiffness_new), from_native(first_out), from_native(second_out))
+    stiffness_new = finish(updated, swap_core(updated))
+    first_new = jnp.where(far == 0, first_new[0], first_new[1])
+    second_new = jnp.where(far == 0, second_new[0], second_new[1])
+    return (from_native(stiffness_new), from_native(first_new), from_native(second_new))
 
 
 def solution(mesh):

time: 71.3 us -> 66.6 us (0.934)
  local copies, waits for them, and re-layouts: 6.66 us -> 0.1 us
  waiting for transfers between devices: 25.8 us -> 29.8 us
  starting transfers between devices: 20.6 us -> 18.4 us
  Pallas kernels: 14.8 us -> 16.3 us
  other arithmetic: 2.02 us -> 1 us
    ppermute x3 -> x2, waiting for transfers between devices: 1.1 us -> 12.4 us  [swap_even(): return lax.ppermute(block, 'gy', pairs + [(j, i) for i, j in pairs])]
    ppermute x3 -> x2, waiting for transfers between devices: 7.59 us -> 0.69 us  [swap_odd(): return lax.ppermute(block, 'gy', pairs + [(j, i) for i, j in pairs])]
    unnamed x36 -> x22, local copies, waits for them, and re-layouts: 6.64 us -> 0.05 us
    ppermute x3 -> x2, starting transfers between devices: 12.5 us -> 8.55 us  [swap_odd(): return lax.ppermute(block, 'gy', pairs + [(j, i) for i, j in pairs])]
    pallas_call x3 -> x2, Pallas kernels: 0.64 us -> 3.31 us  [pack(): pl.pallas_call(kernel, out_shape=(shape, shape), in_specs=[pl.BlockSpec(m...]
    another operation x1, other arithmetic: 0.99 us -> 0.02 us  [body(): moments = jnp.stack([first, second])]
    ppermute x3 -> x2, starting transfers between devices: 1.8 us -> 2.67 us  [swap_even(): return lax.ppermute(block, 'gy', pairs + [(j, i) for i, j in pairs])]
  transfers between devices with their start and end apart: 12 -> 10, of which waited for: 9 -> 8; matrix products, arithmetic and copies ran while one was open for 2% -> 1% of each run, Pallas kernels for 20% -> 20%
where the time goes in v4:
time: 66.6 us; the launch traced here: 66.4 us
  waiting for transfers between devices  29.8 us (45%)
  starting transfers between devices  18.4 us (28%)
  Pallas kernels  16.3 us (24%)
  other arithmetic  1 us (2%)
  between operations  0.85 us (1%)
    ppermute x2, waiting for transfers between devices, swap_far(): return lax.ppermute(block, 'shot', [(0, 2), (2, 0), (1, 3), (3, 1)])  13.7 us
    ppermute x2, waiting for transfers between devices, swap_even(): return lax.ppermute(block, 'gy', pairs + [(j, i) for i, j in pairs])  12.4 us
    ppermute x2, starting transfers between devices, swap_odd(): return lax.ppermute(block, 'gy', pairs + [(j, i) for i, j in pairs])  8.55 us
    pallas_call x1, Pallas kernels, forward(): pl.pallas_call(forward_kernel, out_shape=outs, in_specs=[SMEM] * 2 + [VME...  6.55 us
    pallas_call x1, Pallas kernels, adjoint(): pl.pallas_call(adjoint_kernel, out_shape=(part, part), in_specs=[VMEM] *...  5.58 us
    ppermute x4, starting transfers between devices, swap_core(): return lax.ppermute(block, 'shot', [(0, 1), (1, 0), (2, 3), (3, 2)])  4.05 us
    pallas_call x2, Pallas kernels, pack(): pl.pallas_call(kernel, out_shape=(shape, shape), in_specs=[pl.BlockSpec(m...  3.31 us
    ppermute x2, starting transfers between devices, swap_far(): return lax.ppermute(block, 'shot', [(0, 2), (2, 0), (1, 3), (3, 1)])  3.14 us
  transfers between devices with their start and end apart: 10, of which 8 were waited for; matrix products, arithmetic and copies ran while one was open for 1% of the time, Pallas kernels for 20%

profile of v4, /device:TPU:97, one launch (start us, length us, event | category | flops | bytes accessed | tf_op | source)
XLA Modules:
  0.0 66.4 jit_solution(5461435407021681213)
XLA Ops:
  0.7 1.9 %pack_first.1 = (f32[204,8,128]{2,1,0:T(8,128)S(1)}, f32[204,8,128]{2,1,0:T(8,128)S(1)}) custom-call(f32[16,64,128]{2,1,0:T(8,128)} %bitcast.72, f32[16,64,128]{2,1,0:T(8,128)} %bitcast.77, f32[16,64,128]{2,1,0:T(8,128)} %bitcast.75, s32[8,128]{1,0:T(8,128)} %bitcast.85, f32[4,8,128]{2,1,0:T(8,128)} %bitcast.83), custom_call_target="tpu_custom_call" | custom-call | bytes 65536 | tf_op jit(solution)/shard_map/pack_first/pallas_call | solution.py:168
  2.6 1.4 %collective-permute-start = (f32[204,8,128]{2,1,0:T(8,128)S(1)}, f32[204,8,128]{2,1,0:T(8,128)S(1)}, u32[]{:S(2)}, u32[]{:S(2)}) collective-permute-start(f32[204,8,128]{2,1,0:T(8,128)S(1)} %get-tuple-element.35), channel_id=1, source_target_pairs={{0,1},{2,3},{4,5},{6,7},{8,9},{10,11},{12,13},{14,15},{16,17},{18,... | collective-permute-start | bytes 2506760 | tf_op jit(solution)/shard_map/ppermute | solution.py:542
  4.0 4.3 %collective-permute-start.2 = (f32[204,8,128]{2,1,0:T(8,128)S(1)}, f32[204,8,128]{2,1,0:T(8,128)S(1)}, u32[]{:S(2)}, u32[]{:S(2)}) collective-permute-start(f32[204,8,128]{2,1,0:T(8,128)S(1)} %get-tuple-element.38), channel_id=1, source_target_pairs={{1,2},{3,4},{5,6},{7,8},{9,10},{11,12},{13,14},{15,16},{17,18},{19... | collective-permute-start | bytes 2506760 | tf_op jit(solution)/shard_map/ppermute | solution.py:548
  8.3 1.4 %pack_adjoint.1 = (f32[144,8,128]{2,1,0:T(8,128)S(1)}, f32[144,8,128]{2,1,0:T(8,128)S(1)}) custom-call(f32[16,64,128]{2,1,0:T(8,128)} %bitcast.79, f32[16,64,128]{2,1,0:T(8,128)} %bitcast.81), custom_call_target="tpu_custom_call" | custom-call | bytes 65536 | tf_op jit(solution)/shard_map/pack_adjoint/pallas_call | solution.py:168
  9.7 12.4 %collective-permute-done.even = f32[204,8,128]{2,1,0:T(8,128)S(1)} collective-permute-done((f32[204,8,128]{2,1,0:T(8,128)S(1)}, f32[204,8,128]{2,1,0:T(8,128)S(1)}, u32[]{:S(2)}, u32[]{:S(2)}) %collective-permute-start) | collective-permute-done | bytes 835616 | tf_op jit(solution)/shard_map/ppermute | solution.py:542
  22.1 1.3 %collective-permute-start.1 = (f32[144,8,128]{2,1,0:T(8,128)S(1)}, f32[144,8,128]{2,1,0:T(8,128)S(1)}, u32[]{:S(2)}, u32[]{:S(2)}) collective-permute-start(f32[144,8,128]{2,1,0:T(8,128)S(1)} %get-tuple-element.36), channel_id=1, source_target_pairs={{0,1},{2,3},{4,5},{6,7},{8,9},{10,11},{12,13},{14,15},{16,17},{18,... | collective-permute-start | bytes 1769480 | tf_op jit(solution)/shard_map/ppermute | solution.py:542
  23.4 4.3 %collective-permute-start.5 = (f32[144,8,128]{2,1,0:T(8,128)S(1)}, f32[144,8,128]{2,1,0:T(8,128)S(1)}, u32[]{:S(2)}, u32[]{:S(2)}) collective-permute-start(f32[144,8,128]{2,1,0:T(8,128)S(1)} %get-tuple-element.41), channel_id=1, source_target_pairs={{1,2},{3,4},{5,6},{7,8},{9,10},{11,12},{13,14},{15,16},{17,18},{19... | collective-permute-start | bytes 1769480 | tf_op jit(solution)/shard_map/ppermute | solution.py:548
  27.7 2.2 %collective-permute-start.3 = (f32[46,8,128]{2,1,0:T(8,128)S(1)}, f32[46,8,128]{2,1,0:T(8,128)S(1)}, u32[]{:S(2)}, u32[]{:S(2)}) collective-permute-start(f32[46,8,128]{2,1,0:T(8,128)S(1)} %slice.34), channel_id=1, source_target_pairs={{0,64},{64,0},{128,192},{192,128},{1,65},{65,1},{129,193},{193,129... | collective-permute-start | bytes 565256 | tf_op jit(solution)/shard_map/ppermute | solution.py:552
  30.1 0.9 %collective-permute-done.3.even_other = f32[46,8,128]{2,1,0:T(8,128)S(1)} collective-permute-done((f32[46,8,128]{2,1,0:T(8,128)S(1)}, f32[46,8,128]{2,1,0:T(8,128)S(1)}, u32[]{:S(2)}, u32[]{:S(2)}) %collective-permute-start.3) | collective-permute-done | bytes 188448 | tf_op jit(solution)/shard_map/ppermute | solution.py:552
  31.0 0.5 collective-permute-done.4.odd_other
  31.5 6.6 %forward.1 = (f32[24,16,8,128]{3,2,1,0:T(8,128)S(1)}, f32[24,16,8,128]{3,2,1,0:T(8,128)S(1)}, f32[24,16,8,128]{3,2,1,0:T(8,128)S(1)}, f32[24,16,8,128]{3,2,1,0:T...) custom-call(s32[1,3]{1,0:T(1,128)S(1)} %copy-done.7, ...), custom_call_target="tpu_custom_call" | custom-call | flops 33554432 | bytes 16777216 | tf_op jit(solution)/shard_map/forward/pallas_call | solution.py:405
  38.1 2.5 %collective-permute-start.6 = (f32[2,4,64,128]{3,2,1,0:T(8,128)S(1)}, f32[2,4,64,128]{3,2,1,0:T(8,128)S(1)}, u32[]{:S(2)}, u32[]{:S(2)}) collective-permute-start(f32[2,4,64,128]{3,2,1,0:T(8,128)S(1)} %pad_maximum_fusion.1), channel_id=1, source_target_pairs={{0,128},{128,0},{64,192},{192,64},{1,129},{129,1},{65,193},{193,65... | collective-permute-start | bytes 786440 | tf_op jit(solution)/shard_map/ppermute | solution.py:556
  40.6 0.7 %collective-permute-done.5.odd = f32[144,8,128]{2,1,0:T(8,128)S(1)} collective-permute-done((f32[144,8,128]{2,1,0:T(8,128)S(1)}, f32[144,8,128]{2,1,0:T(8,128)S(1)}, u32[]{:S(2)}, u32[]{:S(2)}) %collective-permute-start.5) | collective-permute-done | bytes 589856 | tf_op jit(solution)/shard_map/ppermute | solution.py:548
  41.3 5.6 %adjoint.1 = (f32[2,4,64,128]{3,2,1,0:T(8,128)S(1)}, f32[2,4,64,128]{3,2,1,0:T(8,128)S(1)}) custom-call(f32[16,64,128]{2,1,0:T(8,128)S(1)} %bitcast.80, f32[16,64,128]{2,1,0:T(8,128)S(1)} %bitcast.82, f32[144,8,128]{2,1,0:T(8,128)S(1)} %collective-permute-done.1.even, f32[144,8,128]{2,1,0:T(8,128)S(1)} %collective-permute-done.5.odd, ...), custom_call_target="tpu_custom_call" | custom-call | flops 33554432 | bytes 16777216 | tf_op jit(solution)/shard_map/adjoint/pallas_call | solution.py:497
  46.9 5.2 %collective-permute-done.6 = f32[2,4,64,128]{3,2,1,0:T(8,128)S(1)} collective-permute-done((f32[2,4,64,128]{3,2,1,0:T(8,128)S(1)}, f32[2,4,64,128]{3,2,1,0:T(8,128)S(1)}, u32[]{:S(2)}, u32[]{:S(2)}) %collective-permute-start.6) | collective-permute-done | bytes 262176 | tf_op jit(solution)/shard_map/ppermute | solution.py:556
  52.1 0.5 collective-permute-start.7
  52.6 1.2 %collective-permute-done.7 = f32[2,4,64,128]{3,2,1,0:T(8,128)S(1)} collective-permute-done((f32[2,4,64,128]{3,2,1,0:T(8,128)S(1)}, f32[2,4,64,128]{3,2,1,0:T(8,128)S(1)}, u32[]{:S(2)}, u32[]{:S(2)}) %collective-permute-start.7) | collective-permute-done | bytes 262176 | tf_op jit(solution)/shard_map/ppermute | solution.py:552
  53.8 0.6 collective-permute-start.8
  54.4 8.5 %collective-permute-done.8 = f32[2,4,64,128]{3,2,1,0:T(8,128)S(1)} collective-permute-done((f32[2,4,64,128]{3,2,1,0:T(8,128)S(1)}, f32[2,4,64,128]{3,2,1,0:T(8,128)S(1)}, u32[]{:S(2)}, u32[]{:S(2)}) %collective-permute-start.8) | collective-permute-done | bytes 262176 | tf_op jit(solution)/shard_map/ppermute | solution.py:556
  62.9 0.2 fusion.8
  63.1 1.3 %collective-permute-start.9 = (f32[2,4,64,128]{3,2,1,0:T(8,128)S(1)}, f32[2,4,64,128]{3,2,1,0:T(8,128)S(1)}, u32[]{:S(2)}, u32[]{:S(2)}) collective-permute-start(f32[2,4,64,128]{3,2,1,0:T(8,128)S(1)} %get-tuple-element.63.mine), channel_id=1, source_target_pairs={{0,64},{64,0},{128,192},{192,128},{1,65},{65,1},{129,193},{193,129... | collective-permute-start | bytes 786440 | tf_op jit(solution)/shard_map/ppermute | solution.py:552
  64.4 0.7 %fusion.9 = (f32[4,8,1024]{2,1,0:T(8,128)}, f32[4,8,1024]{2,1,0:T(8,128)}) fusion(f32[2,4,64,128]{3,2,1,0:T(8,128)S(1)} %get-tuple-element.65, pred[]{:T(512)S(6)} %eq.12, f32[2,4,64,128]{3,2,1,0:T(8,128)S(1)} %get-tuple-element.64), kind=kLoop, calls=%fused_computation.16 | loop fusion | flops 65536 | bytes 786433 | tf_op jit(solution)/shard_map/reshape | solution.py:51
  65.2 0.4 collective-permute-done.9.other
  65.6 0.8 %finish.1 = f32[16,64,128]{2,1,0:T(8,128)} custom-call(f32[2,4,64,128]{3,2,1,0:T(8,128)S(1)} %get-tuple-element.63.mine, f32[2,4,64,128]{3,2,1,0:T(8,128)S(1)} %collective-permute-done.9.other), custom_call_target="tpu_custom_call" | custom-call | tf_op jit(solution)/shard_map/finish/pallas_call | solution.py:528
  (30 shorter events, 0.3 us)
Async XLA Ops:
  0.6 29.4 %copy-start.9 = (f32[4,8,1024]{2,1,0:T(8,128)S(1)}, f32[4,8,1024]{2,1,0:T(8,128)}, u32[]{:S(2)}) copy-start(f32[4,8,1024]{2,1,0:T(8,128)} %param.12) | copy-start | bytes 393220
  0.6 29.4 %copy-start.10 = (f32[4,8,1024]{2,1,0:T(8,128)S(1)}, f32[4,8,1024]{2,1,0:T(8,128)}, u32[]{:S(2)}) copy-start(f32[4,8,1024]{2,1,0:T(8,128)} %param.13) | copy-start | bytes 393220
  0.7 30.8 %copy-start = (f32[16,8,1024]{2,1,0:T(8,128)S(1)}, f32[16,8,1024]{2,1,0:T(8,128)}, u32[]{:S(2)}) copy-start(f32[16,8,1024]{2,1,0:T(8,128)} %param.11) | copy-start | bytes 1572868
  0.7 30.8 %copy-start.1 = (f32[1,16,8,1024]{3,2,1,0:T(8,128)S(1)}, f32[1,16,8,1024]{3,2,1,0:T(8,128)}, u32[]{:S(2)}) copy-start(f32[1,16,8,1024]{3,2,1,0:T(8,128)} %param.14) | copy-start | bytes 1572868
  0.7 30.8 %copy-start.2 = (f32[1,16,8,1024]{3,2,1,0:T(8,128)S(1)}, f32[1,16,8,1024]{3,2,1,0:T(8,128)}, u32[]{:S(2)}) copy-start(f32[1,16,8,1024]{3,2,1,0:T(8,128)} %param.15) | copy-start | bytes 1572868
  0.7 30.8 %copy-start.5 = (f32[1,4,8,128]{3,2,1,0:T(8,128)S(1)}, f32[1,4,8,128]{3,2,1,0:T(8,128)}, u32[]{:S(2)}) copy-start(f32[1,4,8,128]{3,2,1,0:T(8,128)} %param.18) | copy-start | bytes 49156
  0.7 30.8 %copy-start.6 = (s32[1,8,128]{2,1,0:T(8,128)S(1)}, s32[1,8,128]{2,1,0:T(8,128)}, u32[]{:S(2)}) copy-start(s32[1,8,128]{2,1,0:T(8,128)} %param.19) | copy-start | bytes 12292
  0.7 30.8 %copy-start.7 = (s32[1,3]{1,0:T(1,128)S(1)}, s32[1,3]{1,0:T(1,128)}, u32[]{:S(2)}) copy-start(s32[1,3]{1,0:T(1,128)} %source_pos.1) | copy-start | bytes 40
  0.7 30.8 %copy-start.8 = (f32[1,4]{1,0:T(1,128)S(1)}, f32[1,4]{1,0:T(1,128)}, u32[]{:S(2)}) copy-start(f32[1,4]{1,0:T(1,128)} %source_wave.1) | copy-start | bytes 52
  2.6 19.5 %collective-permute-start = (f32[204,8,128]{2,1,0:T(8,128)S(1)}, f32[204,8,128]{2,1,0:T(8,128)S(1)}, u32[]{:S(2)}, u32[]{:S(2)}) collective-permute-start(f32[204,8,128]{2,1,0:T(8,128)S(1)} %get-tuple-element.35), channel_id=1, source_target_pairs={{0,1},{2,3},{4,5},{6,7},{8,9},{10,11},{12,13},{14,15},{16,17},{18,... | collective-permute-start | bytes 2506760 | tf_op jit(solution)/shard_map/ppermute | solution.py:542
  4.0 26.0 %collective-permute-start.2 = (f32[204,8,128]{2,1,0:T(8,128)S(1)}, f32[204,8,128]{2,1,0:T(8,128)S(1)}, u32[]{:S(2)}, u32[]{:S(2)}) collective-permute-start(f32[204,8,128]{2,1,0:T(8,128)S(1)} %get-tuple-element.38), channel_id=1, source_target_pairs={{1,2},{3,4},{5,6},{7,8},{9,10},{11,12},{13,14},{15,16},{17,18},{19... | collective-permute-start | bytes 2506760 | tf_op jit(solution)/shard_map/ppermute | solution.py:548
  22.1 15.9 %collective-permute-start.1 = (f32[144,8,128]{2,1,0:T(8,128)S(1)}, f32[144,8,128]{2,1,0:T(8,128)S(1)}, u32[]{:S(2)}, u32[]{:S(2)}) collective-permute-start(f32[144,8,128]{2,1,0:T(8,128)S(1)} %get-tuple-element.36), channel_id=1, source_target_pairs={{0,1},{2,3},{4,5},{6,7},{8,9},{10,11},{12,13},{14,15},{16,17},{18,... | collective-permute-start | bytes 1769480 | tf_op jit(solution)/shard_map/ppermute | solution.py:542
  23.4 17.9 %collective-permute-start.5 = (f32[144,8,128]{2,1,0:T(8,128)S(1)}, f32[144,8,128]{2,1,0:T(8,128)S(1)}, u32[]{:S(2)}, u32[]{:S(2)}) collective-permute-start(f32[144,8,128]{2,1,0:T(8,128)S(1)} %get-tuple-element.41), channel_id=1, source_target_pairs={{1,2},{3,4},{5,6},{7,8},{9,10},{11,12},{13,14},{15,16},{17,18},{19... | collective-permute-start | bytes 1769480 | tf_op jit(solution)/shard_map/ppermute | solution.py:548
  27.7 3.3 %collective-permute-start.3 = (f32[46,8,128]{2,1,0:T(8,128)S(1)}, f32[46,8,128]{2,1,0:T(8,128)S(1)}, u32[]{:S(2)}, u32[]{:S(2)}) collective-permute-start(f32[46,8,128]{2,1,0:T(8,128)S(1)} %slice.34), channel_id=1, source_target_pairs={{0,64},{64,0},{128,192},{192,128},{1,65},{65,1},{129,193},{193,129... | collective-permute-start | bytes 565256 | tf_op jit(solution)/shard_map/ppermute | solution.py:552
  30.0 1.5 %collective-permute-start.4 = (f32[46,8,128]{2,1,0:T(8,128)S(1)}, f32[46,8,128]{2,1,0:T(8,128)S(1)}, u32[]{:S(2)}, u32[]{:S(2)}) collective-permute-start(f32[46,8,128]{2,1,0:T(8,128)S(1)} %slice.44), channel_id=1, source_target_pairs={{0,64},{64,0},{128,192},{192,128},{1,65},{65,1},{129,193},{193,129... | collective-permute-start | bytes 565256 | tf_op jit(solution)/shard_map/ppermute | solution.py:552
  30.1 11.2 %copy-start.3 = (f32[1,16,8,1024]{3,2,1,0:T(8,128)S(1)}, f32[1,16,8,1024]{3,2,1,0:T(8,128)}, u32[]{:S(2)}) copy-start(f32[1,16,8,1024]{3,2,1,0:T(8,128)} %param.17) | copy-start | bytes 1572868
  30.1 11.2 %copy-start.4 = (f32[1,16,8,1024]{3,2,1,0:T(8,128)S(1)}, f32[1,16,8,1024]{3,2,1,0:T(8,128)}, u32[]{:S(2)}) copy-start(f32[1,16,8,1024]{3,2,1,0:T(8,128)} %param.16) | copy-start | bytes 1572868
  38.1 14.1 %collective-permute-start.6 = (f32[2,4,64,128]{3,2,1,0:T(8,128)S(1)}, f32[2,4,64,128]{3,2,1,0:T(8,128)S(1)}, u32[]{:S(2)}, u32[]{:S(2)}) collective-permute-start(f32[2,4,64,128]{3,2,1,0:T(8,128)S(1)} %pad_maximum_fusion.1), channel_id=1, source_target_pairs={{0,128},{128,0},{64,192},{192,64},{1,129},{129,1},{65,193},{193,65... | collective-permute-start | bytes 786440 | tf_op jit(solution)/shard_map/ppermute | solution.py:556
  52.1 1.6 %collective-permute-start.7 = (f32[2,4,64,128]{3,2,1,0:T(8,128)S(1)}, f32[2,4,64,128]{3,2,1,0:T(8,128)S(1)}, u32[]{:S(2)}, u32[]{:S(2)}) collective-permute-start(f32[2,4,64,128]{3,2,1,0:T(8,128)S(1)} %get-tuple-element.62), channel_id=1, source_target_pairs={{0,64},{64,0},{128,192},{192,128},{1,65},{65,1},{129,193},{193,129... | collective-permute-start | bytes 786440 | tf_op jit(solution)/shard_map/ppermute | solution.py:552
  53.8 9.1 %collective-permute-start.8 = (f32[2,4,64,128]{3,2,1,0:T(8,128)S(1)}, f32[2,4,64,128]{3,2,1,0:T(8,128)S(1)}, u32[]{:S(2)}, u32[]{:S(2)}) collective-permute-start(f32[2,4,64,128]{3,2,1,0:T(8,128)S(1)} %add.24), channel_id=1, source_target_pairs={{0,128},{128,0},{64,192},{192,64},{1,129},{129,1},{65,193},{193,65... | collective-permute-start | bytes 786440 | tf_op jit(solution)/shard_map/ppermute | solution.py:556
  63.1 2.5 %collective-permute-start.9 = (f32[2,4,64,128]{3,2,1,0:T(8,128)S(1)}, f32[2,4,64,128]{3,2,1,0:T(8,128)S(1)}, u32[]{:S(2)}, u32[]{:S(2)}) collective-permute-start(f32[2,4,64,128]{3,2,1,0:T(8,128)S(1)} %get-tuple-element.63.mine), channel_id=1, source_target_pairs={{0,64},{64,0},{128,192},{192,128},{1,65},{65,1},{129,193},{193,129... | collective-permute-start | bytes 786440 | tf_op jit(solution)/shard_map/ppermute | solution.py:552

commit v5 on v4

--- a/solution.py
+++ b/solution.py
@@ -245,8 +245,8 @@
         cells(bottom - 1 + k, CONE - k)
 
 
-def leap(now, before, after, base, diag, cx, cy, cz, outer, lane, slope, inject=None):
-    def cells(e, planes, slope_row):
+def leap(now, before, after, base, diag, cx, cy, cz, rows, lane, slope, inject=None):
+    for e, planes in rows:
         f = e - base
         for z in range(planes):
             u = now[f, z]
@@ -262,23 +262,23 @@
             if z == 0 and inject is not None:
                 acc = acc + inject[e - OFF + EDGE]
             after[f, z] = acc
-            if slope_row is not None:
-                slope[slope_row, z] = following - u
-
-    for r in range(ROWS):
-        cells(OFF + r, NZ, r)
-    for e, planes in outer:
-        cells(e, planes, None)
-
-
-def outer_rows(k, cone):
+            if OFF <= e < OFF + ROWS:
+                slope[e - OFF, z] = following - u
+
+
+def inner_rows(k):
+    return [(OFF + y, NZ) for y in range(k + 1, ROWS - 1 - k)]
+
+
+def step_rows(k, cone, skip=()):
     whole = STEPS - k
-    rows = [(OFF - whole + j, NZ) for j in range(whole)] + [(OFF + ROWS + j, NZ) for j in range(whole)]
+    rows = [(OFF + y, NZ) for y in range(ROWS)]
+    rows += [(OFF - whole + j, NZ) for j in range(whole)] + [(OFF + ROWS + j, NZ) for j in range(whole)]
     if cone:
         for j in range(CONE):
             planes = min(CONE - j, whole)
             rows += [(OFF - 1 - whole - j, planes), (OFF + ROWS + whole + j, planes)]
-    return rows
+    return [row for row in rows if row not in skip]
 
 
 def three_parts(f):
@@ -329,8 +329,8 @@
 
 
 def forward_kernel(
-    source_pos, source_wave, u0, u1, s, even, odd, even_other, odd_other, receivers, observed,
-    w1, w2, w3, w4, w5, d1, d2, d3, d4, d5, diag, cx, cy, cz, surf,
+    source_pos, source_wave, u0, u1, s, even, odd, other, receivers, observed, l6, l7,
+    w1, w2, w3, w4, w5, d1, d2, d3, d4, d5, diag, cx, cy, cz, surf, m6, m5, m4, m3, m_before, g6, g5, g4,
     stiff, before, edge,
 ):
     lane, tile = iotas()
@@ -358,7 +358,7 @@
             edge[2 * i] = ref[TILE_A - 2]
             edge[2 * i + 1] = ref[TILE_A - 1]
 
-    by_parity(((even, even_other), (odd, odd_other)), halos)
+    by_parity(((even, other.at[:TILE_S]), (odd, other.at[TILE_S:])), halos)
     coefficients(stiff, diag, cx, cy, cz, lane, tile)
     gy = lax.axis_index("gy")
 
@@ -377,7 +377,7 @@
     for k in range(STEPS):
         older = before if k == 0 else waves[k - 1]
         after = waves[k + 1]
-        leap(waves[k], older, after, 0, diag, cx, cy, cz, outer_rows(k, True), lane, slopes[k])
+        leap(waves[k], older, after, 0, diag, cx, cy, cz, step_rows(k, True), lane, slopes[k])
         reach = STEPS - k + CONE
 
         @pl.when((e_src >= OFF - reach) & (e_src < OFF + ROWS + reach))
@@ -396,12 +396,22 @@
     edges = [jnp.concatenate([edge[2 * i], edge[2 * i + 1]], 0) for i in range(2)]
     misfit_surfaces(waves, receivers, observed, edges, surf, lane, tile)
 
+    fill(m6, l6, REACH)
+    fill(m_before, l7, REACH)
+    lams = (m6, m5, m4, m3)
+    for k, slope in enumerate((g6, g5, g4)):
+        older = m_before if k == 0 else lams[k - 1]
+        leap(
+            lams[k], older, lams[k + 1], OFF - REACH, diag, cx, cy, cz, inner_rows(k), lane, slope, surf.at[STEPS - 1 - k]
+        )
+
 
 def forward(*args):
     one = jax.ShapeDtypeStruct(FIELD, f32)
     own = jax.ShapeDtypeStruct((ROWS, NZ, XT, LANES), f32)
     surf = jax.ShapeDtypeStruct((STEPS, SURF_ROWS, XT, LANES), f32)
-    outs = (one,) * (STEPS + 1) + (own,) * (STEPS + 1) + (one,) * 4 + (surf,)
+    short = jax.ShapeDtypeStruct(SHORT, f32)
+    outs = (one,) * (STEPS + 1) + (own,) * (STEPS + 1) + (one,) * 4 + (surf,) + (short,) * 5 + (own,) * 3
     return pl.pallas_call(
         forward_kernel,
         out_shape=outs,
@@ -415,17 +425,14 @@
 
 
 def adjoint_kernel(
-    l6, l7, even, odd, w1, w2, w3, w4, w5, d1, d2, d3, d4, d5, diag, cx, cy, cz, surf,
-    keep, send,
-    m6, m5, m4, m3, m2, before, g6, g5, g4, g3, face_y, grad,
+    odd, even, w1, w2, w3, w4, w5, d1, d2, d3, d4, d5, diag, cx, cy, cz, surf, *rest
 ):
+    m6, m5, m4, m3, before, g6, g5, g4, keep, send, m2, g3, face_y, grad = rest[8:]
     lane, tile = iotas()
     x_end = (lane == LANES - 1) & (tile == XT - 1)
     x_side = x_end | ((lane == 0) & (tile == 0))
     lams = (m6, m5, m4, m3, m2)
     slopes = (g6, g5, g4, g3)
-    fill(m6, l6, REACH)
-    fill(before, l7, REACH)
 
     def halos(low, high):
         fill_halo(m6, REACH, low, high, 0, REACH)
@@ -434,10 +441,8 @@
     by_parity((even, odd), halos)
     for k in range(STEPS):
         older = before if k == 0 else lams[k - 1]
-        leap(
-            lams[k], older, lams[k + 1], OFF - REACH, diag, cx, cy, cz, outer_rows(k, False), lane, slopes[k],
-            surf.at[STEPS - 1 - k],
-        )
+        rows = step_rows(k, False, inner_rows(k))
+        leap(lams[k], older, lams[k + 1], OFF - REACH, diag, cx, cy, cz, rows, lane, slopes[k], surf.at[STEPS - 1 - k])
 
     pairs = ((w5, m6, d5, g6), (w4, m5, d4, g5), (w3, m4, d3, g4), (w2, m3, d2, g3), (w1, m2, d1, None))
     for z in range(NZ):
@@ -493,22 +498,25 @@
 
 def adjoint(*args):
     part = jax.ShapeDtypeStruct((2, 4, XT * ROWS, LANES), f32)
-    own = pltpu.VMEM((ROWS, NZ, XT, LANES), f32)
+    own = jax.ShapeDtypeStruct((ROWS, NZ, XT, LANES), f32)
+    outs = (jax.ShapeDtypeStruct(SHORT, f32),) * 5 + (own,) * 3 + (part, part)
+    first = len(args) - 8
     return pl.pallas_call(
         adjoint_kernel,
-        out_shape=(part, part),
+        out_shape=outs,
         in_specs=[VMEM] * len(args),
-        out_specs=(VMEM, VMEM),
-        scratch_shapes=[pltpu.VMEM(SHORT, f32)] * (STEPS + 2)
-        + [own] * STEPS
-        + [
+        out_specs=(VMEM,) * len(outs),
+        input_output_aliases={first + i: i for i in range(8)},
+        scratch_shapes=[
+            pltpu.VMEM(SHORT, f32),
+            pltpu.VMEM((ROWS, NZ, XT, LANES), f32),
             pltpu.VMEM((NZ, XT, LANES), f32),
             pltpu.VMEM((NZ, XT * ROWS, LANES), f32),
         ],
         compiler_params=pltpu.CompilerParams(vmem_limit_bytes=16 << 20),
         cost_estimate=pl.CostEstimate(flops=1 << 25, bytes_accessed=1 << 24, transcendentals=0),
         name="adjoint",
-    )(*args)
+    )(*args)[-2:]
 
 
 def finish_kernel(mine, other, out, sems):
@@ -579,16 +587,14 @@
     a_even, a_odd = pack(pack_first_kernel, "pack_first", TILE_A, s, u1, u0, receiver_x[0], observed[0])
     l_even, l_odd = pack(pack_adjoint_kernel, "pack_adjoint", TILE_L, l6, l7)
     a_even, a_odd = swap_even(a_even), swap_odd(a_odd)
-    l_even, l_odd, a_even = lax.optimization_barrier((l_even, l_odd, a_even))
-    l_even, l_odd = swap_even(l_even), swap_odd(l_odd)
-    even_other, odd_other = swap_core(a_even[:TILE_S]), swap_core(a_odd[:TILE_S])
-    *fields, surf = forward(
-        source_pos, source_wave, u0, u1, s, a_even, a_odd, even_other, odd_other, receiver_x[0], observed[0]
+    moments = jnp.stack([first, second])
+    l_even, l_odd, moments, a_even = lax.optimization_barrier((l_even, l_odd, moments, a_even))
+    l_even, l_odd, moments = swap_even(l_even), swap_odd(l_odd), swap_far(moments)
+    other = swap_core(jnp.concatenate([a_even[:TILE_S], a_odd[:TILE_S]]))
+    fields = forward(
+        source_pos, source_wave, u0, u1, s, a_even, a_odd, other, receiver_x[0], observed[0], l6, l7
     )
-    moments = jnp.stack([first, second])
-    l_even, moments, surf = lax.optimization_barrier((l_even, moments, surf))
-    moments = swap_far(moments)
-    keep, send = adjoint(l6, l7, l_even, l_odd, *fields, surf)
+    keep, send = adjoint(l_odd, l_even, *fields)
     keep, send, moments = lax.optimization_barrier((keep, send, moments))
     chip_sum = keep + swap_core(send)
     share = chip_sum + swap_far(chip_sum)

time: 66.6 us -> 66 us (level)
    ppermute x2, waiting for transfers between devices: 13.7 us -> 15.2 us  [swap_far(): return lax.ppermute(block, 'shot', [(0, 2), (2, 0), (1, 3), (3, 1)])]
    ppermute x4 -> x3, waiting for transfers between devices: 2.94 us -> 1.6 us  [swap_core(): return lax.ppermute(block, 'shot', [(0, 1), (1, 0), (2, 3), (3, 2)])]
    ppermute x2, starting transfers between devices: 2.67 us -> 1.47 us  [swap_even(): return lax.ppermute(block, 'gy', pairs + [(j, i) for i, j in pairs])]
    pallas_call x1, Pallas kernels: 5.58 us -> 4.39 us  [adjoint(): pl.pallas_call(adjoint_kernel, out_shape=outs, in_specs=[VMEM] * len(args...]
    pallas_call x1, Pallas kernels: 6.55 us -> 7.71 us  [forward(): pl.pallas_call(forward_kernel, out_shape=outs, in_specs=[SMEM] * 2 + [VME...]
    ppermute x2, starting transfers between devices: 8.55 us -> 9.37 us  [swap_odd(): return lax.ppermute(block, 'gy', pairs + [(j, i) for i, j in pairs])]
    ppermute x4 -> x3, starting transfers between devices: 4.05 us -> 3.68 us  [swap_core(): return lax.ppermute(block, 'shot', [(0, 1), (1, 0), (2, 3), (3, 2)])]
  transfers between devices with their start and end apart: 10 -> 9, of which waited for: 8 -> 6; matrix products, arithmetic and copies ran while one was open for 1% -> 1% of each run, Pallas kernels for 20% -> 21%
where the time goes in v5:
time: 66 us; the launch traced here: 65.8 us
  waiting for transfers between devices  29.6 us (45%)
  starting transfers between devices  17.9 us (27%)
  Pallas kernels  16.2 us (25%)
  other arithmetic  1.02 us (2%)
  between operations  0.91 us (1%)
    ppermute x2, waiting for transfers between devices, swap_far(): return lax.ppermute(block, 'shot', [(0, 2), (2, 0), (1, 3), (3, 1)])  15.2 us
    ppermute x2, waiting for transfers between devices, swap_even(): return lax.ppermute(block, 'gy', pairs + [(j, i) for i, j in pairs])  12.2 us
    ppermute x2, starting transfers between devices, swap_odd(): return lax.ppermute(block, 'gy', pairs + [(j, i) for i, j in pairs])  9.37 us
    pallas_call x1, Pallas kernels, forward(): pl.pallas_call(forward_kernel, out_shape=outs, in_specs=[SMEM] * 2 + [VME...  7.71 us
    pallas_call x1, Pallas kernels, adjoint(): pl.pallas_call(adjoint_kernel, out_shape=outs, in_specs=[VMEM] * len(args...  4.39 us
    ppermute x3, starting transfers between devices, swap_core(): return lax.ppermute(block, 'shot', [(0, 1), (1, 0), (2, 3), (3, 2)])  3.68 us
    ppermute x2, starting transfers between devices, swap_far(): return lax.ppermute(block, 'shot', [(0, 2), (2, 0), (1, 3), (3, 1)])  3.37 us
    pallas_call x2, Pallas kernels, pack(): pl.pallas_call(kernel, out_shape=(shape, shape), in_specs=[pl.BlockSpec(m...  3.31 us
  transfers between devices with their start and end apart: 9, of which 6 were waited for; matrix products, arithmetic and copies ran while one was open for 1% of the time, Pallas kernels for 21%

profile of v5, /device:TPU:97, one launch (start us, length us, event | category | flops | bytes accessed | tf_op | source)
XLA Modules:
  0.0 65.8 jit_solution(2149888103036699708)
XLA Ops:
  0.7 1.8 %pack_first.1 = (f32[204,8,128]{2,1,0:T(8,128)S(1)}, f32[204,8,128]{2,1,0:T(8,128)S(1)}) custom-call(f32[16,64,128]{2,1,0:T(8,128)} %bitcast.72, f32[16,64,128]{2,1,0:T(8,128)} %bitcast.77, f32[16,64,128]{2,1,0:T(8,128)} %bitcast.75, s32[8,128]{1,0:T(8,128)} %bitcast.85, f32[4,8,128]{2,1,0:T(8,128)} %bitcast.83), custom_call_target="tpu_custom_call" | custom-call | bytes 65536 | tf_op jit(solution)/shard_map/pack_first/pallas_call | solution.py:168
  2.4 1.4 %collective-permute-start = (f32[204,8,128]{2,1,0:T(8,128)S(1)}, f32[204,8,128]{2,1,0:T(8,128)S(1)}, u32[]{:S(2)}, u32[]{:S(2)}) collective-permute-start(f32[204,8,128]{2,1,0:T(8,128)S(1)} %get-tuple-element.41), channel_id=1, source_target_pairs={{0,1},{2,3},{4,5},{6,7},{8,9},{10,11},{12,13},{14,15},{16,17},{18,... | collective-permute-start | bytes 2506760 | tf_op jit(solution)/shard_map/ppermute | solution.py:550
  3.8 4.3 %collective-permute-start.3 = (f32[204,8,128]{2,1,0:T(8,128)S(1)}, f32[204,8,128]{2,1,0:T(8,128)S(1)}, u32[]{:S(2)}, u32[]{:S(2)}) collective-permute-start(f32[204,8,128]{2,1,0:T(8,128)S(1)} %get-tuple-element.45), channel_id=1, source_target_pairs={{1,2},{3,4},{5,6},{7,8},{9,10},{11,12},{13,14},{15,16},{17,18},{19... | collective-permute-start | bytes 2506760 | tf_op jit(solution)/shard_map/ppermute | solution.py:556
  8.1 0.0 copy-start.4
  8.1 1.5 %pack_adjoint.1 = (f32[144,8,128]{2,1,0:T(8,128)S(1)}, f32[144,8,128]{2,1,0:T(8,128)S(1)}) custom-call(f32[16,64,128]{2,1,0:T(8,128)} %bitcast.79, f32[16,64,128]{2,1,0:T(8,128)} %bitcast.81), custom_call_target="tpu_custom_call" | custom-call | bytes 65536 | tf_op jit(solution)/shard_map/pack_adjoint/pallas_call | solution.py:168
  9.7 0.0 copy-start.1
  9.8 12.2 %collective-permute-done.even = f32[204,8,128]{2,1,0:T(8,128)S(1)} collective-permute-done((f32[204,8,128]{2,1,0:T(8,128)S(1)}, f32[204,8,128]{2,1,0:T(8,128)S(1)}, u32[]{:S(2)}, u32[]{:S(2)}) %collective-permute-start) | collective-permute-done | bytes 835616 | tf_op jit(solution)/shard_map/ppermute | solution.py:550
  22.0 5.1 %collective-permute-start.1 = (f32[144,8,128]{2,1,0:T(8,128)S(1)}, f32[144,8,128]{2,1,0:T(8,128)S(1)}, u32[]{:S(2)}, u32[]{:S(2)}) collective-permute-start(f32[144,8,128]{2,1,0:T(8,128)S(1)} %get-tuple-element.42), channel_id=1, source_target_pairs={{1,2},{3,4},{5,6},{7,8},{9,10},{11,12},{13,14},{15,16},{17,18},{19... | collective-permute-start | bytes 1769480 | tf_op jit(solution)/shard_map/ppermute | solution.py:556
  27.1 0.1 collective-permute-start.2
  27.2 0.6 collective-permute-done.3.odd
  27.9 2.0 %collective-permute-start.4 = (f32[92,8,128]{2,1,0:T(8,128)S(1)}, f32[92,8,128]{2,1,0:T(8,128)S(1)}, u32[]{:S(2)}, u32[]{:S(2)}) collective-permute-start(f32[92,8,128]{2,1,0:T(8,128)S(1)} %pad_maximum_fusion), channel_id=1, source_target_pairs={{0,64},{64,0},{128,192},{192,128},{1,65},{65,1},{129,193},{193,129... | collective-permute-start | bytes 1130504 | tf_op jit(solution)/shard_map/ppermute | solution.py:560
  29.9 2.8 %collective-permute-start.5 = (f32[2,4,64,128]{3,2,1,0:T(8,128)S(1)}, f32[2,4,64,128]{3,2,1,0:T(8,128)S(1)}, u32[]{:S(2)}, u32[]{:S(2)}) collective-permute-start(f32[2,4,64,128]{3,2,1,0:T(8,128)S(1)} %pad_maximum_fusion.2), channel_id=1, source_target_pairs={{0,128},{128,0},{64,192},{192,64},{1,129},{129,1},{65,193},{193,65... | collective-permute-start | bytes 786440 | tf_op jit(solution)/shard_map/ppermute | solution.py:564
  32.7 7.7 %forward.1 = (f32[24,16,8,128]{3,2,1,0:T(8,128)S(1)}, f32[24,16,8,128]{3,2,1,0:T(8,128)S(1)}, f32[24,16,8,128]{3,2,1,0:T(8,128)S(1)}, f32[24,16,8,128]{3,2,1,0:T...) custom-call(s32[1,3]{1,0:T(1,128)S(1)} %copy-done.7, ...), custom_call_target="tpu_custom_call" | custom-call | flops 33554432 | bytes 16777216 | tf_op jit(solution)/shard_map/forward/pallas_call | solution.py:415
  40.4 4.4 %adjoint.1 = (f32[18,16,8,128]{3,2,1,0:T(8,128)S(1)}, f32[18,16,8,128]{3,2,1,0:T(8,128)S(1)}, f32[18,16,8,128]{3,2,1,0:T(8,128)S(1)}, f32[18,16,8,128]{3,2,1,0:T...) custom-call(f32[144,8,128]{2,1,0:T(8,128)S(1)} %collective-permute-d, ...), custom_call_target="tpu_custom_call", output_to_operand_aliasing={{0}: (17, {}), {1}: (18, {}), {2}: (19, {}), {3}: (20, {}),... | custom-call | flops 33554432 | bytes 16777216 | tf_op jit(solution)/shard_map/adjoint/pallas_call | solution.py:504
  44.8 6.7 %collective-permute-done.5 = f32[2,4,64,128]{3,2,1,0:T(8,128)S(1)} collective-permute-done((f32[2,4,64,128]{3,2,1,0:T(8,128)S(1)}, f32[2,4,64,128]{3,2,1,0:T(8,128)S(1)}, u32[]{:S(2)}, u32[]{:S(2)}) %collective-permute-start.5) | collective-permute-done | bytes 262176 | tf_op jit(solution)/shard_map/ppermute | solution.py:564
  51.5 0.4 collective-permute-start.6
  52.0 1.2 %collective-permute-done.6 = f32[2,4,64,128]{3,2,1,0:T(8,128)S(1)} collective-permute-done((f32[2,4,64,128]{3,2,1,0:T(8,128)S(1)}, f32[2,4,64,128]{3,2,1,0:T(8,128)S(1)}, u32[]{:S(2)}, u32[]{:S(2)}) %collective-permute-start.6) | collective-permute-done | bytes 262176 | tf_op jit(solution)/shard_map/ppermute | solution.py:560
  53.2 0.6 collective-permute-start.7
  53.8 8.5 %collective-permute-done.7 = f32[2,4,64,128]{3,2,1,0:T(8,128)S(1)} collective-permute-done((f32[2,4,64,128]{3,2,1,0:T(8,128)S(1)}, f32[2,4,64,128]{3,2,1,0:T(8,128)S(1)}, u32[]{:S(2)}, u32[]{:S(2)}) %collective-permute-start.7) | collective-permute-done | bytes 262176 | tf_op jit(solution)/shard_map/ppermute | solution.py:564
  62.3 0.2 fusion.8
  62.5 1.3 %collective-permute-start.8 = (f32[2,4,64,128]{3,2,1,0:T(8,128)S(1)}, f32[2,4,64,128]{3,2,1,0:T(8,128)S(1)}, u32[]{:S(2)}, u32[]{:S(2)}) collective-permute-start(f32[2,4,64,128]{3,2,1,0:T(8,128)S(1)} %get-tuple-element.75.mine), channel_id=1, source_target_pairs={{0,64},{64,0},{128,192},{192,128},{1,65},{65,1},{129,193},{193,129... | collective-permute-start | bytes 786440 | tf_op jit(solution)/shard_map/ppermute | solution.py:560
  63.8 0.7 %fusion.9 = (f32[4,8,1024]{2,1,0:T(8,128)}, f32[4,8,1024]{2,1,0:T(8,128)}) fusion(f32[2,4,64,128]{3,2,1,0:T(8,128)S(1)} %get-tuple-element.77, pred[]{:T(512)S(6)} %eq.12, f32[2,4,64,128]{3,2,1,0:T(8,128)S(1)} %get-tuple-element.76), kind=kLoop, calls=%fused_computation.17 | loop fusion | flops 65536 | bytes 786433 | tf_op jit(solution)/shard_map/reshape | solution.py:51
  64.5 0.4 collective-permute-done.8.other
  65.0 0.8 %finish.1 = f32[16,64,128]{2,1,0:T(8,128)} custom-call(f32[2,4,64,128]{3,2,1,0:T(8,128)S(1)} %get-tuple-element.75.mine, f32[2,4,64,128]{3,2,1,0:T(8,128)S(1)} %collective-permute-done.8.other), custom_call_target="tpu_custom_call" | custom-call | tf_op jit(solution)/shard_map/finish/pallas_call | solution.py:536
  (29 shorter events, 0.2 us)
Async XLA Ops:
  0.6 9.1 %copy-start.9 = (f32[4,8,1024]{2,1,0:T(8,128)S(1)}, f32[4,8,1024]{2,1,0:T(8,128)}, u32[]{:S(2)}) copy-start(f32[4,8,1024]{2,1,0:T(8,128)} %param.12) | copy-start | bytes 393220
  0.6 9.1 %copy-start.10 = (f32[4,8,1024]{2,1,0:T(8,128)S(1)}, f32[4,8,1024]{2,1,0:T(8,128)}, u32[]{:S(2)}) copy-start(f32[4,8,1024]{2,1,0:T(8,128)} %param.13) | copy-start | bytes 393220
  2.4 19.5 %collective-permute-start = (f32[204,8,128]{2,1,0:T(8,128)S(1)}, f32[204,8,128]{2,1,0:T(8,128)S(1)}, u32[]{:S(2)}, u32[]{:S(2)}) collective-permute-start(f32[204,8,128]{2,1,0:T(8,128)S(1)} %get-tuple-element.41), channel_id=1, source_target_pairs={{0,1},{2,3},{4,5},{6,7},{8,9},{10,11},{12,13},{14,15},{16,17},{18,... | collective-permute-start | bytes 2506760 | tf_op jit(solution)/shard_map/ppermute | solution.py:550
  3.8 24.0 %collective-permute-start.3 = (f32[204,8,128]{2,1,0:T(8,128)S(1)}, f32[204,8,128]{2,1,0:T(8,128)S(1)}, u32[]{:S(2)}, u32[]{:S(2)}) collective-permute-start(f32[204,8,128]{2,1,0:T(8,128)S(1)} %get-tuple-element.45), channel_id=1, source_target_pairs={{1,2},{3,4},{5,6},{7,8},{9,10},{11,12},{13,14},{15,16},{17,18},{19... | collective-permute-start | bytes 2506760 | tf_op jit(solution)/shard_map/ppermute | solution.py:556
  8.1 24.5 %copy-start.3 = (f32[1,16,8,1024]{3,2,1,0:T(8,128)S(1)}, f32[1,16,8,1024]{3,2,1,0:T(8,128)}, u32[]{:S(2)}) copy-start(f32[1,16,8,1024]{3,2,1,0:T(8,128)} %param.17) | copy-start | bytes 1572868
  8.1 24.5 %copy-start.4 = (f32[1,16,8,1024]{3,2,1,0:T(8,128)S(1)}, f32[1,16,8,1024]{3,2,1,0:T(8,128)}, u32[]{:S(2)}) copy-start(f32[1,16,8,1024]{3,2,1,0:T(8,128)} %param.16) | copy-start | bytes 1572868
  9.7 23.0 %copy-start = (f32[16,8,1024]{2,1,0:T(8,128)S(1)}, f32[16,8,1024]{2,1,0:T(8,128)}, u32[]{:S(2)}) copy-start(f32[16,8,1024]{2,1,0:T(8,128)} %param.11) | copy-start | bytes 1572868
  9.7 23.0 %copy-start.1 = (f32[1,16,8,1024]{3,2,1,0:T(8,128)S(1)}, f32[1,16,8,1024]{3,2,1,0:T(8,128)}, u32[]{:S(2)}) copy-start(f32[1,16,8,1024]{3,2,1,0:T(8,128)} %param.14) | copy-start | bytes 1572868
  9.7 23.0 %copy-start.2 = (f32[1,16,8,1024]{3,2,1,0:T(8,128)S(1)}, f32[1,16,8,1024]{3,2,1,0:T(8,128)}, u32[]{:S(2)}) copy-start(f32[1,16,8,1024]{3,2,1,0:T(8,128)} %param.15) | copy-start | bytes 1572868
  9.7 23.0 %copy-start.5 = (f32[1,4,8,128]{3,2,1,0:T(8,128)S(1)}, f32[1,4,8,128]{3,2,1,0:T(8,128)}, u32[]{:S(2)}) copy-start(f32[1,4,8,128]{3,2,1,0:T(8,128)} %param.18) | copy-start | bytes 49156
  9.7 23.0 %copy-start.6 = (s32[1,8,128]{2,1,0:T(8,128)S(1)}, s32[1,8,128]{2,1,0:T(8,128)}, u32[]{:S(2)}) copy-start(s32[1,8,128]{2,1,0:T(8,128)} %param.19) | copy-start | bytes 12292
  9.7 23.0 %copy-start.7 = (s32[1,3]{1,0:T(1,128)S(1)}, s32[1,3]{1,0:T(1,128)}, u32[]{:S(2)}) copy-start(s32[1,3]{1,0:T(1,128)} %source_pos.1) | copy-start | bytes 40
  9.7 23.0 %copy-start.8 = (f32[1,4]{1,0:T(1,128)S(1)}, f32[1,4]{1,0:T(1,128)}, u32[]{:S(2)}) copy-start(f32[1,4]{1,0:T(1,128)} %source_wave.1) | copy-start | bytes 52
  22.0 18.4 %collective-permute-start.1 = (f32[144,8,128]{2,1,0:T(8,128)S(1)}, f32[144,8,128]{2,1,0:T(8,128)S(1)}, u32[]{:S(2)}, u32[]{:S(2)}) collective-permute-start(f32[144,8,128]{2,1,0:T(8,128)S(1)} %get-tuple-element.42), channel_id=1, source_target_pairs={{1,2},{3,4},{5,6},{7,8},{9,10},{11,12},{13,14},{15,16},{17,18},{19... | collective-permute-start | bytes 1769480 | tf_op jit(solution)/shard_map/ppermute | solution.py:556
  27.1 13.3 %collective-permute-start.2 = (f32[144,8,128]{2,1,0:T(8,128)S(1)}, f32[144,8,128]{2,1,0:T(8,128)S(1)}, u32[]{:S(2)}, u32[]{:S(2)}) collective-permute-start(f32[144,8,128]{2,1,0:T(8,128)S(1)} %get-tuple-element.43), channel_id=1, source_target_pairs={{0,1},{2,3},{4,5},{6,7},{8,9},{10,11},{12,13},{14,15},{16,17},{18,... | collective-permute-start | bytes 1769480 | tf_op jit(solution)/shard_map/ppermute | solution.py:550
  27.9 4.7 %collective-permute-start.4 = (f32[92,8,128]{2,1,0:T(8,128)S(1)}, f32[92,8,128]{2,1,0:T(8,128)S(1)}, u32[]{:S(2)}, u32[]{:S(2)}) collective-permute-start(f32[92,8,128]{2,1,0:T(8,128)S(1)} %pad_maximum_fusion), channel_id=1, source_target_pairs={{0,64},{64,0},{128,192},{192,128},{1,65},{65,1},{129,193},{193,129... | collective-permute-start | bytes 1130504 | tf_op jit(solution)/shard_map/ppermute | solution.py:560
  29.9 21.7 %collective-permute-start.5 = (f32[2,4,64,128]{3,2,1,0:T(8,128)S(1)}, f32[2,4,64,128]{3,2,1,0:T(8,128)S(1)}, u32[]{:S(2)}, u32[]{:S(2)}) collective-permute-start(f32[2,4,64,128]{3,2,1,0:T(8,128)S(1)} %pad_maximum_fusion.2), channel_id=1, source_target_pairs={{0,128},{128,0},{64,192},{192,64},{1,129},{129,1},{65,193},{193,65... | collective-permute-start | bytes 786440 | tf_op jit(solution)/shard_map/ppermute | solution.py:564
  51.5 1.6 %collective-permute-start.6 = (f32[2,4,64,128]{3,2,1,0:T(8,128)S(1)}, f32[2,4,64,128]{3,2,1,0:T(8,128)S(1)}, u32[]{:S(2)}, u32[]{:S(2)}) collective-permute-start(f32[2,4,64,128]{3,2,1,0:T(8,128)S(1)} %get-tuple-element.74), channel_id=1, source_target_pairs={{0,64},{64,0},{128,192},{192,128},{1,65},{65,1},{129,193},{193,129... | collective-permute-start | bytes 786440 | tf_op jit(solution)/shard_map/ppermute | solution.py:560
  53.2 9.1 %collective-permute-start.7 = (f32[2,4,64,128]{3,2,1,0:T(8,128)S(1)}, f32[2,4,64,128]{3,2,1,0:T(8,128)S(1)}, u32[]{:S(2)}, u32[]{:S(2)}) collective-permute-start(f32[2,4,64,128]{3,2,1,0:T(8,128)S(1)} %add.24), channel_id=1, source_target_pairs={{0,128},{128,0},{64,192},{192,64},{1,129},{129,1},{65,193},{193,65... | collective-permute-start | bytes 786440 | tf_op jit(solution)/shard_map/ppermute | solution.py:564
  62.5 2.5 %collective-permute-start.8 = (f32[2,4,64,128]{3,2,1,0:T(8,128)S(1)}, f32[2,4,64,128]{3,2,1,0:T(8,128)S(1)}, u32[]{:S(2)}, u32[]{:S(2)}) collective-permute-start(f32[2,4,64,128]{3,2,1,0:T(8,128)S(1)} %get-tuple-element.75.mine), channel_id=1, source_target_pairs={{0,64},{64,0},{128,192},{192,128},{1,65},{65,1},{129,193},{193,129... | collective-permute-start | bytes 786440 | tf_op jit(solution)/shard_map/ppermute | solution.py:560

commit v6 on v5

--- a/solution.py
+++ b/solution.py
@@ -519,6 +519,27 @@
     )(*args)[-2:]
 
 
+def blend_kernel(first, second, moments, first_two, second_two):
+    far = lax.axis_index("shot") // 2
+    first_two[far] = BETA_ONE * first[...]
+    first_two[1 - far] = BETA_ONE * moments[0]
+    second_two[far] = BETA_TWO * second[...]
+    second_two[1 - far] = BETA_TWO * moments[1]
+
+
+def blend(first, second, moments):
+    two = jax.ShapeDtypeStruct((2, 4, XT * ROWS, LANES), f32)
+    return pl.pallas_call(
+        blend_kernel,
+        out_shape=(two, two),
+        in_specs=[VMEM] * 3,
+        out_specs=(VMEM, VMEM),
+        compiler_params=pltpu.CompilerParams(vmem_limit_bytes=4 << 20),
+        cost_estimate=pl.CostEstimate(flops=0, bytes_accessed=1 << 24, transcendentals=0),
+        name="blend",
+    )(first, second, moments)
+
+
 def finish_kernel(mine, other, out, sems):
     core = core_index()
     copies = []
@@ -595,15 +616,15 @@
         source_pos, source_wave, u0, u1, s, a_even, a_odd, other, receiver_x[0], observed[0], l6, l7
     )
     keep, send = adjoint(l_odd, l_even, *fields)
-    keep, send, moments = lax.optimization_barrier((keep, send, moments))
+    keep, moments = lax.optimization_barrier((keep, moments))
+    first_two, second_two = blend(first, second, moments)
     chip_sum = keep + swap_core(send)
+    chip_sum, first_two, second_two = lax.optimization_barrier((chip_sum, first_two, second_two))
     share = chip_sum + swap_far(chip_sum)
-    first_two = jnp.where(far == 0, jnp.stack([first, moments[0]]), jnp.stack([moments[0], first]))
-    second_two = jnp.where(far == 0, jnp.stack([second, moments[1]]), jnp.stack([moments[1], second]))
     halves = s.reshape(2, 2, 4, XT * ROWS, LANES)
     stiff_two = jnp.where(core == 0, halves[:, 0], halves[:, 1])
-    first_new = BETA_ONE * first_two + (1.0 - BETA_ONE) * share
-    second_new = BETA_TWO * second_two + (1.0 - BETA_TWO) * share * share
+    first_new = first_two + (1.0 - BETA_ONE) * share
+    second_new = second_two + (1.0 - BETA_TWO) * share * share
     updated = stiff_two - LEARN_RATE * (first_new / (1.0 - BETA_ONE**ADAM_TICKS)) / (
         jnp.sqrt(second_new / (1.0 - BETA_TWO**ADAM_TICKS)) + ADAM_EPS
     )

time: 66 us -> 64.4 us (0.976)
  waiting for transfers between devices: 29.6 us -> 25.9 us
  starting transfers between devices: 17.9 us -> 20.1 us
    ppermute x2, waiting for transfers between devices: 15.2 us -> 12.6 us  [swap_far(): return lax.ppermute(block, 'shot', [(0, 2), (2, 0), (1, 3), (3, 1)])]
    ppermute x3, starting transfers between devices: 3.68 us -> 5.85 us  [swap_core(): return lax.ppermute(block, 'shot', [(0, 1), (1, 0), (2, 3), (3, 2)])]
    ppermute x3, waiting for transfers between devices: 1.6 us -> 0.44 us  [swap_core(): return lax.ppermute(block, 'shot', [(0, 1), (1, 0), (2, 3), (3, 2)])]
  transfers between devices with their start and end apart: 9 -> 9, of which waited for: 6 -> 5; matrix products, arithmetic and copies ran while one was open for 1% -> 1% of each run, Pallas kernels for 21% -> 21%
where the time goes in v6:
time: 64.4 us; the launch traced here: 64.2 us
  waiting for transfers between devices  25.9 us (40%)
  starting transfers between devices  20.1 us (31%)
  Pallas kernels  16.3 us (25%)
  other arithmetic  1.02 us (2%)
  between operations  0.92 us (1%)
    ppermute x2, waiting for transfers between devices, swap_far(): return lax.ppermute(block, 'shot', [(0, 2), (2, 0), (1, 3), (3, 1)])  12.6 us
    ppermute x2, waiting for transfers between devices, swap_even(): return lax.ppermute(block, 'gy', pairs + [(j, i) for i, j in pairs])  12.2 us
    ppermute x2, starting transfers between devices, swap_odd(): return lax.ppermute(block, 'gy', pairs + [(j, i) for i, j in pairs])  9.37 us
    pallas_call x1, Pallas kernels, forward(): pl.pallas_call(forward_kernel, out_shape=outs, in_specs=[SMEM] * 2 + [VME...  7.71 us
    ppermute x3, starting transfers between devices, swap_core(): return lax.ppermute(block, 'shot', [(0, 1), (1, 0), (2, 3), (3, 2)])  5.85 us
    pallas_call x1, Pallas kernels, adjoint(): pl.pallas_call(adjoint_kernel, out_shape=outs, in_specs=[VMEM] * len(args...  4.39 us
    ppermute x2, starting transfers between devices, swap_far(): return lax.ppermute(block, 'shot', [(0, 2), (2, 0), (1, 3), (3, 1)])  3.37 us
    pallas_call x2, Pallas kernels, pack(): pl.pallas_call(kernel, out_shape=(shape, shape), in_specs=[pl.BlockSpec(m...  3.31 us
  transfers between devices with their start and end apart: 9, of which 5 were waited for; matrix products, arithmetic and copies ran while one was open for 1% of the time, Pallas kernels for 21%

profile of v6, /device:TPU:97, one launch (start us, length us, event | category | flops | bytes accessed | tf_op | source)
XLA Modules:
  0.0 64.2 jit_solution(11814725591233113252)
XLA Ops:
  0.7 1.8 %pack_first.1 = (f32[204,8,128]{2,1,0:T(8,128)S(1)}, f32[204,8,128]{2,1,0:T(8,128)S(1)}) custom-call(f32[16,64,128]{2,1,0:T(8,128)} %bitcast.76, f32[16,64,128]{2,1,0:T(8,128)} %bitcast.81, f32[16,64,128]{2,1,0:T(8,128)} %bitcast.79, s32[8,128]{1,0:T(8,128)} %bitcast.93, f32[4,8,128]{2,1,0:T(8,128)} %bitcast.91), custom_call_target="tpu_custom_call" | custom-call | bytes 65536 | tf_op jit(solution)/shard_map/pack_first/pallas_call | solution.py:168
  2.4 1.4 %collective-permute-start = (f32[204,8,128]{2,1,0:T(8,128)S(1)}, f32[204,8,128]{2,1,0:T(8,128)S(1)}, u32[]{:S(2)}, u32[]{:S(2)}) collective-permute-start(f32[204,8,128]{2,1,0:T(8,128)S(1)} %get-tuple-element.45), channel_id=1, source_target_pairs={{0,1},{2,3},{4,5},{6,7},{8,9},{10,11},{12,13},{14,15},{16,17},{18,... | collective-permute-start | bytes 2506760 | tf_op jit(solution)/shard_map/ppermute | solution.py:571
  3.8 4.3 %collective-permute-start.3 = (f32[204,8,128]{2,1,0:T(8,128)S(1)}, f32[204,8,128]{2,1,0:T(8,128)S(1)}, u32[]{:S(2)}, u32[]{:S(2)}) collective-permute-start(f32[204,8,128]{2,1,0:T(8,128)S(1)} %get-tuple-element.49), channel_id=1, source_target_pairs={{1,2},{3,4},{5,6},{7,8},{9,10},{11,12},{13,14},{15,16},{17,18},{19... | collective-permute-start | bytes 2506760 | tf_op jit(solution)/shard_map/ppermute | solution.py:577
  8.1 0.0 copy-start.3
  8.1 1.5 %pack_adjoint.1 = (f32[144,8,128]{2,1,0:T(8,128)S(1)}, f32[144,8,128]{2,1,0:T(8,128)S(1)}) custom-call(f32[16,64,128]{2,1,0:T(8,128)} %bitcast.83, f32[16,64,128]{2,1,0:T(8,128)} %bitcast.85), custom_call_target="tpu_custom_call" | custom-call | bytes 65536 | tf_op jit(solution)/shard_map/pack_adjoint/pallas_call | solution.py:168
  9.7 0.0 copy-start
  9.8 12.2 %collective-permute-done.even = f32[204,8,128]{2,1,0:T(8,128)S(1)} collective-permute-done((f32[204,8,128]{2,1,0:T(8,128)S(1)}, f32[204,8,128]{2,1,0:T(8,128)S(1)}, u32[]{:S(2)}, u32[]{:S(2)}) %collective-permute-start) | collective-permute-done | bytes 835616 | tf_op jit(solution)/shard_map/ppermute | solution.py:571
  22.0 5.1 %collective-permute-start.1 = (f32[144,8,128]{2,1,0:T(8,128)S(1)}, f32[144,8,128]{2,1,0:T(8,128)S(1)}, u32[]{:S(2)}, u32[]{:S(2)}) collective-permute-start(f32[144,8,128]{2,1,0:T(8,128)S(1)} %get-tuple-element.46), channel_id=1, source_target_pairs={{1,2},{3,4},{5,6},{7,8},{9,10},{11,12},{13,14},{15,16},{17,18},{19... | collective-permute-start | bytes 1769480 | tf_op jit(solution)/shard_map/ppermute | solution.py:577
  27.1 0.1 collective-permute-start.2
  27.2 0.6 collective-permute-done.3.odd
  27.9 2.0 %collective-permute-start.4 = (f32[92,8,128]{2,1,0:T(8,128)S(1)}, f32[92,8,128]{2,1,0:T(8,128)S(1)}, u32[]{:S(2)}, u32[]{:S(2)}) collective-permute-start(f32[92,8,128]{2,1,0:T(8,128)S(1)} %pad_maximum_fusion), channel_id=1, source_target_pairs={{0,64},{64,0},{128,192},{192,128},{1,65},{65,1},{129,193},{193,129... | collective-permute-start | bytes 1130504 | tf_op jit(solution)/shard_map/ppermute | solution.py:581
  29.9 2.8 %collective-permute-start.5 = (f32[2,4,64,128]{3,2,1,0:T(8,128)S(1)}, f32[2,4,64,128]{3,2,1,0:T(8,128)S(1)}, u32[]{:S(2)}, u32[]{:S(2)}) collective-permute-start(f32[2,4,64,128]{3,2,1,0:T(8,128)S(1)} %pad_maximum_fusion.1), channel_id=1, source_target_pairs={{0,128},{128,0},{64,192},{192,64},{1,129},{129,1},{65,193},{193,65... | collective-permute-start | bytes 786440 | tf_op jit(solution)/shard_map/ppermute | solution.py:585
  32.7 7.7 %forward.1 = (f32[24,16,8,128]{3,2,1,0:T(8,128)S(1)}, f32[24,16,8,128]{3,2,1,0:T(8,128)S(1)}, f32[24,16,8,128]{3,2,1,0:T(8,128)S(1)}, f32[24,16,8,128]{3,2,1,0:T...) custom-call(s32[1,3]{1,0:T(1,128)S(1)} %copy-done.9, ...), custom_call_target="tpu_custom_call" | custom-call | flops 33554432 | bytes 16777216 | tf_op jit(solution)/shard_map/forward/pallas_call | solution.py:415
  40.4 4.4 %adjoint.1 = (f32[18,16,8,128]{3,2,1,0:T(8,128)S(1)}, f32[18,16,8,128]{3,2,1,0:T(8,128)S(1)}, f32[18,16,8,128]{3,2,1,0:T(8,128)S(1)}, f32[18,16,8,128]{3,2,1,0:T...) custom-call(f32[144,8,128]{2,1,0:T(8,128)S(1)} %collective-permute-d, ...), custom_call_target="tpu_custom_call", output_to_operand_aliasing={{0}: (17, {}), {1}: (18, {}), {2}: (19, {}), {3}: (20, {}),... | custom-call | flops 33554432 | bytes 16777216 | tf_op jit(solution)/shard_map/adjoint/pallas_call | solution.py:504
  44.8 2.5 %collective-permute-start.6 = (f32[2,4,64,128]{3,2,1,0:T(8,128)S(1)}, f32[2,4,64,128]{3,2,1,0:T(8,128)S(1)}, u32[]{:S(2)}, u32[]{:S(2)}) collective-permute-start(f32[2,4,64,128]{3,2,1,0:T(8,128)S(1)} %get-tuple-element.76), channel_id=1, source_target_pairs={{0,64},{64,0},{128,192},{192,128},{1,65},{65,1},{129,193},{193,129... | collective-permute-start | bytes 786440 | tf_op jit(solution)/shard_map/ppermute | solution.py:581
  47.4 4.2 %collective-permute-done.5.moments = f32[2,4,64,128]{3,2,1,0:T(8,128)S(1)} collective-permute-done((f32[2,4,64,128]{3,2,1,0:T(8,128)S(1)}, f32[2,4,64,128]{3,2,1,0:T(8,128)S(1)}, u32[]{:S(2)}, u32[]{:S(2)}) %collective-permute-start.5) | collective-permute-done | bytes 262176 | tf_op jit(solution)/shard_map/ppermute | solution.py:585
  51.5 0.1 blend.1
  51.7 0.6 collective-permute-start.7
  52.3 8.4 %collective-permute-done.7 = f32[2,4,64,128]{3,2,1,0:T(8,128)S(1)} collective-permute-done((f32[2,4,64,128]{3,2,1,0:T(8,128)S(1)}, f32[2,4,64,128]{3,2,1,0:T(8,128)S(1)}, u32[]{:S(2)}, u32[]{:S(2)}) %collective-permute-start.7) | collective-permute-done | bytes 262176 | tf_op jit(solution)/shard_map/ppermute | solution.py:585
  60.7 0.2 fusion.3
  60.9 1.4 %collective-permute-start.8 = (f32[2,4,64,128]{3,2,1,0:T(8,128)S(1)}, f32[2,4,64,128]{3,2,1,0:T(8,128)S(1)}, u32[]{:S(2)}, u32[]{:S(2)}) collective-permute-start(f32[2,4,64,128]{3,2,1,0:T(8,128)S(1)} %get-tuple-element.83.mine), channel_id=1, source_target_pairs={{0,64},{64,0},{128,192},{192,128},{1,65},{65,1},{129,193},{193,129... | collective-permute-start | bytes 786440 | tf_op jit(solution)/shard_map/ppermute | solution.py:581
  62.3 0.7 %fusion.4 = (f32[4,8,1024]{2,1,0:T(8,128)}, f32[4,8,1024]{2,1,0:T(8,128)}) fusion(f32[2,4,64,128]{3,2,1,0:T(8,128)S(1)} %get-tuple-element.85, pred[]{:T(512)S(6)} %eq.10, f32[2,4,64,128]{3,2,1,0:T(8,128)S(1)} %get-tuple-element.84), kind=kLoop, calls=%fused_computation.11 | loop fusion | flops 65536 | bytes 786433 | tf_op jit(solution)/shard_map/reshape | solution.py:51
  63.0 0.4 collective-permute-done.8.other
  63.4 0.8 %finish.1 = f32[16,64,128]{2,1,0:T(8,128)} custom-call(f32[2,4,64,128]{3,2,1,0:T(8,128)S(1)} %get-tuple-element.83.mine, f32[2,4,64,128]{3,2,1,0:T(8,128)S(1)} %collective-permute-done.8.other), custom_call_target="tpu_custom_call" | custom-call | tf_op jit(solution)/shard_map/finish/pallas_call | solution.py:557
  (29 shorter events, 0.2 us)
Async XLA Ops:
  0.6 9.1 %copy-start.5 = (f32[4,8,1024]{2,1,0:T(8,128)S(1)}, f32[4,8,1024]{2,1,0:T(8,128)}, u32[]{:S(2)}) copy-start(f32[4,8,1024]{2,1,0:T(8,128)} %param.12) | copy-start | bytes 393220
  0.6 9.1 %copy-start.6 = (f32[4,8,1024]{2,1,0:T(8,128)S(1)}, f32[4,8,1024]{2,1,0:T(8,128)}, u32[]{:S(2)}) copy-start(f32[4,8,1024]{2,1,0:T(8,128)} %param.13) | copy-start | bytes 393220
  2.4 19.5 %collective-permute-start = (f32[204,8,128]{2,1,0:T(8,128)S(1)}, f32[204,8,128]{2,1,0:T(8,128)S(1)}, u32[]{:S(2)}, u32[]{:S(2)}) collective-permute-start(f32[204,8,128]{2,1,0:T(8,128)S(1)} %get-tuple-element.45), channel_id=1, source_target_pairs={{0,1},{2,3},{4,5},{6,7},{8,9},{10,11},{12,13},{14,15},{16,17},{18,... | collective-permute-start | bytes 2506760 | tf_op jit(solution)/shard_map/ppermute | solution.py:571
  3.8 24.0 %collective-permute-start.3 = (f32[204,8,128]{2,1,0:T(8,128)S(1)}, f32[204,8,128]{2,1,0:T(8,128)S(1)}, u32[]{:S(2)}, u32[]{:S(2)}) collective-permute-start(f32[204,8,128]{2,1,0:T(8,128)S(1)} %get-tuple-element.49), channel_id=1, source_target_pairs={{1,2},{3,4},{5,6},{7,8},{9,10},{11,12},{13,14},{15,16},{17,18},{19... | collective-permute-start | bytes 2506760 | tf_op jit(solution)/shard_map/ppermute | solution.py:577
  8.1 24.5 %copy-start.3 = (f32[1,16,8,1024]{3,2,1,0:T(8,128)S(1)}, f32[1,16,8,1024]{3,2,1,0:T(8,128)}, u32[]{:S(2)}) copy-start(f32[1,16,8,1024]{3,2,1,0:T(8,128)} %param.17) | copy-start | bytes 1572868
  8.1 24.5 %copy-start.4 = (f32[1,16,8,1024]{3,2,1,0:T(8,128)S(1)}, f32[1,16,8,1024]{3,2,1,0:T(8,128)}, u32[]{:S(2)}) copy-start(f32[1,16,8,1024]{3,2,1,0:T(8,128)} %param.16) | copy-start | bytes 1572868
  9.7 23.0 %copy-start = (f32[16,8,1024]{2,1,0:T(8,128)S(1)}, f32[16,8,1024]{2,1,0:T(8,128)}, u32[]{:S(2)}) copy-start(f32[16,8,1024]{2,1,0:T(8,128)} %param.11) | copy-start | bytes 1572868
  9.7 23.0 %copy-start.1 = (f32[1,16,8,1024]{3,2,1,0:T(8,128)S(1)}, f32[1,16,8,1024]{3,2,1,0:T(8,128)}, u32[]{:S(2)}) copy-start(f32[1,16,8,1024]{3,2,1,0:T(8,128)} %param.14) | copy-start | bytes 1572868
  9.7 23.0 %copy-start.2 = (f32[1,16,8,1024]{3,2,1,0:T(8,128)S(1)}, f32[1,16,8,1024]{3,2,1,0:T(8,128)}, u32[]{:S(2)}) copy-start(f32[1,16,8,1024]{3,2,1,0:T(8,128)} %param.15) | copy-start | bytes 1572868
  9.7 23.0 %copy-start.7 = (f32[1,4,8,128]{3,2,1,0:T(8,128)S(1)}, f32[1,4,8,128]{3,2,1,0:T(8,128)}, u32[]{:S(2)}) copy-start(f32[1,4,8,128]{3,2,1,0:T(8,128)} %param.18) | copy-start | bytes 49156
  9.7 23.0 %copy-start.8 = (s32[1,8,128]{2,1,0:T(8,128)S(1)}, s32[1,8,128]{2,1,0:T(8,128)}, u32[]{:S(2)}) copy-start(s32[1,8,128]{2,1,0:T(8,128)} %param.19) | copy-start | bytes 12292
  9.7 23.0 %copy-start.9 = (s32[1,3]{1,0:T(1,128)S(1)}, s32[1,3]{1,0:T(1,128)}, u32[]{:S(2)}) copy-start(s32[1,3]{1,0:T(1,128)} %source_pos.1) | copy-start | bytes 40
  9.7 23.0 %copy-start.10 = (f32[1,4]{1,0:T(1,128)S(1)}, f32[1,4]{1,0:T(1,128)}, u32[]{:S(2)}) copy-start(f32[1,4]{1,0:T(1,128)} %source_wave.1) | copy-start | bytes 52
  22.0 18.4 %collective-permute-start.1 = (f32[144,8,128]{2,1,0:T(8,128)S(1)}, f32[144,8,128]{2,1,0:T(8,128)S(1)}, u32[]{:S(2)}, u32[]{:S(2)}) collective-permute-start(f32[144,8,128]{2,1,0:T(8,128)S(1)} %get-tuple-element.46), channel_id=1, source_target_pairs={{1,2},{3,4},{5,6},{7,8},{9,10},{11,12},{13,14},{15,16},{17,18},{19... | collective-permute-start | bytes 1769480 | tf_op jit(solution)/shard_map/ppermute | solution.py:577
  27.1 13.3 %collective-permute-start.2 = (f32[144,8,128]{2,1,0:T(8,128)S(1)}, f32[144,8,128]{2,1,0:T(8,128)S(1)}, u32[]{:S(2)}, u32[]{:S(2)}) collective-permute-start(f32[144,8,128]{2,1,0:T(8,128)S(1)} %get-tuple-element.47), channel_id=1, source_target_pairs={{0,1},{2,3},{4,5},{6,7},{8,9},{10,11},{12,13},{14,15},{16,17},{18,... | collective-permute-start | bytes 1769480 | tf_op jit(solution)/shard_map/ppermute | solution.py:571
  27.9 4.7 %collective-permute-start.4 = (f32[92,8,128]{2,1,0:T(8,128)S(1)}, f32[92,8,128]{2,1,0:T(8,128)S(1)}, u32[]{:S(2)}, u32[]{:S(2)}) collective-permute-start(f32[92,8,128]{2,1,0:T(8,128)S(1)} %pad_maximum_fusion), channel_id=1, source_target_pairs={{0,64},{64,0},{128,192},{192,128},{1,65},{65,1},{129,193},{193,129... | collective-permute-start | bytes 1130504 | tf_op jit(solution)/shard_map/ppermute | solution.py:581
  29.9 21.7 %collective-permute-start.5 = (f32[2,4,64,128]{3,2,1,0:T(8,128)S(1)}, f32[2,4,64,128]{3,2,1,0:T(8,128)S(1)}, u32[]{:S(2)}, u32[]{:S(2)}) collective-permute-start(f32[2,4,64,128]{3,2,1,0:T(8,128)S(1)} %pad_maximum_fusion.1), channel_id=1, source_target_pairs={{0,128},{128,0},{64,192},{192,64},{1,129},{129,1},{65,193},{193,65... | collective-permute-start | bytes 786440 | tf_op jit(solution)/shard_map/ppermute | solution.py:585
  44.8 6.8 %collective-permute-start.6 = (f32[2,4,64,128]{3,2,1,0:T(8,128)S(1)}, f32[2,4,64,128]{3,2,1,0:T(8,128)S(1)}, u32[]{:S(2)}, u32[]{:S(2)}) collective-permute-start(f32[2,4,64,128]{3,2,1,0:T(8,128)S(1)} %get-tuple-element.76), channel_id=1, source_target_pairs={{0,64},{64,0},{128,192},{192,128},{1,65},{65,1},{129,193},{193,129... | collective-permute-start | bytes 786440 | tf_op jit(solution)/shard_map/ppermute | solution.py:581
  51.7 9.0 %collective-permute-start.7 = (f32[2,4,64,128]{3,2,1,0:T(8,128)S(1)}, f32[2,4,64,128]{3,2,1,0:T(8,128)S(1)}, u32[]{:S(2)}, u32[]{:S(2)}) collective-permute-start(f32[2,4,64,128]{3,2,1,0:T(8,128)S(1)} %add.24), channel_id=1, source_target_pairs={{0,128},{128,0},{64,192},{192,64},{1,129},{129,1},{65,193},{193,65... | collective-permute-start | bytes 786440 | tf_op jit(solution)/shard_map/ppermute | solution.py:585
  60.9 2.5 %collective-permute-start.8 = (f32[2,4,64,128]{3,2,1,0:T(8,128)S(1)}, f32[2,4,64,128]{3,2,1,0:T(8,128)S(1)}, u32[]{:S(2)}, u32[]{:S(2)}) collective-permute-start(f32[2,4,64,128]{3,2,1,0:T(8,128)S(1)} %get-tuple-element.83.mine), channel_id=1, source_target_pairs={{0,64},{64,0},{128,192},{192,128},{1,65},{65,1},{129,193},{193,129... | collective-permute-start | bytes 786440 | tf_op jit(solution)/shard_map/ppermute | solution.py:581

commit v7 on v6

--- a/solution.py
+++ b/solution.py
@@ -35,6 +35,7 @@
 TILE_L = (2 * REACH - 1) * NZ
 HALF = 0.5 * TIME_STEP_SQ
 PACK_VMEM = 56 << 20
+FIRST_VMEM = 119 << 19
 
 f32 = jnp.float32
 VMEM = pl.BlockSpec(memory_space=pltpu.VMEM)
@@ -163,15 +164,16 @@
     by_parity((even, odd), lambda low, high: pack_fields((l6, l7), (REACH, REACH - 1), low, high, 0))
 
 
-def pack(kernel, name, tiles, *arrays):
+def pack(kernel, name, tiles, kept, limit, *arrays):
     shape = pltpu.VMEM((tiles, XT, LANES), f32)
+    here = [pltpu.VMEM(a.shape, a.dtype) for a in arrays]
     return pl.pallas_call(
         kernel,
-        out_shape=(shape, shape),
+        out_shape=(shape, shape, *here[:kept]),
         in_specs=[pl.BlockSpec(memory_space=pl.ANY)] * len(arrays),
-        out_specs=(VMEM, VMEM),
-        scratch_shapes=[pltpu.VMEM(a.shape, a.dtype) for a in arrays] + [pltpu.SemaphoreType.DMA((len(arrays),))],
-        compiler_params=pltpu.CompilerParams(vmem_limit_bytes=PACK_VMEM),
+        out_specs=(VMEM,) * (2 + kept),
+        scratch_shapes=here[kept:] + [pltpu.SemaphoreType.DMA((len(arrays),))],
+        compiler_params=pltpu.CompilerParams(vmem_limit_bytes=limit),
         cost_estimate=pl.CostEstimate(flops=0, bytes_accessed=1 << 16, transcendentals=0),
         name=name,
     )(*arrays)
@@ -605,15 +607,16 @@
     l6, l7 = native(adjoint_now[0]), native(adjoint_next[0])
     first, second = native(first_moment), native(second_moment)
 
-    a_even, a_odd = pack(pack_first_kernel, "pack_first", TILE_A, s, u1, u0, receiver_x[0], observed[0])
-    l_even, l_odd = pack(pack_adjoint_kernel, "pack_adjoint", TILE_L, l6, l7)
+    a_even, a_odd, s_here, u1, u0 = pack(
+        pack_first_kernel, "pack_first", TILE_A, 3, FIRST_VMEM, s, u1, u0, receiver_x[0], observed[0])
+    l_even, l_odd = pack(pack_adjoint_kernel, "pack_adjoint", TILE_L, 0, PACK_VMEM, l6, l7)
     a_even, a_odd = swap_even(a_even), swap_odd(a_odd)
     moments = jnp.stack([first, second])
     l_even, l_odd, moments, a_even = lax.optimization_barrier((l_even, l_odd, moments, a_even))
     l_even, l_odd, moments = swap_even(l_even), swap_odd(l_odd), swap_far(moments)
     other = swap_core(jnp.concatenate([a_even[:TILE_S], a_odd[:TILE_S]]))
     fields = forward(
-        source_pos, source_wave, u0, u1, s, a_even, a_odd, other, receiver_x[0], observed[0], l6, l7
+        source_pos, source_wave, u0, u1, s_here, a_even, a_odd, other, receiver_x[0], observed[0], l6, l7
     )
     keep, send = adjoint(l_odd, l_even, *fields)
     keep, moments = lax.optimization_barrier((keep, moments))

time: 64.4 us -> 64.4 us (level)
  no operation moved by 1% of the time
where the time goes in v7:
time: 64.4 us; the launch traced here: 64.2 us
  waiting for transfers between devices  26 us (40%)
  starting transfers between devices  20.2 us (31%)
  Pallas kernels  16.1 us (25%)
  other arithmetic  1.01 us (2%)
  between operations  0.89 us (1%)
    ppermute x2, waiting for transfers between devices, swap_far(): return lax.ppermute(block, 'shot', [(0, 2), (2, 0), (1, 3), (3, 1)])  12.6 us
    ppermute x2, waiting for transfers between devices, swap_even(): return lax.ppermute(block, 'gy', pairs + [(j, i) for i, j in pairs])  12.3 us
    ppermute x2, starting transfers between devices, swap_odd(): return lax.ppermute(block, 'gy', pairs + [(j, i) for i, j in pairs])  9.37 us
    pallas_call x1, Pallas kernels, forward(): pl.pallas_call(forward_kernel, out_shape=outs, in_specs=[SMEM] * 2 + [VME...  7.64 us
    ppermute x3, starting transfers between devices, swap_core(): return lax.ppermute(block, 'shot', [(0, 1), (1, 0), (2, 3), (3, 2)])  5.94 us
    pallas_call x1, Pallas kernels, adjoint(): pl.pallas_call(adjoint_kernel, out_shape=outs, in_specs=[VMEM] * len(args...  4.34 us
    ppermute x2, starting transfers between devices, swap_far(): return lax.ppermute(block, 'shot', [(0, 2), (2, 0), (1, 3), (3, 1)])  3.37 us
    pallas_call x2, Pallas kernels, pack(): pl.pallas_call(kernel, out_shape=(shape, shape, *here[:kept]), in_specs=[...  3.24 us
  transfers between devices with their start and end apart: 9, of which 5 were waited for; matrix products, arithmetic and copies ran while one was open for 1% of the time, Pallas kernels for 21%

profile of v7, /device:TPU:97, one launch (start us, length us, event | category | flops | bytes accessed | tf_op | source)
XLA Modules:
  0.0 64.2 jit_solution(9046991255142796963)
XLA Ops:
  0.7 1.8 %pack_first.1 = (f32[204,8,128]{2,1,0:T(8,128)S(1)}, f32[204,8,128]{2,1,0:T(8,128)S(1)}, f32[16,64,128]{2,1,0:T(8,128)S(1)}, f32[16,64,128]{2,1,0:T(8,128)S(1)}, f32[16,64,128]{2,1,0:T(8,128)S(1)}) custom-call(f32[16,64,128]{2,1,0:T(8,128)} %bitcast.88, f32[16,64,128]{2,1,0:T(8,128)} %bitcast.90, f32[16,64,128]{2,1,0:T(8,128)} %bitcast.91, ...), custom_call_target="tpu_custom_call" | custom-call | bytes 65536 | tf_op jit(solution)/shard_map/pack_first/pallas_call | solution.py:170
  2.5 1.4 %collective-permute-start = (f32[204,8,128]{2,1,0:T(8,128)S(1)}, f32[204,8,128]{2,1,0:T(8,128)S(1)}, u32[]{:S(2)}, u32[]{:S(2)}) collective-permute-start(f32[204,8,128]{2,1,0:T(8,128)S(1)} %get-tuple-element.48), channel_id=1, source_target_pairs={{0,1},{2,3},{4,5},{6,7},{8,9},{10,11},{12,13},{14,15},{16,17},{18,... | collective-permute-start | bytes 2506760 | tf_op jit(solution)/shard_map/ppermute | solution.py:573
  3.8 4.3 %collective-permute-start.3 = (f32[204,8,128]{2,1,0:T(8,128)S(1)}, f32[204,8,128]{2,1,0:T(8,128)S(1)}, u32[]{:S(2)}, u32[]{:S(2)}) collective-permute-start(f32[204,8,128]{2,1,0:T(8,128)S(1)} %get-tuple-element.55), channel_id=1, source_target_pairs={{1,2},{3,4},{5,6},{7,8},{9,10},{11,12},{13,14},{15,16},{17,18},{19... | collective-permute-start | bytes 2506760 | tf_op jit(solution)/shard_map/ppermute | solution.py:579
  8.1 1.4 %pack_adjoint.1 = (f32[144,8,128]{2,1,0:T(8,128)S(1)}, f32[144,8,128]{2,1,0:T(8,128)S(1)}) custom-call(f32[16,64,128]{2,1,0:T(8,128)} %bitcast.76, f32[16,64,128]{2,1,0:T(8,128)} %bitcast.78), custom_call_target="tpu_custom_call" | custom-call | bytes 65536 | tf_op jit(solution)/shard_map/pack_adjoint/pallas_call | solution.py:170
  9.6 0.0 copy-start
  9.6 0.0 copy-start.5
  9.7 12.3 %collective-permute-done.even = f32[204,8,128]{2,1,0:T(8,128)S(1)} collective-permute-done((f32[204,8,128]{2,1,0:T(8,128)S(1)}, f32[204,8,128]{2,1,0:T(8,128)S(1)}, u32[]{:S(2)}, u32[]{:S(2)}) %collective-permute-start) | collective-permute-done | bytes 835616 | tf_op jit(solution)/shard_map/ppermute | solution.py:573
  22.0 5.1 %collective-permute-start.1 = (f32[144,8,128]{2,1,0:T(8,128)S(1)}, f32[144,8,128]{2,1,0:T(8,128)S(1)}, u32[]{:S(2)}, u32[]{:S(2)}) collective-permute-start(f32[144,8,128]{2,1,0:T(8,128)S(1)} %get-tuple-element.49), channel_id=1, source_target_pairs={{1,2},{3,4},{5,6},{7,8},{9,10},{11,12},{13,14},{15,16},{17,18},{19... | collective-permute-start | bytes 1769480 | tf_op jit(solution)/shard_map/ppermute | solution.py:579
  27.1 0.1 collective-permute-start.2
  27.2 0.6 collective-permute-done.3.odd
  27.9 2.0 %collective-permute-start.4 = (f32[92,8,128]{2,1,0:T(8,128)S(1)}, f32[92,8,128]{2,1,0:T(8,128)S(1)}, u32[]{:S(2)}, u32[]{:S(2)}) collective-permute-start(f32[92,8,128]{2,1,0:T(8,128)S(1)} %pad_maximum_fusion), channel_id=1, source_target_pairs={{0,64},{64,0},{128,192},{192,128},{1,65},{65,1},{129,193},{193,129... | collective-permute-start | bytes 1130504 | tf_op jit(solution)/shard_map/ppermute | solution.py:583
  29.9 2.8 %collective-permute-start.5 = (f32[2,4,64,128]{3,2,1,0:T(8,128)S(1)}, f32[2,4,64,128]{3,2,1,0:T(8,128)S(1)}, u32[]{:S(2)}, u32[]{:S(2)}) collective-permute-start(f32[2,4,64,128]{3,2,1,0:T(8,128)S(1)} %pad_maximum_fusion.1), channel_id=1, source_target_pairs={{0,128},{128,0},{64,192},{192,64},{1,129},{129,1},{65,193},{193,65... | collective-permute-start | bytes 786440 | tf_op jit(solution)/shard_map/ppermute | solution.py:587
  32.7 7.6 %forward.1 = (f32[24,16,8,128]{3,2,1,0:T(8,128)S(1)}, f32[24,16,8,128]{3,2,1,0:T(8,128)S(1)}, f32[24,16,8,128]{3,2,1,0:T(8,128)S(1)}, f32[24,16,8,128]{3,2,1,0:T...) custom-call(s32[1,3]{1,0:T(1,128)S(1)} %copy-done.6, ...), custom_call_target="tpu_custom_call" | custom-call | flops 33554432 | bytes 16777216 | tf_op jit(solution)/shard_map/forward/pallas_call | solution.py:417
  40.4 4.3 %adjoint.1 = (f32[18,16,8,128]{3,2,1,0:T(8,128)S(1)}, f32[18,16,8,128]{3,2,1,0:T(8,128)S(1)}, f32[18,16,8,128]{3,2,1,0:T(8,128)S(1)}, f32[18,16,8,128]{3,2,1,0:T...) custom-call(f32[144,8,128]{2,1,0:T(8,128)S(1)} %collective-permute-d, ...), custom_call_target="tpu_custom_call", output_to_operand_aliasing={{0}: (17, {}), {1}: (18, {}), {2}: (19, {}), {3}: (20, {}),... | custom-call | flops 33554432 | bytes 16777216 | tf_op jit(solution)/shard_map/adjoint/pallas_call | solution.py:506
  44.7 2.6 %collective-permute-start.6 = (f32[2,4,64,128]{3,2,1,0:T(8,128)S(1)}, f32[2,4,64,128]{3,2,1,0:T(8,128)S(1)}, u32[]{:S(2)}, u32[]{:S(2)}) collective-permute-start(f32[2,4,64,128]{3,2,1,0:T(8,128)S(1)} %get-tuple-element.82), channel_id=1, source_target_pairs={{0,64},{64,0},{128,192},{192,128},{1,65},{65,1},{129,193},{193,129... | collective-permute-start | bytes 786440 | tf_op jit(solution)/shard_map/ppermute | solution.py:583
  47.3 4.2 %collective-permute-done.5.moments = f32[2,4,64,128]{3,2,1,0:T(8,128)S(1)} collective-permute-done((f32[2,4,64,128]{3,2,1,0:T(8,128)S(1)}, f32[2,4,64,128]{3,2,1,0:T(8,128)S(1)}, u32[]{:S(2)}, u32[]{:S(2)}) %collective-permute-start.5) | collective-permute-done | bytes 262176 | tf_op jit(solution)/shard_map/ppermute | solution.py:587
  51.5 0.1 blend.1
  51.7 0.6 collective-permute-start.7
  52.3 8.4 %collective-permute-done.7 = f32[2,4,64,128]{3,2,1,0:T(8,128)S(1)} collective-permute-done((f32[2,4,64,128]{3,2,1,0:T(8,128)S(1)}, f32[2,4,64,128]{3,2,1,0:T(8,128)S(1)}, u32[]{:S(2)}, u32[]{:S(2)}) %collective-permute-start.7) | collective-permute-done | bytes 262176 | tf_op jit(solution)/shard_map/ppermute | solution.py:587
  60.7 0.2 fusion.3
  60.9 1.4 %collective-permute-start.8 = (f32[2,4,64,128]{3,2,1,0:T(8,128)S(1)}, f32[2,4,64,128]{3,2,1,0:T(8,128)S(1)}, u32[]{:S(2)}, u32[]{:S(2)}) collective-permute-start(f32[2,4,64,128]{3,2,1,0:T(8,128)S(1)} %get-tuple-element.89.mine), channel_id=1, source_target_pairs={{0,64},{64,0},{128,192},{192,128},{1,65},{65,1},{129,193},{193,129... | collective-permute-start | bytes 786440 | tf_op jit(solution)/shard_map/ppermute | solution.py:583
  62.3 0.7 %fusion.4 = (f32[4,8,1024]{2,1,0:T(8,128)}, f32[4,8,1024]{2,1,0:T(8,128)}) fusion(f32[2,4,64,128]{3,2,1,0:T(8,128)S(1)} %get-tuple-element.91, pred[]{:T(512)S(6)} %eq.10, f32[2,4,64,128]{3,2,1,0:T(8,128)S(1)} %get-tuple-element.90), kind=kLoop, calls=%fused_computation.11 | loop fusion | flops 65536 | bytes 786433 | tf_op jit(solution)/shard_map/reshape | solution.py:52
  63.0 0.4 collective-permute-done.8.other
  63.4 0.8 %finish.1 = f32[16,64,128]{2,1,0:T(8,128)} custom-call(f32[2,4,64,128]{3,2,1,0:T(8,128)S(1)} %get-tuple-element.89.mine, f32[2,4,64,128]{3,2,1,0:T(8,128)S(1)} %collective-permute-done.8.other), custom_call_target="tpu_custom_call" | custom-call | tf_op jit(solution)/shard_map/finish/pallas_call | solution.py:559
  (25 shorter events, 0.2 us)
Async XLA Ops:
  0.6 9.0 %copy-start.2 = (f32[4,8,1024]{2,1,0:T(8,128)S(1)}, f32[4,8,1024]{2,1,0:T(8,128)}, u32[]{:S(2)}) copy-start(f32[4,8,1024]{2,1,0:T(8,128)} %param.12) | copy-start | bytes 393220
  0.6 9.0 %copy-start.3 = (f32[4,8,1024]{2,1,0:T(8,128)S(1)}, f32[4,8,1024]{2,1,0:T(8,128)}, u32[]{:S(2)}) copy-start(f32[4,8,1024]{2,1,0:T(8,128)} %param.13) | copy-start | bytes 393220
  2.5 19.5 %collective-permute-start = (f32[204,8,128]{2,1,0:T(8,128)S(1)}, f32[204,8,128]{2,1,0:T(8,128)S(1)}, u32[]{:S(2)}, u32[]{:S(2)}) collective-permute-start(f32[204,8,128]{2,1,0:T(8,128)S(1)} %get-tuple-element.48), channel_id=1, source_target_pairs={{0,1},{2,3},{4,5},{6,7},{8,9},{10,11},{12,13},{14,15},{16,17},{18,... | collective-permute-start | bytes 2506760 | tf_op jit(solution)/shard_map/ppermute | solution.py:573
  3.8 24.0 %collective-permute-start.3 = (f32[204,8,128]{2,1,0:T(8,128)S(1)}, f32[204,8,128]{2,1,0:T(8,128)S(1)}, u32[]{:S(2)}, u32[]{:S(2)}) collective-permute-start(f32[204,8,128]{2,1,0:T(8,128)S(1)} %get-tuple-element.55), channel_id=1, source_target_pairs={{1,2},{3,4},{5,6},{7,8},{9,10},{11,12},{13,14},{15,16},{17,18},{19... | collective-permute-start | bytes 2506760 | tf_op jit(solution)/shard_map/ppermute | solution.py:579
  9.6 23.1 %copy-start = (f32[1,16,8,1024]{3,2,1,0:T(8,128)S(1)}, f32[1,16,8,1024]{3,2,1,0:T(8,128)}, u32[]{:S(2)}) copy-start(f32[1,16,8,1024]{3,2,1,0:T(8,128)} %param.17) | copy-start | bytes 1572868
  9.6 23.1 %copy-start.1 = (f32[1,16,8,1024]{3,2,1,0:T(8,128)S(1)}, f32[1,16,8,1024]{3,2,1,0:T(8,128)}, u32[]{:S(2)}) copy-start(f32[1,16,8,1024]{3,2,1,0:T(8,128)} %param.16) | copy-start | bytes 1572868
  9.6 23.1 %copy-start.4 = (f32[1,4,8,128]{3,2,1,0:T(8,128)S(1)}, f32[1,4,8,128]{3,2,1,0:T(8,128)}, u32[]{:S(2)}) copy-start(f32[1,4,8,128]{3,2,1,0:T(8,128)} %param.18) | copy-start | bytes 49156
  9.6 23.1 %copy-start.5 = (s32[1,8,128]{2,1,0:T(8,128)S(1)}, s32[1,8,128]{2,1,0:T(8,128)}, u32[]{:S(2)}) copy-start(s32[1,8,128]{2,1,0:T(8,128)} %param.19) | copy-start | bytes 12292
  9.6 23.0 %copy-start.6 = (s32[1,3]{1,0:T(1,128)S(1)}, s32[1,3]{1,0:T(1,128)}, u32[]{:S(2)}) copy-start(s32[1,3]{1,0:T(1,128)} %source_pos.1) | copy-start | bytes 40
  9.6 23.0 %copy-start.7 = (f32[1,4]{1,0:T(1,128)S(1)}, f32[1,4]{1,0:T(1,128)}, u32[]{:S(2)}) copy-start(f32[1,4]{1,0:T(1,128)} %source_wave.1) | copy-start | bytes 52
  22.0 18.3 %collective-permute-start.1 = (f32[144,8,128]{2,1,0:T(8,128)S(1)}, f32[144,8,128]{2,1,0:T(8,128)S(1)}, u32[]{:S(2)}, u32[]{:S(2)}) collective-permute-start(f32[144,8,128]{2,1,0:T(8,128)S(1)} %get-tuple-element.49), channel_id=1, source_target_pairs={{1,2},{3,4},{5,6},{7,8},{9,10},{11,12},{13,14},{15,16},{17,18},{19... | collective-permute-start | bytes 1769480 | tf_op jit(solution)/shard_map/ppermute | solution.py:579
  27.1 13.2 %collective-permute-start.2 = (f32[144,8,128]{2,1,0:T(8,128)S(1)}, f32[144,8,128]{2,1,0:T(8,128)S(1)}, u32[]{:S(2)}, u32[]{:S(2)}) collective-permute-start(f32[144,8,128]{2,1,0:T(8,128)S(1)} %get-tuple-element.50), channel_id=1, source_target_pairs={{0,1},{2,3},{4,5},{6,7},{8,9},{10,11},{12,13},{14,15},{16,17},{18,... | collective-permute-start | bytes 1769480 | tf_op jit(solution)/shard_map/ppermute | solution.py:573
  27.9 4.7 %collective-permute-start.4 = (f32[92,8,128]{2,1,0:T(8,128)S(1)}, f32[92,8,128]{2,1,0:T(8,128)S(1)}, u32[]{:S(2)}, u32[]{:S(2)}) collective-permute-start(f32[92,8,128]{2,1,0:T(8,128)S(1)} %pad_maximum_fusion), channel_id=1, source_target_pairs={{0,64},{64,0},{128,192},{192,128},{1,65},{65,1},{129,193},{193,129... | collective-permute-start | bytes 1130504 | tf_op jit(solution)/shard_map/ppermute | solution.py:583
  29.9 21.7 %collective-permute-start.5 = (f32[2,4,64,128]{3,2,1,0:T(8,128)S(1)}, f32[2,4,64,128]{3,2,1,0:T(8,128)S(1)}, u32[]{:S(2)}, u32[]{:S(2)}) collective-permute-start(f32[2,4,64,128]{3,2,1,0:T(8,128)S(1)} %pad_maximum_fusion.1), channel_id=1, source_target_pairs={{0,128},{128,0},{64,192},{192,64},{1,129},{129,1},{65,193},{193,65... | collective-permute-start | bytes 786440 | tf_op jit(solution)/shard_map/ppermute | solution.py:587
  44.7 16.0 %copy-start.8 = (f32[16,8,1024]{2,1,0:T(8,128)S(1)}, f32[16,8,1024]{2,1,0:T(8,128)}, u32[]{:S(2)}) copy-start(f32[16,8,1024]{2,1,0:T(8,128)} %param.11) | copy-start | bytes 1572868
  44.7 6.9 %collective-permute-start.6 = (f32[2,4,64,128]{3,2,1,0:T(8,128)S(1)}, f32[2,4,64,128]{3,2,1,0:T(8,128)S(1)}, u32[]{:S(2)}, u32[]{:S(2)}) collective-permute-start(f32[2,4,64,128]{3,2,1,0:T(8,128)S(1)} %get-tuple-element.82), channel_id=1, source_target_pairs={{0,64},{64,0},{128,192},{192,128},{1,65},{65,1},{129,193},{193,129... | collective-permute-start | bytes 786440 | tf_op jit(solution)/shard_map/ppermute | solution.py:583
  51.7 9.0 %collective-permute-start.7 = (f32[2,4,64,128]{3,2,1,0:T(8,128)S(1)}, f32[2,4,64,128]{3,2,1,0:T(8,128)S(1)}, u32[]{:S(2)}, u32[]{:S(2)}) collective-permute-start(f32[2,4,64,128]{3,2,1,0:T(8,128)S(1)} %add.24), channel_id=1, source_target_pairs={{0,128},{128,0},{64,192},{192,64},{1,129},{129,1},{65,193},{193,65... | collective-permute-start | bytes 786440 | tf_op jit(solution)/shard_map/ppermute | solution.py:587
  60.9 2.5 %collective-permute-start.8 = (f32[2,4,64,128]{3,2,1,0:T(8,128)S(1)}, f32[2,4,64,128]{3,2,1,0:T(8,128)S(1)}, u32[]{:S(2)}, u32[]{:S(2)}) collective-permute-start(f32[2,4,64,128]{3,2,1,0:T(8,128)S(1)} %get-tuple-element.89.mine), channel_id=1, source_target_pairs={{0,64},{64,0},{128,192},{192,128},{1,65},{65,1},{129,193},{193,129... | collective-permute-start | bytes 786440 | tf_op jit(solution)/shard_map/ppermute | solution.py:583
